TPU v7x, 32 devices: a whole 2x2x4 slice. The times are simulated.
32 devices in a mesh: seq: 8 (over y, x, core), chan: 4 (over z).
Axes of the slice: x: 2, y: 2, z: 4, core: 2. Of those that a mesh axis runs over, the one named last changes fastest.
Arguments:
- latent: bfloat16 [4096, 16], P(('seq', 'chan')), may hold values from -140 to 140
- in_weight: bfloat16 [9, 16, 384], P(None, 'chan'), may hold values from -2 to 2
- in_bias: float32 [384], P('chan'), may hold values from -1.75 to 1.75
- norm_gain: float32 [3, 2, 384], P(None, None, 'chan'), may hold values from 0.1 to 1.9
- norm_shift: float32 [3, 2, 384], P(None, None, 'chan'), may hold values from -1.75 to 1.75
- res_weight: bfloat16 [3, 2, 9, 384, 384], P(None, None, None, 'chan'), may hold values from -2 to 2
- res_bias: float32 [3, 2, 384], P(None, None, 'chan'), may hold values from -1.75 to 1.75
- up_weight: bfloat16 [9, 384, 192], P(None, 'chan'), may hold values from -0.109375 to 0.109375
- up_bias: float32 [192], P('chan'), may hold values from -1.75 to 1.75
Outputs:
- image: bfloat16 [192, 32, 512], P('chan', 'seq')
All inputs are finite; a program needn't handle non-finite values.
Results may differ from a plain program's by a relative error of at most 0.022.
Values may be sent and summed in bfloat16 or wider, within the bound.
No kernel may reach another device: no remote copies, remote signals or barrier semaphores. Data moves between devices by JAX's collectives and lax.ppermute only.
A program may use at most 64 MiB of HBM per device.

v0:
```python
import jax
import jax.numpy as jnp
from jax import lax
from jax.sharding import PartitionSpec as P

CH = 384
LAYERS = 3
LAT_W = 256


EPS = 1e-06


def padded_2(array, sides, width):
    for axis, dim in sides:
        peers, length = (lax.axis_size(axis), array.shape[dim])
        up = [(i, (i + 1) % peers) for i in range(peers - 1)]
        down = [(j, i) for i, j in up]
        last = lax.slice_in_dim(array, length - width, length, axis=dim)
        first = lax.slice_in_dim(array, 0, width, axis=dim)
        before = lax.ppermute(last, axis, up)
        after = lax.ppermute(first, axis, down)
        array = jnp.concatenate([before, array, after], axis=dim)
    return array


def with_rims(field):
    return padded_2(field, (("seq", 1),), 1)


def gather_columns(padded):
    chans = padded.shape[0]
    height = padded.shape[1] - 2
    width = padded.shape[2]
    framed = jnp.pad(padded, ((0, 0), (0, 0), (1, 1)))
    shifted = [
        framed[:, row_off : row_off + height, col_off : col_off + width]
        for row_off in range(3)
        for col_off in range(3)
    ]
    return jnp.stack(shifted, 0).reshape(9 * chans, height * width)


def contract(flat_weight, columns):
    return lax.dot_general(
        flat_weight, columns, (((0,), (0,)), ((), ())), preferred_element_type=jnp.float32
    )


def conv_block(padded, weight, bias):
    columns = gather_columns(padded)
    flat_weight = weight.reshape(-1, weight.shape[2])
    out_share = flat_weight.shape[1] // lax.axis_size("chan")
    partial_value = lax.psum_scatter(
        contract(flat_weight, columns).astype(jnp.bfloat16), "chan", scatter_dimension=0, tiled=True
    ).astype(jnp.float32)
    return (partial_value + bias[:, None]).reshape(out_share, padded.shape[1] - 2, padded.shape[2])


def up_block(padded, weight, bias):
    columns = gather_columns(padded)
    flat_weight = weight.reshape(-1, weight.shape[2])
    out_share = flat_weight.shape[1] // lax.axis_size("chan")
    partial_value = lax.psum_scatter(
        contract(flat_weight, columns).astype(jnp.bfloat16), "chan", scatter_dimension=0, tiled=True
    ).astype(jnp.float32)
    return (partial_value + bias[:, None]).reshape(out_share, padded.shape[1] - 2, padded.shape[2])


def rms_norm(values, gain_vec, shift_vec):
    squares = jnp.sum(values * values, axis=0)
    totals = lax.psum(squares, "chan")
    scale = lax.rsqrt(totals / float(CH) + EPS)
    return values * scale[None] * gain_vec[:, None, None] + shift_vec[:, None, None]


def body(
    latent, in_weight, in_bias, norm_gain, norm_shift, res_weight, res_bias, up_weight, up_bias
):
    own_quarter = lax.all_to_all(latent, "chan", split_axis=1, concat_axis=0, tiled=True)
    slab_rows = own_quarter.shape[0] // LAT_W
    slab_field = own_quarter.T.reshape(own_quarter.shape[1], slab_rows, LAT_W)
    stream = conv_block(with_rims(slab_field), in_weight, in_bias).astype(jnp.bfloat16)
    for layer_idx in range(LAYERS):
        normed = jax.nn.silu(
            rms_norm(stream.astype(jnp.float32), norm_gain[layer_idx, 0], norm_shift[layer_idx, 0])
        ).astype(jnp.bfloat16)
        middle = conv_block(with_rims(normed), res_weight[layer_idx, 0], res_bias[layer_idx, 0])
        branch_in = jax.nn.silu(
            rms_norm(middle, norm_gain[layer_idx, 1], norm_shift[layer_idx, 1])
        ).astype(jnp.bfloat16)
        branch_out = conv_block(
            with_rims(branch_in), res_weight[layer_idx, 1], res_bias[layer_idx, 1]
        )
        stream = (stream.astype(jnp.float32) + branch_out).astype(jnp.bfloat16)
    rimmed = with_rims(stream)
    widened = jnp.repeat(jnp.repeat(rimmed, 2, axis=1), 2, axis=2)[:, 1:-1, :]
    return up_block(widened, up_weight, up_bias).astype(jnp.bfloat16)


def solution(mesh):
    placed = (
        P(("seq", "chan"), None),
        P(None, "chan", None),
        P("chan"),
        P(None, None, "chan"),
        P(None, None, "chan"),
        P(None, None, None, "chan", None),
        P(None, None, "chan"),
        P(None, "chan", None),
        P("chan"),
    )
    return jax.shard_map(
        body, mesh=mesh, in_specs=placed, out_specs=P("chan", "seq", None), check_vma=False
    )
```

profile of v0, /device:TPU:0, one launch (start us, length us, event | category | flops | bytes accessed | tf_op | source)
XLA Modules:
  0.0 379.9 jit_solution(16725370018003030780)
XLA Ops:
  6.5 12.0 %all_to_all.19 = bf16[128,4,4]{0,2,1:T(4,128)(2,1)S(1)} all-to-all(bf16[128,4,4]{0,2,1:T(4,128)(2,1)} %bitcast.420), channel_id=1, replica_groups=mesh['seq'=8,'chan'=4] {'chan'}, dimensions={1} | all-to-all | bytes 8192 | tf_op jit(solution)/shard_map/all_to_all | solution.py:80
  22.0 2.7 collective-permute-done.1
  26.5 1.4 slice_bitcast_fusion.46
  27.9 19.5 %reduce-scatter.25.cloned.1.call-done = bf16[96,512]{1,0:T(8,128)(2,1)} async-done(((bf16[384,512]{1,0:T(8,128)(2,1)}), bf16[96,512]{1,0:T(8,128)(2,1)}) %reduce-scatter.25.cloned.1.call-update) | async-done | bytes 98320
  49.2 8.7 %psum.42 = f32[2,256]{1,0:T(2,128)S(1)} all-reduce(f32[2,256]{1,0:T(2,128)S(1)} %reduce_sum.67), channel_id=1, replica_groups=mesh['seq'=8,'chan'=4] {'chan'}, use_global_device_ids=true, to_apply=%region_2.3 | all-reduce | flops 512 | bytes 4096 | tf_op jit(solution)/shard_map/psum | solution.py:72
  60.9 3.7 fusion.62
  69.6 22.3 %reduce-scatter.27.cloned.1.call-done = bf16[96,512]{1,0:T(8,128)(2,1)} async-done(((bf16[384,512]{1,0:T(8,128)(2,1)}), bf16[96,512]{1,0:T(8,128)(2,1)}) %reduce-scatter.27.cloned.1.call-update) | async-done | bytes 98320
  93.1 8.7 %psum.43 = f32[2,256]{1,0:T(2,128)S(1)} all-reduce(f32[2,256]{1,0:T(2,128)S(1)} %reduce_sum.69), channel_id=1, replica_groups=mesh['seq'=8,'chan'=4] {'chan'}, use_global_device_ids=true, to_apply=%region_5.6 | all-reduce | flops 512 | bytes 4096 | tf_op jit(solution)/shard_map/psum | solution.py:72
  103.4 1.9 collective-permute-start.4
  106.7 3.2 collective-permute-done.5
  116.5 22.3 %reduce-scatter.29.cloned.1.call-done = bf16[96,512]{1,0:T(8,128)(2,1)} async-done(((bf16[384,512]{1,0:T(8,128)(2,1)}), bf16[96,512]{1,0:T(8,128)(2,1)}) %reduce-scatter.29.cloned.1.call-update) | async-done | bytes 98320
  140.6 8.7 %psum.44 = f32[2,256]{1,0:T(2,128)S(1)} all-reduce(f32[2,256]{1,0:T(2,128)S(1)} %reduce_sum.71), channel_id=1, replica_groups=mesh['seq'=8,'chan'=4] {'chan'}, use_global_device_ids=true, to_apply=%region_8.9 | all-reduce | flops 512 | bytes 4096 | tf_op jit(solution)/shard_map/psum | solution.py:72
  152.4 3.4 collective-permute-done.7
  157.7 1.8 fusion.3
  160.5 22.3 %reduce-scatter.31.cloned.1.call-done = bf16[96,512]{1,0:T(8,128)(2,1)} async-done(((bf16[384,512]{1,0:T(8,128)(2,1)}), bf16[96,512]{1,0:T(8,128)(2,1)}) %reduce-scatter.31.cloned.1.call-update) | async-done | bytes 98320
  184.1 8.7 %psum.45 = f32[2,256]{1,0:T(2,128)S(1)} all-reduce(f32[2,256]{1,0:T(2,128)S(1)} %reduce_sum.73), channel_id=1, replica_groups=mesh['seq'=8,'chan'=4] {'chan'}, use_global_device_ids=true, to_apply=%region_11.12 | all-reduce | flops 512 | bytes 4096 | tf_op jit(solution)/shard_map/psum | solution.py:72
  193.7 1.9 collective-permute-start.8
  195.6 1.5 collective-permute-start.9
  197.2 2.8 collective-permute-done.9
  205.8 22.3 %reduce-scatter.33.cloned.1.call-done = bf16[96,512]{1,0:T(8,128)(2,1)} async-done(((bf16[384,512]{1,0:T(8,128)(2,1)}), bf16[96,512]{1,0:T(8,128)(2,1)}) %reduce-scatter.33.cloned.1.call-update) | async-done | bytes 98320
  230.0 8.7 %psum.46 = f32[2,256]{1,0:T(2,128)S(1)} all-reduce(f32[2,256]{1,0:T(2,128)S(1)} %reduce_sum.75), channel_id=1, replica_groups=mesh['seq'=8,'chan'=4] {'chan'}, use_global_device_ids=true, to_apply=%region_14.15 | all-reduce | flops 512 | bytes 4096 | tf_op jit(solution)/shard_map/psum | solution.py:72
  241.8 3.4 collective-permute-done.11
  248.8 22.3 %reduce-scatter.35.cloned.1.call-done = bf16[96,512]{1,0:T(8,128)(2,1)} async-done(((bf16[384,512]{1,0:T(8,128)(2,1)}), bf16[96,512]{1,0:T(8,128)(2,1)}) %reduce-scatter.35.cloned.1.call-update) | async-done | bytes 98320
  272.3 8.8 %psum.47 = f32[2,256]{1,0:T(2,128)S(1)} all-reduce(f32[2,256]{1,0:T(2,128)S(1)} %reduce_sum.77), channel_id=1, replica_groups=mesh['seq'=8,'chan'=4] {'chan'}, use_global_device_ids=true, to_apply=%region_17.18 | all-reduce | flops 512 | bytes 4096 | tf_op jit(solution)/shard_map/psum | solution.py:72
  284.1 3.4 collective-permute-done.13
  291.1 22.3 %reduce-scatter.37.cloned.1.call-done = bf16[96,512]{1,0:T(8,128)(2,1)} async-done(((bf16[384,512]{1,0:T(8,128)(2,1)}), bf16[96,512]{1,0:T(8,128)(2,1)}) %reduce-scatter.37.cloned.1.call-update) | async-done | bytes 98320
  315.9 1.5 collective-permute-start.15
  317.5 3.3 collective-permute-done.15
  332.0 10.0 %copy.104 = bf16[9,96,4,512]{3,2,1,0:T(4,128)(2,1)} copy(bf16[9,96,4,512]{1,2,3,0:T(4,128)(2,1)} %bitcast_dynamic-update-slice_fusion) | data formatting | bytes 7077888 | tf_op jit(solution)/shard_map/stack | solution.py:41
  342.0 3.1 copy.154
  345.2 1.9 fusion
  347.1 24.1 %reduce-scatter.23.cloned.1.call-done = bf16[48,2048]{1,0:T(8,128)(2,1)} async-done(((bf16[192,2048]{1,0:T(8,128)(2,1)}), bf16[48,2048]{1,0:T(8,128)(2,1)}) %reduce-scatter.23.cloned.1.call-update) | async-done | bytes 196624 | tf_op jit(solution)/shard_map/reduce_scatter | solution.py:64
  (230 shorter events, 72.4 us)
Async XLA Ops:
  6.5 338.6 %copy-start = (bf16[9,96,192]{2,1,0:T(8,128)(2,1)S(1)}, bf16[9,96,192]{2,1,0:T(8,128)(2,1)}, u32[]{:S(2)}) copy-start(bf16[9,96,192]{2,1,0:T(8,128)(2,1)} %param.16) | copy-start | bytes 995332
  6.5 40.9 %reduce-scatter.25.cloned.1.call-start = ((), (), s32[]{:S(2)}) async-start(), calls=%async_computation.10 | async-start | bytes 491520
  18.6 3.4 collective-permute-start
  19.9 4.8 %collective-permute-start.1 = (bf16[4,1,256]{2,1,0:T(2,128)(2,1)S(1)}, bf16[4,1,256]{2,1,0:T(2,128)(2,1)S(1)}, u32[]{:S(2)}, u32[]{:S(2)}) collective-permute-start(bf16[4,1,256]{2,1,0:T(2,128)(2,1)S(1)} %get-tuple-element.42), channel_id=1, source_target_pairs={{4,0},{8,4},{12,8},{16,12},{20,16},{24,20},{28,24},{5,1},{9,5},{13... | collective-permute-start | bytes 6152 | tf_op jit(solution)/shard_map/ppermute | solution.py:22
  26.5 65.4 %reduce-scatter.27.cloned.1.call-start = ((), (), s32[]{:S(2)}) async-start(), calls=%async_computation.11 | async-start | bytes 491520
  27.9 36.6 %copy-start.4 = (f32[96]{0:T(128)}, f32[96]{0:T(128)S(1)}, u32[]{:S(2)}) copy-start(f32[96]{0:T(128)S(1)} %get-tuple-element.59) | copy-start | bytes 1156
  27.9 36.6 %copy-start.5 = (f32[96]{0:T(128)}, f32[96]{0:T(128)S(1)}, u32[]{:S(2)}) copy-start(f32[96]{0:T(128)S(1)} %get-tuple-element.62) | copy-start | bytes 1156
  27.9 165.0 %copy-start.3 = (f32[96]{0:T(128)}, f32[96]{0:T(128)S(1)}, u32[]{:S(2)}) copy-start(f32[96]{0:T(128)S(1)} %get-tuple-element.65) | copy-start | bytes 1156
  58.3 6.4 %collective-permute-start.2 = (bf16[96,1,256]{2,0,1:T(8,128)(2,1)S(1)}, bf16[96,1,256]{2,0,1:T(8,128)(2,1)S(1)}, u32[]{:S(2)}, u32[]{:S(2)}) collective-permute-start(bf16[96,1,256]{2,0,1:T(8,128)(2,1)S(1)} %get-tuple-element.39), channel_id=1, source_target_pairs={{0,4},{4,8},{8,12},{12,16},{16,20},{20,24},{24,28},{1,5},{5,9},{9,... | collective-permute-start | bytes 147464 | tf_op jit(solution)/shard_map/ppermute | solution.py:21
  59.6 5.1 %collective-permute-start.3 = (bf16[96,1,256]{2,0,1:T(8,128)(2,1)S(1)}, bf16[96,1,256]{2,0,1:T(8,128)(2,1)S(1)}, u32[]{:S(2)}, u32[]{:S(2)}) collective-permute-start(bf16[96,1,256]{2,0,1:T(8,128)(2,1)S(1)} %get-tuple-element.40), channel_id=1, source_target_pairs={{4,0},{8,4},{12,8},{16,12},{20,16},{24,20},{28,24},{5,1},{9,5},{13... | collective-permute-start | bytes 147464 | tf_op jit(solution)/shard_map/ppermute | solution.py:22
  68.9 69.9 %reduce-scatter.29.cloned.1.call-start = ((), (), s32[]{:S(2)}) async-start(), calls=%async_computation.12 | async-start | bytes 491520
  103.4 3.3 collective-permute-start.4
  105.2 4.7 %collective-permute-start.5 = (bf16[96,1,256]{2,0,1:T(8,128)(2,1)}, bf16[96,1,256]{2,0,1:T(8,128)(2,1)}, u32[]{:S(2)}, u32[]{:S(2)}) collective-permute-start(bf16[96,1,256]{2,0,1:T(8,128)(2,1)} %get-tuple-element.38), channel_id=1, source_target_pairs={{4,0},{8,4},{12,8},{16,12},{20,16},{24,20},{28,24},{5,1},{9,5},{13... | collective-permute-start | bytes 147464 | tf_op jit(solution)/shard_map/ppermute | solution.py:22
  116.5 66.4 %reduce-scatter.31.cloned.1.call-start = ((), (), s32[]{:S(2)}) async-start(), calls=%async_computation.13 | async-start | bytes 491520
  149.7 2.7 collective-permute-start.6
  151.0 4.8 %collective-permute-start.7 = (bf16[96,1,256]{2,0,1:T(8,128)(2,1)S(1)}, bf16[96,1,256]{2,0,1:T(8,128)(2,1)S(1)}, u32[]{:S(2)}, u32[]{:S(2)}) collective-permute-start(bf16[96,1,256]{2,0,1:T(8,128)(2,1)S(1)} %get-tuple-element.36), channel_id=1, source_target_pairs={{4,0},{8,4},{12,8},{16,12},{20,16},{24,20},{28,24},{5,1},{9,5},{13... | collective-permute-start | bytes 147464 | tf_op jit(solution)/shard_map/ppermute | solution.py:22
  156.1 27.8 %copy-start.9 = (f32[96]{0:T(128)S(1)}, f32[96]{0:T(128)}, u32[]{:S(2)}) copy-start(f32[96]{0:T(128)} %get-tuple-element.45) | copy-start | bytes 1156
  159.5 44.6 %copy-start.1 = (bf16[1,1,9,96,384]{4,3,2,1,0:T(8,128)(2,1)S(1)}, bf16[1,1,9,96,384]{4,3,2,1,0:T(8,128)(2,1)}, u32[]{:S(2)}) copy-start(bf16[1,1,9,96,384]{4,3,2,1,0:T(8,128)(2,1)} %get-tuple-element.10) | copy-start | bytes 1990660
  160.5 67.7 %reduce-scatter.33.cloned.1.call-start = ((), (), s32[]{:S(2)}) async-start(), calls=%async_computation.14 | async-start | bytes 491520
  193.7 3.5 collective-permute-start.8
  195.6 4.5 %collective-permute-start.9 = (bf16[96,1,256]{2,0,1:T(8,128)(2,1)}, bf16[96,1,256]{2,0,1:T(8,128)(2,1)S(1)}, u32[]{:S(2)}, u32[]{:S(2)}) collective-permute-start(bf16[96,1,256]{2,0,1:T(8,128)(2,1)} %get-tuple-element.34), channel_id=1, source_target_pairs={{4,0},{8,4},{12,8},{16,12},{20,16},{24,20},{28,24},{5,1},{9,5},{13... | collective-permute-start | bytes 147464 | tf_op jit(solution)/shard_map/ppermute | solution.py:22
  205.8 65.3 %reduce-scatter.35.cloned.1.call-start = ((), (), s32[]{:S(2)}) async-start(), calls=%async_computation.15 | async-start | bytes 491520
  239.1 2.7 collective-permute-start.10
  240.4 4.8 %collective-permute-start.11 = (bf16[96,1,256]{2,0,1:T(8,128)(2,1)S(1)}, bf16[96,1,256]{2,0,1:T(8,128)(2,1)S(1)}, u32[]{:S(2)}, u32[]{:S(2)}) collective-permute-start(bf16[96,1,256]{2,0,1:T(8,128)(2,1)S(1)} %get-tuple-element.32), channel_id=1, source_target_pairs={{4,0},{8,4},{12,8},{16,12},{20,16},{24,20},{28,24},{5,1},{9,5},{13... | collective-permute-start | bytes 147464 | tf_op jit(solution)/shard_map/ppermute | solution.py:22
  245.4 26.7 %copy-start.8 = (f32[96]{0:T(128)S(1)}, f32[96]{0:T(128)}, u32[]{:S(2)}) copy-start(f32[96]{0:T(128)} %get-tuple-element.48) | copy-start | bytes 1156
  248.8 64.6 %reduce-scatter.37.cloned.1.call-start = ((), (), s32[]{:S(2)}) async-start(), calls=%async_computation.16 | async-start | bytes 491520
  281.4 2.7 collective-permute-start.12
  282.7 4.8 %collective-permute-start.13 = (bf16[96,1,256]{2,0,1:T(8,128)(2,1)S(1)}, bf16[96,1,256]{2,0,1:T(8,128)(2,1)S(1)}, u32[]{:S(2)}, u32[]{:S(2)}) collective-permute-start(bf16[96,1,256]{2,0,1:T(8,128)(2,1)S(1)} %get-tuple-element.30), channel_id=1, source_target_pairs={{4,0},{8,4},{12,8},{16,12},{20,16},{24,20},{28,24},{5,1},{9,5},{13... | collective-permute-start | bytes 147464 | tf_op jit(solution)/shard_map/ppermute | solution.py:22
  287.7 26.7 %copy-start.7 = (f32[96]{0:T(128)S(1)}, f32[96]{0:T(128)}, u32[]{:S(2)}) copy-start(f32[96]{0:T(128)} %get-tuple-element.43) | copy-start | bytes 1156
  291.1 80.2 %reduce-scatter.23.cloned.1.call-start = ((), (), s32[]{:S(2)}) async-start(), calls=%async_computation.9 | async-start | bytes 983040 | tf_op jit(solution)/shard_map/reduce_scatter | solution.py:64
  314.6 2.8 collective-permute-start.14
  315.9 4.8 %collective-permute-start.15 = (bf16[96,1,256]{2,0,1:T(8,128)(2,1)S(1)}, bf16[96,1,256]{2,0,1:T(8,128)(2,1)S(1)}, u32[]{:S(2)}, u32[]{:S(2)}) collective-permute-start(bf16[96,1,256]{2,0,1:T(8,128)(2,1)S(1)} %get-tuple-element.28), channel_id=1, source_target_pairs={{4,0},{8,4},{12,8},{16,12},{20,16},{24,20},{28,24},{5,1},{9,5},{13... | collective-permute-start | bytes 147464 | tf_op jit(solution)/shard_map/ppermute | solution.py:22
  (3 other events, 32.8 us)
Sparse Core Ops, SparseCore 0:
  26.6 20.7 reduce-scatter.24
  69.0 22.8 reduce-scatter.26
  116.6 22.1 reduce-scatter.28
  160.6 22.2 reduce-scatter.30
  205.9 22.2 reduce-scatter.32
  248.9 22.1 reduce-scatter.34
  291.2 22.1 reduce-scatter.36
  347.2 23.9 reduce-scatter.22
where the time goes:
time: 382 us; the launch traced here: 380 us
  waiting for transfers between devices  200 us (52%)
  blocking collectives  64.4 us (17%)
  local copies, waits for them, and re-layouts  57.1 us (15%)
  starting transfers between devices  22.5 us (6%)
  between operations  14.8 us (4%)
  other arithmetic  13.7 us (4%)
  matrix products  7.59 us (2%)
    unnamed x15, waiting for transfers between devices  153 us
    psum x6, blocking collectives, rms_norm(): totals = lax.psum(squares, 'chan')  52.4 us
    unnamed x89, local copies, waits for them, and re-layouts  28.5 us
    reduce_scatter x1, waiting for transfers between devices, up_block(): lax.psum_scatter(contract(flat_weight, columns).astype(jnp.bfloat16), 'ch...  24.1 us
    ppermute x8, waiting for transfers between devices, padded_2(): after = lax.ppermute(first, axis, down)  22.3 us
    another operation x16, local copies, waits for them, and re-layouts, gather_columns(): return jnp.stack(shifted, 0).reshape(9 * chans, height * width)  17.3 us
    all_to_all x1, blocking collectives, body(): lax.all_to_all(latent, 'chan', split_axis=1, concat_axis=0, tiled=True)  12 us
    ppermute x8, starting transfers between devices, padded_2(): before = lax.ppermute(last, axis, up)  11.5 us
  transfers between devices with their start and end apart: 24, of which 15 were waited for; matrix products, arithmetic and copies ran while one was open for 2% of the time, Pallas kernels for 0%

commit v1 on v0

v1 whole, which is shorter than its diff:
```python
import functools
import jax
import jax.numpy as jnp
from jax import lax
from jax.experimental import pallas as pl
from jax.experimental.pallas import tpu as pltpu
from jax.sharding import PartitionSpec as P

LAT_W = 256
EPS = 1e-06
HALO = 8
VMEM_BYTES = 48 * 1024 * 1024

CORE, NEAR, FAR = 1, 2, 4


def place():
    seq = lax.axis_index("seq")
    return lax.rem(seq, 2), lax.rem(lax.div(seq, 2), 4)


def swap(array, mask):
    seqs, chans = lax.axis_size("seq"), lax.axis_size("chan")
    pairs = [(s * chans + c, (s ^ mask) * chans + c) for s in range(seqs) for c in range(chans)]
    return lax.ppermute(array, ("seq", "chan"), pairs)


def shift(array):
    seqs, chans = lax.axis_size("seq"), lax.axis_size("chan")
    pairs = [(s * chans + c, s * chans + (c + 1) % chans) for s in range(seqs) for c in range(chans)]
    return lax.ppermute(array, ("seq", "chan"), pairs)


def spread(own):
    units = own.shape[0]
    half = units // 2
    held = own
    pieces = []
    for step in range(1, lax.axis_size("chan")):
        held = shift(held)
        near = swap(held, NEAR)
        far = swap(held, FAR)
        low = swap(far[:half], NEAR)
        high = swap(near[half:], FAR)
        for chip, first, array in ((0, 0, held), (1, 0, near), (2, 0, far), (3, 0, low), (3, half, high)):
            pieces.append(((step, chip, 0, first, array.shape[0]), array))
            pieces.append(((step, chip, 1, first, array.shape[0]), swap(array, CORE)))
    return tuple(p[0] for p in pieces), tuple(p[1] for p in pieces)


def own_slice(units, per_chip):
    core, chip = place()
    rows = units.shape[1] // 2
    return lax.dynamic_slice(units, (chip * per_chip, core * rows, 0), (per_chip, rows, units.shape[2]))


def load_weights(meta, per_chip, chans, own, pieces, weights, sems):
    core, chip = place()
    chan = lax.axis_index("chan")
    copies = []
    for ref, first, start, count in own:
        depth = ref.shape[1]
        base = pl.multiple_of(chan * depth, 16)
        copies.append((ref.at[pl.ds(first, count)], weights.at[pl.ds(start, count), pl.ds(base, depth), :]))
    for (step, chip_mask, core_mask, first, count), ref in zip(meta, pieces):
        depth = ref.shape[1]
        shard = lax.rem(chan + chans - step, chans)
        start = (chip ^ chip_mask) * per_chip + first
        base = pl.multiple_of(shard * (2 * depth) + (core ^ core_mask) * depth, 16)
        copies.append((ref, weights.at[pl.ds(start, count), pl.ds(base, depth), :]))
    started = [pltpu.make_async_copy(src, dst, sems.at[i]) for i, (src, dst) in enumerate(copies)]
    for copy in started:
        copy.start()

    def wait():
        for copy in started:
            copy.wait()

    return wait


def inside(rows, width, first_row, first_col, height):
    row = first_row + lax.broadcasted_iota(jnp.int32, (rows, width, 1), 0)
    col = first_col + lax.broadcasted_iota(jnp.int32, (rows, width, 1), 1)
    ok = (row >= 0) & (row < height) & (col >= 0) & (col < LAT_W)
    return jnp.where(ok, 1.0, 0.0).astype(jnp.float32).reshape(rows * width, 1)


def norm_act(values, gain, shift_by, mask):
    mean_sq = jnp.mean(values * values, axis=1, keepdims=True)
    scaled = values * lax.rsqrt(mean_sq + EPS) * gain + shift_by
    return scaled / (1.0 + jnp.exp(-scaled)) * mask


def set_columns(cols, values):
    cells, chans = values.shape
    cols[:cells, :chans] = pltpu.roll(values, 1, 0).astype(jnp.bfloat16)
    cols[:cells, chans : 2 * chans] = values.astype(jnp.bfloat16)
    cols[:cells, 2 * chans :] = pltpu.roll(values, cells - 1, 0).astype(jnp.bfloat16)


def conv(cols, weights, unit, rows, width):
    chans = weights.shape[1]
    total = None
    for row_tap in range(3):
        taps = weights[unit + 3 * row_tap : unit + 3 * row_tap + 3].reshape(3 * chans, chans)
        part = jnp.dot(
            cols[row_tap * width : (row_tap + rows) * width, :], taps, preferred_element_type=jnp.float32
        )
        total = part if total is None else total + part
    return total


def res_block(stream, rows, width, block, unit, params, cols, weights, corner, height, wait):
    gain, shift_by, bias = params
    first_row, first_col = corner
    mask = inside(rows, width, first_row, first_col, height)
    set_columns(cols, norm_act(stream, gain[2 * block][None], shift_by[2 * block][None], mask))
    if wait is not None:
        wait()
    middle = conv(cols, weights, unit, rows - 2, width) + bias[2 * block][None]
    mask = inside(rows - 2, width, first_row + 1, first_col, height)
    set_columns(cols, norm_act(middle, gain[2 * block + 1][None], shift_by[2 * block + 1][None], mask))
    branch = conv(cols, weights, unit + 9, rows - 4, width) + bias[2 * block + 1][None]
    kept = stream[2 * width : (rows - 2) * width]
    return (kept + branch).astype(jnp.bfloat16).astype(jnp.float32)


def tile_corner(slab_rows, tile_cols, halo):
    return (
        lax.axis_index("seq") * slab_rows - halo,
        lax.axis_index("chan") * tile_cols - HALO,
    )


def early_kernel(meta, per_chip, chans, blocks, width, slab_rows, height, n_pieces, *refs):
    stream_ref, gain, shift_by, bias, res_ref = refs[:5]
    pieces = refs[5 : 5 + n_pieces]
    out_ref, weights, cols, sems = refs[5 + n_pieces :]
    wait = load_weights(
        meta, per_chip, chans, ((res_ref, 0, 0, 18 * blocks),), pieces, weights, sems
    )
    rows = stream_ref.shape[0] // width
    halo = (rows - slab_rows) // 2
    tile_cols = LAT_W // chans
    stream = stream_ref[...].astype(jnp.float32)
    for block in range(blocks):
        stream = res_block(
            stream, rows, width, block, 18 * block, (gain, shift_by, bias), cols, weights,
            tile_corner(slab_rows, tile_cols, halo), height, wait if block == 0 else None,
        )
        rows, halo = rows - 4, halo - 2
    out_ref[...] = stream.astype(jnp.bfloat16)


def late_kernel(meta, per_chip, chans, first_block, blocks, width, slab_rows, height, n_pieces, *refs):
    stream_ref, gain, shift_by, bias, up_bias, res_ref, up_ref = refs[:7]
    pieces = refs[7 : 7 + n_pieces]
    out_ref, weights, cols, woven, sems = refs[7 + n_pieces :]
    n_units = 18 * (blocks - first_block)
    wait = load_weights(
        meta, per_chip, chans,
        ((res_ref, 18 * first_block, 0, n_units), (up_ref, 0, n_units, up_ref.shape[0])),
        pieces, weights, sems,
    )
    rows = stream_ref.shape[0] // width
    halo = (rows - slab_rows) // 2
    tile_cols = LAT_W // chans
    stream = stream_ref[...].astype(jnp.float32)
    for block in range(first_block, blocks):
        stream = res_block(
            stream, rows, width, block, 18 * (block - first_block), (gain, shift_by, bias), cols, weights,
            tile_corner(slab_rows, tile_cols, halo), height, wait if block == first_block else None,
        )
        rows, halo = rows - 4, halo - 2
    first_row, first_col = tile_corner(slab_rows, tile_cols, halo)
    framed = (stream * inside(rows, width, first_row, first_col, height)).astype(jnp.bfloat16)
    outs = up_bias.shape[1]
    products = []
    for pair in range(5):
        both = jnp.dot(framed, weights[n_units + pair], preferred_element_type=jnp.float32)
        products += [both[:, :outs], both[:, outs:]]
    cells = rows * width
    even, odd = [], []
    for row_tap in range(3):
        left, mid, right = products[3 * row_tap : 3 * row_tap + 3]
        even.append(pltpu.roll(left, 1, 0) + mid + right)
        odd.append(left + mid + pltpu.roll(right, cells - 1, 0))
    share = outs // chans
    for row in range(slab_rows):
        for low in range(2):
            for parity, parts in ((0, even), (1, odd)):
                total = up_bias[...]
                for row_tap in range(3):
                    at = (row + 1 + (low + row_tap - 1) // 2) * width + HALO
                    total = total + parts[row_tap][at : at + tile_cols]
                for tile in range(woven.shape[0]):
                    lanes = total[:, 128 * tile : 128 * tile + 128]
                    if lanes.shape[1] < 128:
                        blank = jnp.zeros((tile_cols, 128 - lanes.shape[1]), jnp.float32)
                        lanes = jnp.concatenate([lanes, blank], 1)
                    woven[tile, pl.ds(parity, tile_cols, 2), :] = lanes
            turned = jnp.concatenate([woven[tile].T for tile in range(woven.shape[0])], 0)
            for owner in range(chans):
                out_ref[owner, 2 * row + low] = turned[owner * share : (owner + 1) * share].astype(jnp.bfloat16)


def call(kernel, args, n_vmem, out_shape, scratch, flops):
    vmem = pl.BlockSpec(memory_space=pltpu.VMEM)
    return pl.pallas_call(
        kernel,
        out_shape=out_shape,
        in_specs=[vmem] * n_vmem + [pl.BlockSpec(memory_space=pl.ANY)] * (len(args) - n_vmem),
        out_specs=vmem,
        scratch_shapes=scratch,
        compiler_params=pltpu.CompilerParams(vmem_limit_bytes=VMEM_BYTES),
        cost_estimate=pl.CostEstimate(flops=flops, bytes_accessed=16 * 1024 * 1024, transcendentals=0),
    )(*args)


def body(
    latent, in_weight, in_bias, norm_gain, norm_shift, res_weight, res_bias, up_weight, up_bias
):
    seqs, chans = lax.axis_size("seq"), lax.axis_size("chan")
    seq, chan = lax.axis_index("seq"), lax.axis_index("chan")
    layers, _, taps, depth, ch = res_weight.shape
    outs = up_weight.shape[2]
    tokens, lat_share = latent.shape[0], latent.shape[1] // chans
    slab_rows = tokens * chans // LAT_W
    height = slab_rows * seqs
    tile_cols = LAT_W // chans
    width = -(-(tile_cols + 2 * HALO) // 16) * 16
    early = layers - 1

    res_units = res_weight.reshape(layers * 2 * taps, depth, ch)
    per_early = early * 2 * taps // 4
    early_meta, early_pieces = spread(own_slice(res_units[: early * 2 * taps], per_early))
    up_units = jnp.pad(up_weight, ((0, 1), (0, 0), (0, 0))).reshape(-1, 2, depth, outs)
    up_units = up_units.transpose(0, 2, 1, 3).reshape(-1, depth, 2 * outs)
    late_units = jnp.concatenate([res_units[early * 2 * taps :], up_units], 0)
    per_late = -(-late_units.shape[0] // 4)
    late_units = jnp.pad(late_units, ((0, 4 * per_late - late_units.shape[0]), (0, 0), (0, 0)))
    late_meta, late_pieces = spread(own_slice(late_units, per_late))

    smalls = [in_weight, in_bias, norm_gain, norm_shift, res_bias, up_bias, latent]
    flat = jnp.concatenate([a.astype(jnp.float32).reshape(-1) for a in smalls])
    flat = jnp.pad(flat, (0, -flat.shape[0] % 1024))
    packed = lax.all_gather(flat, "chan")
    found, at = [], 0
    for a in smalls:
        found.append(packed[:, at : at + a.size].reshape((chans,) + a.shape))
        at += a.size
    in_w = found[0].transpose(1, 0, 2, 3).reshape(taps * lat_share * chans, ch).astype(jnp.bfloat16)
    in_b = found[1].reshape(ch)
    gain, shift_by, bias = (f.transpose(1, 2, 0, 3).reshape(2 * layers, ch) for f in found[2:5])
    up_b = found[5].reshape(1, outs)
    slab = found[6].astype(jnp.bfloat16).reshape(slab_rows * LAT_W, lat_share * chans)
    frame = lax.all_gather(slab, "seq", tiled=True).reshape(height, LAT_W, lat_share * chans)
    rows = slab_rows + 2 * (HALO - 1)
    framed = jnp.pad(frame, ((HALO, HALO), (HALO + 1, width - tile_cols - HALO + 1), (0, 0)))
    region = lax.dynamic_slice(
        framed, (seq * slab_rows, chan * tile_cols, 0), (rows + 2, width + 2, framed.shape[2])
    )
    patches = jnp.concatenate(
        [region[p : p + rows, r : r + width] for p in range(3) for r in range(3)], axis=2
    ).reshape(rows * width, -1)
    stream = (jnp.dot(patches, in_w, preferred_element_type=jnp.float32) + in_b).astype(jnp.bfloat16)

    def flops(first, blocks):
        cells = sum(slab_rows + 2 * (2 * layers - i) for i in range(2 * first + 1, 2 * blocks + 1)) * width
        return 2 * taps * ch * ch * cells

    early_args = [stream, gain, shift_by, bias, res_units, *early_pieces]
    mid_rows = rows - 4 * early
    stream = call(
        functools.partial(
            early_kernel, early_meta, per_early, chans, early, width, slab_rows, height, len(early_pieces)
        ),
        early_args, 4, jax.ShapeDtypeStruct((mid_rows * width, ch), jnp.bfloat16),
        [
            pltpu.VMEM((4 * per_early, ch, ch), jnp.bfloat16),
            pltpu.VMEM((rows * width, 3 * ch), jnp.bfloat16),
            pltpu.SemaphoreType.DMA((1 + len(early_pieces),)),
        ],
        flops(0, early),
    )
    late_args = [stream, gain, shift_by, bias, up_b, res_units, up_units, *late_pieces]
    shares = call(
        functools.partial(
            late_kernel, late_meta, per_late, chans, early, layers, width, slab_rows, height, len(late_pieces)
        ),
        late_args, 5, jax.ShapeDtypeStruct((chans, 2 * slab_rows, outs // chans, 2 * tile_cols), jnp.bfloat16),
        [
            pltpu.VMEM((4 * per_late, ch, ch), jnp.bfloat16),
            pltpu.VMEM((mid_rows * width, 3 * ch), jnp.bfloat16),
            pltpu.VMEM((-(-outs // 128), 2 * tile_cols, 128), jnp.float32),
            pltpu.SemaphoreType.DMA((2 + len(late_pieces),)),
        ],
        flops(early, layers),
    )
    turned = lax.all_to_all(shares, "chan", 0, 0, tiled=True)
    return turned.transpose(2, 1, 0, 3).reshape(outs // chans, 2 * slab_rows, 2 * LAT_W)


def solution(mesh):
    placed = (
        P(("seq", "chan"), None),
        P(None, "chan", None),
        P("chan"),
        P(None, None, "chan"),
        P(None, None, "chan"),
        P(None, None, None, "chan", None),
        P(None, None, "chan"),
        P(None, "chan", None),
        P("chan"),
    )
    return jax.shard_map(
        body, mesh=mesh, in_specs=placed, out_specs=P("chan", "seq", None), check_vma=False
    )
```

time: 382 us -> 214 us (0.56)
  waiting for transfers between devices: 200 us -> 44.4 us
  Pallas kernels: 0 us -> 31 us
  blocking collectives: 64.4 us -> 39.2 us
  starting transfers between devices: 22.5 us -> 41.2 us
  between operations: 14.8 us -> 0.53 us
  other arithmetic: 13.7 us -> 1.14 us
  matrix products: 7.59 us -> 2.54 us
  local copies, waits for them, and re-layouts: 57.1 us -> 52.7 us
    unnamed x15 -> x0, waiting for transfers between devices: 153 us -> none
    psum x6 -> x0, blocking collectives: 52.4 us -> none  [rms_norm(): totals = lax.psum(squares, 'chan')]
    pallas_call x0 -> x2, Pallas kernels: none -> 31 us  [call(): pl.pallas_call(kernel, out_shape=out_shape, in_specs=[vmem] * n_vmem + [p...]
    all_gather x0 -> x2, blocking collectives: none -> 26.2 us  [the longest x1 15.3 us: body(): packed = lax.all_gather(flat, 'chan')]
    reduce_scatter x1 -> x0, waiting for transfers between devices: 24.1 us -> none  [up_block(): lax.psum_scatter(contract(flat_weight, columns).astype(jnp.bfloat16), 'ch...]
    ppermute x16 -> x60, waiting for transfers between devices: 22.3 us -> 44.4 us  [the longest x54 26.9 us: swap(): return lax.ppermute(array, ('seq', 'chan'), pairs)]
    ppermute x16 -> x60, starting transfers between devices: 22.2 us -> 41.2 us  [the longest x54 35.8 us: swap(): return lax.ppermute(array, ('seq', 'chan'), pairs)]
    another operation x16 -> x0, local copies, waits for them, and re-layouts: 17.3 us -> none  [gather_columns(): return jnp.stack(shifted, 0).reshape(9 * chans, height * width)]
  transfers between devices with their start and end apart: 24 -> 60, of which waited for: 15 -> 12; matrix products, arithmetic and copies ran while one was open for 2% -> 15% of each run, Pallas kernels for 0% -> 11%
where the time goes in v1:
time: 214 us; the launch traced here: 213 us
  local copies, waits for them, and re-layouts  52.7 us (25%)
  waiting for transfers between devices  44.4 us (21%)
  starting transfers between devices  41.2 us (19%)
  blocking collectives  39.2 us (18%)
  Pallas kernels  31 us (14%)
  matrix products  2.54 us (1%)
    ppermute x54, starting transfers between devices, swap(): return lax.ppermute(array, ('seq', 'chan'), pairs)  35.8 us
    pallas_call x2, Pallas kernels, call(): pl.pallas_call(kernel, out_shape=out_shape, in_specs=[vmem] * n_vmem + [p...  31 us
    ppermute x54, waiting for transfers between devices, swap(): return lax.ppermute(array, ('seq', 'chan'), pairs)  26.9 us
    unnamed x94, local copies, waits for them, and re-layouts  20.5 us
    ppermute x6, waiting for transfers between devices, shift(): return lax.ppermute(array, ('seq', 'chan'), pairs)  17.5 us
    all_gather x1, blocking collectives, body(): packed = lax.all_gather(flat, 'chan')  15.3 us
    all_to_all x1, blocking collectives, body(): turned = lax.all_to_all(shares, 'chan', 0, 0, tiled=True)  13 us
    all_gather x1, blocking collectives, body(): lax.all_gather(slab, 'seq', tiled=True)  10.9 us
  transfers between devices with their start and end apart: 60, of which 12 were waited for; matrix products, arithmetic and copies ran while one was open for 15% of the time, Pallas kernels for 11%

profile of v1, /device:TPU:0, one launch (start us, length us, event | category | flops | bytes accessed | tf_op | source)
XLA Modules:
  0.0 212.8 jit_solution(8448502110872512323)
XLA Ops:
  2.6 3.1 %collective-permute-start.30 = (bf16[6,48,384]{2,1,0:T(8,128)(2,1)S(1)}, bf16[6,48,384]{2,1,0:T(8,128)(2,1)S(1)}, u32[]{:S(2)}, u32[]{:S(2)}) collective-permute-start(bf16[6,48,384]{2,1,0:T(8,128)(2,1)S(1)} %fusion.3), channel_id=1, source_target_pairs={{0,1},{1,2},{2,3},{3,0},{4,5},{5,6},{6,7},{7,4},{8,9},{9,10},{10,1... | collective-permute-start | bytes 663560 | tf_op jit(solution)/shard_map/ppermute | solution.py:31
  5.7 1.7 collective-permute-start
  7.4 6.5 %collective-permute-done.30.refs_7_ = bf16[6,48,384]{2,1,0:T(8,128)(2,1)S(1)} collective-permute-done((bf16[6,48,384]{2,1,0:T(8,128)(2,1)S(1)}, bf16[6,48,384]{2,1,0:T(8,128)(2,1)S(1)}, u32[]{:S(2)}, u32[]{:S(2)}) %collective-permute-start.30) | collective-permute-done | bytes 221216 | tf_op jit(solution)/shard_map/ppermute | solution.py:31
  13.9 1.8 collective-permute-start.34
  17.2 3.8 %collective-permute-done.refs_5_ = bf16[9,48,384]{2,1,0:T(8,128)(2,1)S(1)} collective-permute-done((bf16[9,48,384]{2,1,0:T(8,128)(2,1)S(1)}, bf16[9,48,384]{2,1,0:T(8,128)(2,1)S(1)}, u32[]{:S(2)}, u32[]{:S(2)}) %collective-permute-start) | collective-permute-done | bytes 331808 | tf_op jit(solution)/shard_map/ppermute | solution.py:31
  21.1 1.8 collective-permute-start.2
  22.9 3.0 %collective-permute-done.40.refs_17_ = bf16[6,48,384]{2,1,0:T(8,128)(2,1)S(1)} collective-permute-done((bf16[6,48,384]{2,1,0:T(8,128)(2,1)S(1)}, bf16[6,48,384]{2,1,0:T(8,128)(2,1)S(1)}, u32[]{:S(2)}, u32[]{:S(2)}) %collective-permute-start.40) | collective-permute-done | bytes 221216 | tf_op jit(solution)/shard_map/ppermute | solution.py:31
  25.9 1.7 collective-permute-start.36
  29.1 2.6 %collective-permute-done.36.refs_13_ = bf16[3,48,384]{2,1,0:T(8,128)(2,1)S(1)} collective-permute-done((bf16[3,48,384]{2,1,0:T(8,128)(2,1)S(1)}, bf16[3,48,384]{2,1,0:T(8,128)(2,1)S(1)}, u32[]{:S(2)}, u32[]{:S(2)}) %collective-permute-start.36) | collective-permute-done | bytes 110624 | tf_op jit(solution)/shard_map/ppermute | solution.py:25
  32.9 4.4 %collective-permute-done.38.refs_15_ = bf16[3,48,384]{2,1,0:T(8,128)(2,1)S(1)} collective-permute-done((bf16[3,48,384]{2,1,0:T(8,128)(2,1)S(1)}, bf16[3,48,384]{2,1,0:T(8,128)(2,1)S(1)}, u32[]{:S(2)}, u32[]{:S(2)}) %collective-permute-start.38) | collective-permute-done | bytes 110624 | tf_op jit(solution)/shard_map/ppermute | solution.py:25
  37.3 2.0 collective-permute-start.44
  41.3 3.7 %collective-permute-done.50.refs_27_ = bf16[6,48,384]{2,1,0:T(8,128)(2,1)S(1)} collective-permute-done((bf16[6,48,384]{2,1,0:T(8,128)(2,1)S(1)}, bf16[6,48,384]{2,1,0:T(8,128)(2,1)S(1)}, u32[]{:S(2)}, u32[]{:S(2)}) %collective-permute-start.50) | collective-permute-done | bytes 221216 | tf_op jit(solution)/shard_map/ppermute | solution.py:31
  51.0 2.0 collective-permute-start.48
  53.2 7.8 %collective-permute-done.48.refs_25_ = bf16[3,48,384]{2,1,0:T(8,128)(2,1)S(1)} collective-permute-done((bf16[3,48,384]{2,1,0:T(8,128)(2,1)S(1)}, bf16[3,48,384]{2,1,0:T(8,128)(2,1)S(1)}, u32[]{:S(2)}, u32[]{:S(2)}) %collective-permute-start.48) | collective-permute-done | bytes 110624 | tf_op jit(solution)/shard_map/ppermute | solution.py:25
  67.0 1.6 collective-permute-start.14
  71.7 4.5 %collective-permute-done.12.refs_17_ = bf16[9,48,384]{2,1,0:T(8,128)(2,1)} collective-permute-done((bf16[9,48,384]{2,1,0:T(8,128)(2,1)S(1)}, bf16[9,48,384]{2,1,0:T(8,128)(2,1)}, u32[]{:S(2)}, u32[]{:S(2)}) %collective-permute-start.12) | collective-permute-done | bytes 331808 | tf_op jit(solution)/shard_map/ppermute | solution.py:25
  77.3 1.6 collective-permute-start.24
  83.2 5.0 %collective-permute-done.56.refs_33_ = bf16[3,48,384]{2,1,0:T(8,128)(2,1)} collective-permute-done((bf16[3,48,384]{2,1,0:T(8,128)(2,1)S(1)}, bf16[3,48,384]{2,1,0:T(8,128)(2,1)}, u32[]{:S(2)}, u32[]{:S(2)}) %collective-permute-start.56) | collective-permute-done | bytes 110624 | tf_op jit(solution)/shard_map/ppermute | solution.py:25
  94.6 15.3 %all-gather = f32[73728]{0:T(1024)} all-gather(f32[18432]{0:T(1024)S(1)} %pad.16), channel_id=2, replica_groups=mesh['seq'=8,'chan'=4] {'chan'}, dimensions={0}, use_global_device_ids=true | all-gather | bytes 368640 | tf_op jit(solution)/shard_map/all_gather | solution.py:248
  109.9 1.8 reshape.95
  114.3 10.9 %all_gather.11 = bf16[4096,16]{1,0:T(8,128)(2,1)S(1)} all-gather(bf16[512,16]{1,0:T(8,128)(2,1)} %convert_element_type.28), channel_id=1, replica_groups=mesh['seq'=8,'chan'=4] {'seq'}, dimensions={0}, use_global_device_ids=true | all-gather | bytes 147456 | tf_op jit(solution)/shard_map/all_gather | solution.py:258
  128.5 1.7 slice.141
  130.1 1.6 slice.140
  136.4 4.7 %pad_dynamic-slice_fusion.8 = (bf16[16,80,16]{2,1,0:T(8,128)(2,1)}, bf16[16,80,16]{2,1,0:T(8,128)(2,1)}, bf16[16,80,16]{2,1,0:T(8,128)(2,1)}, bf16[16,80,16]{2,1...) fusion(s32[]{:T(128)S(6)} %add.49, s32[]{:T(128)S(6)} %add.43, ...), kind=kLoop, calls=%fused_computation.8 | loop fusion | bytes 499736 | tf_op jit(solution)/shard_map/slice | solution.py:265
  141.8 1.6 convert_element_type.29
  143.4 1.6 copy.30
  145.0 1.6 convert_element_type.31
  147.3 4.2 %concatenate.10 = bf16[16,80,144]{2,1,0:T(8,128)(2,1)} concatenate(bf16[16,80,16]{2,1,0:T(8,128)(2,1)} %get-tuple-element.6, bf16[16,80,16]{2,1,0:T(8,128)(2,1)} %get-tuple-element.7, bf16[16,80,16]{2,1,0:T(8,128)(2,1)} %get-tuple-element.11, bf16[16,80,16]{2,1,0:T(8,128)(2,1)} %get-tuple-element.8, bf16[16,80,16]{2,1,0:T(8,128)(2,1)} %get-tuple-element.9, ...), dimensions={2} | concatenate | bytes 737280 | tf_op jit(solution)/shard_map/concatenate | solution.py:264
  152.1 2.5 %fusion.refs_0_ = bf16[1280,384]{1,0:T(8,128)(2,1)} fusion(bf16[1280,144]{1,0:T(8,128)(2,1)} %bitcast.30, bf16[144,384]{1,0:T(8,128)(2,1)} %convert_element_type.31, f32[384]{0:T(512)S(1)} %add.36), kind=kOutput, calls=%fused_computation.10 | convolution fusion | flops 142540800 | bytes 1463808 | tf_op jit(solution)/shard_map/dot_general | solution.py:267
  167.7 22.5 %shard_map.91.refs_0_ = bf16[640,384]{1,0:T(8,128)(2,1)} custom-call(bf16[1280,384]{1,0:T(8,128)(2,1)} %fusion.refs_0_, f32[6,384]{1,0:T(8,128)S(1)} %reshape.81.refs_1_, f32[6,384]{1,0:T(8,128)S(1)} %reshape.83.refs_2_, f32[6,384]{1,0:T(8,128)S(1)} %reshape.85.refs_3_, bf16[54,96,384]{2,1,0:T(8,128)(2,1)} %bitcast.22, bf16[9,48,384]{2,1,0:T(8,128)(2,1)S(1)} %copy-done.25, ...), custom_call_target="tpu_custom_call" | custom-call | flops 7644119040 | bytes 16777216 | tf_op jit(solution)/shard_map/pallas_call | solution.py:210
  190.3 8.6 %shard_map.92 = bf16[4,4,48,128]{3,2,1,0:T(8,128)(2,1)S(1)} custom-call(bf16[640,384]{1,0:T(8,128)(2,1)} %shard_map.91.refs_0_, f32[6,384]{1,0:T(8,128)S(1)} %reshape.81.refs_1_, f32[6,384]{1,0:T(8,128)S(1)} %reshape.83.refs_2_, f32[6,384]{1,0:T(8,128)S(1)} %reshape.85.refs_3_, f32[1,192]{1,0:T(1,128)S(1)} %reshape.87.refs_4_, ...), custom_call_target="tpu_custom_call" | custom-call | flops 1274019840 | bytes 16777216 | tf_op jit(solution)/shard_map/pallas_call | solution.py:210
  198.9 13.0 %all_to_all.5 = bf16[4,4,48,128]{3,2,1,0:T(8,128)(2,1)S(1)} all-to-all(bf16[4,4,48,128]{3,2,1,0:T(8,128)(2,1)S(1)} %shard_map.92), channel_id=1, replica_groups=mesh['seq'=8,'chan'=4] {'chan'}, dimensions={0} | all-to-all | bytes 393216 | tf_op jit(solution)/shard_map/all_to_all | solution.py:301
  (244 shorter events, 62.4 us)
Async XLA Ops:
  2.6 11.4 %collective-permute-start.30 = (bf16[6,48,384]{2,1,0:T(8,128)(2,1)S(1)}, bf16[6,48,384]{2,1,0:T(8,128)(2,1)S(1)}, u32[]{:S(2)}, u32[]{:S(2)}) collective-permute-start(bf16[6,48,384]{2,1,0:T(8,128)(2,1)S(1)} %fusion.3), channel_id=1, source_target_pairs={{0,1},{1,2},{2,3},{3,0},{4,5},{5,6},{6,7},{7,4},{8,9},{9,10},{10,1... | collective-permute-start | bytes 663560 | tf_op jit(solution)/shard_map/ppermute | solution.py:31
  5.7 15.3 %collective-permute-start = (bf16[9,48,384]{2,1,0:T(8,128)(2,1)S(1)}, bf16[9,48,384]{2,1,0:T(8,128)(2,1)S(1)}, u32[]{:S(2)}, u32[]{:S(2)}) collective-permute-start(bf16[9,48,384]{2,1,0:T(8,128)(2,1)S(1)} %constant_dynamic-slice_fusion), channel_id=1, source_target_pairs={{0,1},{1,2},{2,3},{3,0},{4,5},{5,6},{6,7},{7,4},{8,9},{9,10},{10,1... | collective-permute-start | bytes 995336 | tf_op jit(solution)/shard_map/ppermute | solution.py:31
  15.7 10.2 %collective-permute-start.40 = (bf16[6,48,384]{2,1,0:T(8,128)(2,1)S(1)}, bf16[6,48,384]{2,1,0:T(8,128)(2,1)S(1)}, u32[]{:S(2)}, u32[]{:S(2)}) collective-permute-start(bf16[6,48,384]{2,1,0:T(8,128)(2,1)S(1)} %collective-permute-done.30.refs_7_), channel_id=1, source_target_pairs={{0,1},{1,2},{2,3},{3,0},{4,5},{5,6},{6,7},{7,4},{8,9},{9,10},{10,1... | collective-permute-start | bytes 663560 | tf_op jit(solution)/shard_map/ppermute | solution.py:31
  15.7 11.8 %collective-permute-start.32 = (bf16[6,48,384]{2,1,0:T(8,128)(2,1)S(1)}, bf16[6,48,384]{2,1,0:T(8,128)(2,1)S(1)}, u32[]{:S(2)}, u32[]{:S(2)}) collective-permute-start(bf16[6,48,384]{2,1,0:T(8,128)(2,1)S(1)} %collective-permute-done.30.refs_7_), channel_id=1, source_target_pairs={{0,8},{1,9},{2,10},{3,11},{4,12},{5,13},{6,14},{7,15},{8,0},{9,1},... | collective-permute-start | bytes 663560 | tf_op jit(solution)/shard_map/ppermute | solution.py:25
  17.2 11.9 %collective-permute-start.31 = (bf16[6,48,384]{2,1,0:T(8,128)(2,1)S(1)}, bf16[6,48,384]{2,1,0:T(8,128)(2,1)S(1)}, u32[]{:S(2)}, u32[]{:S(2)}) collective-permute-start(bf16[6,48,384]{2,1,0:T(8,128)(2,1)S(1)} %collective-permute-done.30.refs_7_), channel_id=1, source_target_pairs={{0,4},{1,5},{2,6},{3,7},{4,0},{5,1},{6,2},{7,3},{8,12},{9,13},{10,... | collective-permute-start | bytes 663560 | tf_op jit(solution)/shard_map/ppermute | solution.py:25
  21.0 16.2 %collective-permute-start.10 = (bf16[9,48,384]{2,1,0:T(8,128)(2,1)S(1)}, bf16[9,48,384]{2,1,0:T(8,128)(2,1)S(1)}, u32[]{:S(2)}, u32[]{:S(2)}) collective-permute-start(bf16[9,48,384]{2,1,0:T(8,128)(2,1)S(1)} %collective-permute-done.refs_5_), channel_id=1, source_target_pairs={{0,1},{1,2},{2,3},{3,0},{4,5},{5,6},{6,7},{7,4},{8,9},{9,10},{10,1... | collective-permute-start | bytes 995336 | tf_op jit(solution)/shard_map/ppermute | solution.py:31
  21.1 18.2 %collective-permute-start.2 = (bf16[9,48,384]{2,1,0:T(8,128)(2,1)S(1)}, bf16[9,48,384]{2,1,0:T(8,128)(2,1)S(1)}, u32[]{:S(2)}, u32[]{:S(2)}) collective-permute-start(bf16[9,48,384]{2,1,0:T(8,128)(2,1)S(1)} %collective-permute-done.refs_5_), channel_id=1, source_target_pairs={{0,8},{1,9},{2,10},{3,11},{4,12},{5,13},{6,14},{7,15},{8,0},{9,1},... | collective-permute-start | bytes 995336 | tf_op jit(solution)/shard_map/ppermute | solution.py:25
  27.5 12.5 %collective-permute-start.4 = (bf16[9,48,384]{2,1,0:T(8,128)(2,1)S(1)}, bf16[9,48,384]{2,1,0:T(8,128)(2,1)S(1)}, u32[]{:S(2)}, u32[]{:S(2)}) collective-permute-start(bf16[9,48,384]{2,1,0:T(8,128)(2,1)S(1)} %collective-permute-done.refs_5_), channel_id=1, source_target_pairs={{0,16},{1,17},{2,18},{3,19},{4,20},{5,21},{6,22},{7,23},{8,24},{9,... | collective-permute-start | bytes 995336 | tf_op jit(solution)/shard_map/ppermute | solution.py:25
  29.0 11.0 %collective-permute-start.1 = (bf16[9,48,384]{2,1,0:T(8,128)(2,1)S(1)}, bf16[9,48,384]{2,1,0:T(8,128)(2,1)S(1)}, u32[]{:S(2)}, u32[]{:S(2)}) collective-permute-start(bf16[9,48,384]{2,1,0:T(8,128)(2,1)S(1)} %collective-permute-done.refs_5_), channel_id=1, source_target_pairs={{0,4},{1,5},{2,6},{3,7},{4,0},{5,1},{6,2},{7,3},{8,12},{9,13},{10,... | collective-permute-start | bytes 995336 | tf_op jit(solution)/shard_map/ppermute | solution.py:25
  47.4 14.8 %collective-permute-start.54 = (bf16[6,48,384]{2,1,0:T(8,128)(2,1)S(1)}, bf16[6,48,384]{2,1,0:T(8,128)(2,1)S(1)}, u32[]{:S(2)}, u32[]{:S(2)}) collective-permute-start(bf16[6,48,384]{2,1,0:T(8,128)(2,1)S(1)} %collective-permute-done.50.refs_27_), channel_id=1, source_target_pairs={{0,16},{1,17},{2,18},{3,19},{4,20},{5,21},{6,22},{7,23},{8,24},{9,... | collective-permute-start | bytes 663560 | tf_op jit(solution)/shard_map/ppermute | solution.py:25
  48.8 12.8 %collective-permute-start.8 = (bf16[5,48,384]{2,1,0:T(8,128)(2,1)S(1)}, bf16[5,48,384]{2,1,0:T(8,128)(2,1)}, u32[]{:S(2)}, u32[]{:S(2)}) collective-permute-start(bf16[5,48,384]{2,1,0:T(8,128)(2,1)S(1)} %slice.137), channel_id=1, source_target_pairs={{0,16},{1,17},{2,18},{3,19},{4,20},{5,21},{6,22},{7,23},{8,24},{9,... | collective-permute-start | bytes 552968 | tf_op jit(solution)/shard_map/ppermute | solution.py:25
  49.6 12.0 %collective-permute-start.6 = (bf16[4,48,384]{2,1,0:T(8,128)(2,1)S(1)}, bf16[4,48,384]{2,1,0:T(8,128)(2,1)S(1)}, u32[]{:S(2)}, u32[]{:S(2)}) collective-permute-start(bf16[4,48,384]{2,1,0:T(8,128)(2,1)S(1)} %slice.136), channel_id=1, source_target_pairs={{0,8},{1,9},{2,10},{3,11},{4,12},{5,13},{6,14},{7,15},{8,0},{9,1},... | collective-permute-start | bytes 442376 | tf_op jit(solution)/shard_map/ppermute | solution.py:25
  61.0 10.7 %collective-permute-start.20 = (bf16[9,48,384]{2,1,0:T(8,128)(2,1)S(1)}, bf16[9,48,384]{2,1,0:T(8,128)(2,1)}, u32[]{:S(2)}, u32[]{:S(2)}) collective-permute-start(bf16[9,48,384]{2,1,0:T(8,128)(2,1)S(1)} %collective-permute-done.10.refs_15_), channel_id=1, source_target_pairs={{0,1},{1,2},{2,3},{3,0},{4,5},{5,6},{6,7},{7,4},{8,9},{9,10},{10,1... | collective-permute-start | bytes 995336 | tf_op jit(solution)/shard_map/ppermute | solution.py:31
  66.0 10.2 %collective-permute-start.12 = (bf16[9,48,384]{2,1,0:T(8,128)(2,1)S(1)}, bf16[9,48,384]{2,1,0:T(8,128)(2,1)}, u32[]{:S(2)}, u32[]{:S(2)}) collective-permute-start(bf16[9,48,384]{2,1,0:T(8,128)(2,1)S(1)} %collective-permute-done.10.refs_15_), channel_id=1, source_target_pairs={{0,8},{1,9},{2,10},{3,11},{4,12},{5,13},{6,14},{7,15},{8,0},{9,1},... | collective-permute-start | bytes 995336 | tf_op jit(solution)/shard_map/ppermute | solution.py:25
  67.0 10.2 %collective-permute-start.14 = (bf16[9,48,384]{2,1,0:T(8,128)(2,1)S(1)}, bf16[9,48,384]{2,1,0:T(8,128)(2,1)S(1)}, u32[]{:S(2)}, u32[]{:S(2)}) collective-permute-start(bf16[9,48,384]{2,1,0:T(8,128)(2,1)S(1)} %collective-permute-done.10.refs_15_), channel_id=1, source_target_pairs={{0,16},{1,17},{2,18},{3,19},{4,20},{5,21},{6,22},{7,23},{8,24},{9,... | collective-permute-start | bytes 995336 | tf_op jit(solution)/shard_map/ppermute | solution.py:25
  76.2 50.9 %collective-permute-start.22 = (bf16[9,48,384]{2,1,0:T(8,128)(2,1)}, bf16[9,48,384]{2,1,0:T(8,128)(2,1)}, u32[]{:S(2)}, u32[]{:S(2)}) collective-permute-start(bf16[9,48,384]{2,1,0:T(8,128)(2,1)} %collective-permute-done.20.refs_25_), channel_id=1, source_target_pairs={{0,8},{1,9},{2,10},{3,11},{4,12},{5,13},{6,14},{7,15},{8,0},{9,1},... | collective-permute-start | bytes 995336 | tf_op jit(solution)/shard_map/ppermute | solution.py:25
  77.3 49.9 %collective-permute-start.24 = (bf16[9,48,384]{2,1,0:T(8,128)(2,1)}, bf16[9,48,384]{2,1,0:T(8,128)(2,1)}, u32[]{:S(2)}, u32[]{:S(2)}) collective-permute-start(bf16[9,48,384]{2,1,0:T(8,128)(2,1)} %collective-permute-done.20.refs_25_), channel_id=1, source_target_pairs={{0,16},{1,17},{2,18},{3,19},{4,20},{5,21},{6,22},{7,23},{8,24},{9,... | collective-permute-start | bytes 995336 | tf_op jit(solution)/shard_map/ppermute | solution.py:25
  79.6 14.5 %collective-permute-start.9 = (bf16[5,48,384]{2,1,0:T(8,128)(2,1)}, bf16[5,48,384]{2,1,0:T(8,128)(2,1)}, u32[]{:S(2)}, u32[]{:S(2)}) collective-permute-start(bf16[5,48,384]{2,1,0:T(8,128)(2,1)} %collective-permute-done.8.refs_13_), channel_id=1, source_target_pairs={{0,4},{1,5},{2,6},{3,7},{4,0},{5,1},{6,2},{7,3},{8,12},{9,13},{10,... | collective-permute-start | bytes 552968 | tf_op jit(solution)/shard_map/ppermute | solution.py:25
  81.5 12.5 %collective-permute-start.58 = (bf16[3,48,384]{2,1,0:T(8,128)(2,1)}, bf16[3,48,384]{2,1,0:T(8,128)(2,1)}, u32[]{:S(2)}, u32[]{:S(2)}) collective-permute-start(bf16[3,48,384]{2,1,0:T(8,128)(2,1)} %slice.148), channel_id=1, source_target_pairs={{0,16},{1,17},{2,18},{3,19},{4,20},{5,21},{6,22},{7,23},{8,24},{9,... | collective-permute-start | bytes 331784 | tf_op jit(solution)/shard_map/ppermute | solution.py:25
  88.2 37.8 %collective-permute-start.16 = (bf16[4,48,384]{2,1,0:T(8,128)(2,1)}, bf16[4,48,384]{2,1,0:T(8,128)(2,1)}, u32[]{:S(2)}, u32[]{:S(2)}) collective-permute-start(bf16[4,48,384]{2,1,0:T(8,128)(2,1)} %slice.138), channel_id=1, source_target_pairs={{0,8},{1,9},{2,10},{3,11},{4,12},{5,13},{6,14},{7,15},{8,0},{9,1},... | collective-permute-start | bytes 442376 | tf_op jit(solution)/shard_map/ppermute | solution.py:25
  94.0 41.9 %collective-permute-start.15 = (bf16[9,48,384]{2,1,0:T(8,128)(2,1)}, bf16[9,48,384]{2,1,0:T(8,128)(2,1)}, u32[]{:S(2)}, u32[]{:S(2)}) collective-permute-start(bf16[9,48,384]{2,1,0:T(8,128)(2,1)} %copy-done.22), channel_id=1, source_target_pairs={{0,4},{1,5},{2,6},{3,7},{4,0},{5,1},{6,2},{7,3},{8,12},{9,13},{10,... | collective-permute-start | bytes 995336 | tf_op jit(solution)/shard_map/ppermute | solution.py:25
  94.1 41.8 %collective-permute-start.13 = (bf16[9,48,384]{2,1,0:T(8,128)(2,1)}, bf16[9,48,384]{2,1,0:T(8,128)(2,1)}, u32[]{:S(2)}, u32[]{:S(2)}) collective-permute-start(bf16[9,48,384]{2,1,0:T(8,128)(2,1)} %collective-permute-done.12.refs_17_), channel_id=1, source_target_pairs={{0,4},{1,5},{2,6},{3,7},{4,0},{5,1},{6,2},{7,3},{8,12},{9,13},{10,... | collective-permute-start | bytes 995336 | tf_op jit(solution)/shard_map/ppermute | solution.py:25
  127.1 24.4 %collective-permute-start.21 = (bf16[9,48,384]{2,1,0:T(8,128)(2,1)}, bf16[9,48,384]{2,1,0:T(8,128)(2,1)}, u32[]{:S(2)}, u32[]{:S(2)}) collective-permute-start(bf16[9,48,384]{2,1,0:T(8,128)(2,1)} %collective-permute-done.20.refs_25_), channel_id=1, source_target_pairs={{0,4},{1,5},{2,6},{3,7},{4,0},{5,1},{6,2},{7,3},{8,12},{9,13},{10,... | collective-permute-start | bytes 995336 | tf_op jit(solution)/shard_map/ppermute | solution.py:25
  133.2 18.9 %collective-permute-start.28 = (bf16[5,48,384]{2,1,0:T(8,128)(2,1)}, bf16[5,48,384]{2,1,0:T(8,128)(2,1)}, u32[]{:S(2)}, u32[]{:S(2)}) collective-permute-start(bf16[5,48,384]{2,1,0:T(8,128)(2,1)} %slice.141), channel_id=1, source_target_pairs={{0,16},{1,17},{2,18},{3,19},{4,20},{5,21},{6,22},{7,23},{8,24},{9,... | collective-permute-start | bytes 552968 | tf_op jit(solution)/shard_map/ppermute | solution.py:25
  134.7 16.9 %collective-permute-start.26 = (bf16[4,48,384]{2,1,0:T(8,128)(2,1)}, bf16[4,48,384]{2,1,0:T(8,128)(2,1)}, u32[]{:S(2)}, u32[]{:S(2)}) collective-permute-start(bf16[4,48,384]{2,1,0:T(8,128)(2,1)} %slice.140), channel_id=1, source_target_pairs={{0,8},{1,9},{2,10},{3,11},{4,12},{5,13},{6,14},{7,15},{8,0},{9,1},... | collective-permute-start | bytes 442376 | tf_op jit(solution)/shard_map/ppermute | solution.py:25
  135.9 19.3 %collective-permute-start.23 = (bf16[9,48,384]{2,1,0:T(8,128)(2,1)}, bf16[9,48,384]{2,1,0:T(8,128)(2,1)}, u32[]{:S(2)}, u32[]{:S(2)}) collective-permute-start(bf16[9,48,384]{2,1,0:T(8,128)(2,1)} %collective-permute-done.22.refs_27_), channel_id=1, source_target_pairs={{0,4},{1,5},{2,6},{3,7},{4,0},{5,1},{6,2},{7,3},{8,12},{9,13},{10,... | collective-permute-start | bytes 995336 | tf_op jit(solution)/shard_map/ppermute | solution.py:25
  135.9 19.7 %collective-permute-start.25 = (bf16[9,48,384]{2,1,0:T(8,128)(2,1)}, bf16[9,48,384]{2,1,0:T(8,128)(2,1)}, u32[]{:S(2)}, u32[]{:S(2)}) collective-permute-start(bf16[9,48,384]{2,1,0:T(8,128)(2,1)} %collective-permute-done.24.refs_29_), channel_id=1, source_target_pairs={{0,4},{1,5},{2,6},{3,7},{4,0},{5,1},{6,2},{7,3},{8,12},{9,13},{10,... | collective-permute-start | bytes 995336 | tf_op jit(solution)/shard_map/ppermute | solution.py:25
  154.7 35.5 %collective-permute-start.51 = (bf16[6,48,384]{2,1,0:T(8,128)(2,1)S(1)}, bf16[6,48,384]{2,1,0:T(8,128)(2,1)S(1)}, u32[]{:S(2)}, u32[]{:S(2)}) collective-permute-start(bf16[6,48,384]{2,1,0:T(8,128)(2,1)S(1)} %collective-permute-done.50.refs_27_), channel_id=1, source_target_pairs={{0,4},{1,5},{2,6},{3,7},{4,0},{5,1},{6,2},{7,3},{8,12},{9,13},{10,... | collective-permute-start | bytes 663560 | tf_op jit(solution)/shard_map/ppermute | solution.py:25
  155.1 35.1 %collective-permute-start.53 = (bf16[6,48,384]{2,1,0:T(8,128)(2,1)S(1)}, bf16[6,48,384]{2,1,0:T(8,128)(2,1)S(1)}, u32[]{:S(2)}, u32[]{:S(2)}) collective-permute-start(bf16[6,48,384]{2,1,0:T(8,128)(2,1)S(1)} %collective-permute-done.52.refs_29_), channel_id=1, source_target_pairs={{0,4},{1,5},{2,6},{3,7},{4,0},{5,1},{6,2},{7,3},{8,12},{9,13},{10,... | collective-permute-start | bytes 663560 | tf_op jit(solution)/shard_map/ppermute | solution.py:25
  155.2 35.0 %collective-permute-start.55 = (bf16[6,48,384]{2,1,0:T(8,128)(2,1)S(1)}, bf16[6,48,384]{2,1,0:T(8,128)(2,1)S(1)}, u32[]{:S(2)}, u32[]{:S(2)}) collective-permute-start(bf16[6,48,384]{2,1,0:T(8,128)(2,1)S(1)} %collective-permute-done.54.refs_31_), channel_id=1, source_target_pairs={{0,4},{1,5},{2,6},{3,7},{4,0},{5,1},{6,2},{7,3},{8,12},{9,13},{10,... | collective-permute-start | bytes 663560 | tf_op jit(solution)/shard_map/ppermute | solution.py:25
  155.6 34.6 %collective-permute-start.57 = (bf16[3,48,384]{2,1,0:T(8,128)(2,1)}, bf16[3,48,384]{2,1,0:T(8,128)(2,1)S(1)}, u32[]{:S(2)}, u32[]{:S(2)}) collective-permute-start(bf16[3,48,384]{2,1,0:T(8,128)(2,1)} %collective-permute-done.56.refs_33_), channel_id=1, source_target_pairs={{0,4},{1,5},{2,6},{3,7},{4,0},{5,1},{6,2},{7,3},{8,12},{9,13},{10,... | collective-permute-start | bytes 331784 | tf_op jit(solution)/shard_map/ppermute | solution.py:25
  155.7 34.5 %collective-permute-start.59 = (bf16[3,48,384]{2,1,0:T(8,128)(2,1)}, bf16[3,48,384]{2,1,0:T(8,128)(2,1)S(1)}, u32[]{:S(2)}, u32[]{:S(2)}) collective-permute-start(bf16[3,48,384]{2,1,0:T(8,128)(2,1)} %collective-permute-done.58.refs_35_), channel_id=1, source_target_pairs={{0,4},{1,5},{2,6},{3,7},{4,0},{5,1},{6,2},{7,3},{8,12},{9,13},{10,... | collective-permute-start | bytes 331784 | tf_op jit(solution)/shard_map/ppermute | solution.py:25
  (78 other events, 743.8 us)

commit v2 on v1

v2 whole, which is shorter than its diff:
```python
import functools
import jax
import jax.numpy as jnp
from jax import lax
from jax.experimental import pallas as pl
from jax.experimental.pallas import tpu as pltpu
from jax.sharding import PartitionSpec as P

LAT_W = 256
EPS = 1e-06
HALO = 8
VMEM_BYTES = 60 * 1024 * 1024

CORE, NEAR, FAR = 1, 2, 4


def place():
    seq = lax.axis_index("seq")
    return lax.rem(seq, 2), lax.rem(lax.div(seq, 2), 4)


def swap(array, mask, chan_mask=0):
    seqs, chans = lax.axis_size("seq"), lax.axis_size("chan")
    pairs = [(s * chans + c, (s ^ mask) * chans + (c ^ chan_mask)) for s in range(seqs) for c in range(chans)]
    return lax.ppermute(array, ("seq", "chan"), pairs)


def shift(array):
    seqs, chans = lax.axis_size("seq"), lax.axis_size("chan")
    pairs = [(s * chans + c, s * chans + (c + 1) % chans) for s in range(seqs) for c in range(chans)]
    return lax.ppermute(array, ("seq", "chan"), pairs)


def in_order(found):
    chans, chan = lax.axis_size("chan"), lax.axis_index("chan")
    found = jnp.stack(found)
    return jnp.stack(
        [lax.dynamic_index_in_dim(found, lax.rem(chan + chans - c, chans), 0, False) for c in range(chans)]
    )


def gather_frame(held):
    mask = 1
    while mask < lax.axis_size("seq"):
        held = jnp.concatenate([held, swap(held, mask)], 0)
        mask *= 2
    return held


def thirds(values):
    parts = []
    for _ in range(3):
        part = lax.reduce_precision(values, 8, 7)
        parts.append(part.astype(jnp.bfloat16))
        values = values - part
    return parts


def spread(own, small, finish):
    held, small_held, found, metas, pieces = own, small, [small], [], []
    cut, steps = own.shape[0] // 2, lax.axis_size("chan") - 1
    for step in range(1, steps + 1):
        held, small_held = lax.optimization_barrier((shift(held), small_held))
        small_held = shift(small_held)
        found.append(small_held)
        near = swap(held, NEAR)
        far = swap(held, FAR)
        if step < steps:
            cross = [(0, swap(far[:cut], NEAR)), (cut, swap(near[cut:], FAR))]
        else:
            cross = [(0, swap(held, NEAR | FAR))]
            near, beside = lax.optimization_barrier((near, finish(in_order(found))))
        arrays = [(0, 0, held), (NEAR // 2, 0, near), (FAR // 2, 0, far)]
        arrays += [((NEAR | FAR) // 2, first, array) for first, array in cross]
        for chip, first, array in arrays:
            for core in range(2):
                metas.append((chip, core, step, first))
                pieces.append(swap(array, CORE) if core else array)
    return tuple(metas), pieces, beside


def own_slice(units, per_chip):
    core, chip = place()
    rows = units.shape[1] // 2
    return lax.dynamic_slice(units, (chip * per_chip, core * rows, 0), (per_chip, rows, units.shape[2]))


def load_weights(metas, per_chip, chans, own, pieces, weights, sems):
    core, chip = place()
    chan = lax.axis_index("chan")
    depth = own[0][0].shape[1]
    half = depth // 2
    for ref, begin in own:
        at = 0
        while at < ref.shape[0]:
            owner = (begin + at) // per_chip
            count = min(ref.shape[0] - at, (owner + 1) * per_chip - begin - at)
            base = pl.multiple_of(chan * depth, 16)
            dst = weights.at[pl.ds(begin + at, count), pl.ds(base, depth), :]
            pltpu.make_async_copy(ref.at[pl.ds(at, count)], dst, sems.at[owner, 0]).start()
            at += count
    total = sum(ref.shape[0] for ref, _ in own)
    for (chip_mask, core_mask, step, first), ref in zip(metas, pieces):
        shard = lax.rem(chan + chans - step, chans)
        owner = chip ^ chip_mask
        base = pl.multiple_of(shard * depth + (core ^ core_mask) * half, 16)
        dst = weights.at[pl.ds(owner * per_chip + first, ref.shape[0]), pl.ds(base, half), :]
        pltpu.make_async_copy(ref, dst, sems.at[owner, 2 * step - 1 + core_mask]).start()

    def wait(owner):
        begin = owner * per_chip
        mine = weights.at[pl.ds(begin, min(per_chip, total - begin)), pl.ds(0, depth), :]
        pltpu.make_async_copy(mine, mine, sems.at[owner, 0]).wait()
        slice_of = weights.at[pl.ds(begin, per_chip), pl.ds(0, half), :]
        for i in range(1, 2 * chans - 1):
            pltpu.make_async_copy(slice_of, slice_of, sems.at[owner, i]).wait()

    return wait


def inside(rows, width, first_row, first_col, height):
    row = first_row + lax.broadcasted_iota(jnp.int32, (rows, width, 1), 0)
    col = first_col + lax.broadcasted_iota(jnp.int32, (rows, width, 1), 1)
    ok = (row >= 0) & (row < height) & (col >= 0) & (col < LAT_W)
    return jnp.where(ok, 1.0, 0.0).astype(jnp.float32).reshape(rows * width, 1)


def norm_act(values, gain, shift_by, mask):
    mean_sq = jnp.mean(values * values, axis=1, keepdims=True)
    scaled = values * lax.rsqrt(mean_sq + EPS) * gain + shift_by
    return scaled / (1.0 + jnp.exp(-scaled)) * mask


def set_columns(cols, values):
    cells, chans = values.shape
    cols[:cells, :chans] = pltpu.roll(values, 1, 0).astype(jnp.bfloat16)
    cols[:cells, chans : 2 * chans] = values.astype(jnp.bfloat16)
    cols[:cells, 2 * chans :] = pltpu.roll(values, cells - 1, 0).astype(jnp.bfloat16)


def conv(cols, weights, unit, rows, width):
    chans = weights.shape[1]
    total = None
    for row_tap in range(3):
        taps = weights[unit + 3 * row_tap : unit + 3 * row_tap + 3].reshape(3 * chans, chans)
        part = jnp.dot(
            cols[row_tap * width : (row_tap + rows) * width, :], taps, preferred_element_type=jnp.float32
        )
        total = part if total is None else total + part
    return total


def res_block(stream, rows, width, block, params, cols, weights, corner, height, need):
    gain, shift_by, bias = params
    first_row, first_col = corner
    mask = inside(rows, width, first_row, first_col, height)
    set_columns(cols, norm_act(stream, gain[2 * block][None], shift_by[2 * block][None], mask))
    unit = 18 * block
    need(unit + 9)
    middle = conv(cols, weights, unit, rows - 2, width) + bias[2 * block][None]
    mask = inside(rows - 2, width, first_row + 1, first_col, height)
    set_columns(cols, norm_act(middle, gain[2 * block + 1][None], shift_by[2 * block + 1][None], mask))
    need(unit + 18)
    branch = conv(cols, weights, unit + 9, rows - 4, width) + bias[2 * block + 1][None]
    kept = stream[2 * width : (rows - 2) * width]
    return (kept + branch).astype(jnp.bfloat16).astype(jnp.float32)


def tile_corner(slab_rows, tile_cols, halo):
    return (
        lax.axis_index("seq") * slab_rows - halo,
        lax.axis_index("chan") * tile_cols - HALO,
    )


def enter(frame, in_weight, in_bias, rows, width, slab_rows, height, tile_cols, slab, wide, in_cols, sems):
    lat, tokens = frame.shape[1:]
    blocks = LAT_W // tokens
    first_row, first_col = tile_corner(slab_rows, tile_cols, HALO)
    fetches = []
    for row in range(rows + 2):
        held = (first_row + row >= 0) & (first_row + row < height)
        at = jnp.clip(first_row + row, 0, height - 1)
        owner = lax.div(at, slab_rows) ^ lax.axis_index("seq")
        start = (owner * slab_rows + lax.rem(at, slab_rows)) * blocks
        fetch = pltpu.make_async_copy(frame.at[pl.ds(start, blocks)], slab.at[row], sems.at[row])
        fetches.append((held, fetch))

    def start_all():
        for held, fetch in fetches:
            pl.when(held)(fetch.start)

    def finish():
        for held, fetch in fetches:
            pl.when(held)(fetch.wait)
        for row in range(rows + 2):
            for block in range(blocks):
                wide[row, 2 * HALO + block * tokens : 2 * HALO + (block + 1) * tokens, :] = slab[row, block].astype(jnp.float32).T
        left = pl.multiple_of(lax.axis_index("chan") * tile_cols + HALO, 8)
        region = wide[:, pl.ds(left, width), :].reshape((rows + 2) * width, lat)
        mask = inside(rows + 2, width, first_row, first_col, height)
        set_columns(in_cols, jnp.where(mask > 0.0, region, 0.0))
        total = in_bias[...]
        for row_tap in range(3):
            part = in_cols[row_tap * width : (row_tap + rows) * width, :]
            total = total + jnp.dot(part, in_weight[row_tap], preferred_element_type=jnp.float32)
        return total.astype(jnp.bfloat16).astype(jnp.float32)

    return start_all, finish


def tile_kernel(static, *refs):
    chans, layers, rows, width, slab_rows, height, metas, per_chip = static
    gain, shift_by, bias, in_w, in_b, up_bias, frame, res_ref, up_ref = refs[:9]
    pieces = refs[9 : 9 + len(metas)]
    out_ref, weights, cols, slab, wide, in_cols, woven, slab_sems, sems = refs[9 + len(metas) :]
    tile_cols = LAT_W // chans
    start_all, finish = enter(
        frame, in_w, in_b, rows, width, slab_rows, height, tile_cols, slab, wide, in_cols, slab_sems
    )
    start_all()
    n_res = res_ref.shape[0]
    wait = load_weights(metas, per_chip, chans, ((res_ref, 0), (up_ref, n_res)), pieces, weights, sems)
    waited = [0]

    def need(units):
        while waited[0] * per_chip < units:
            wait(waited[0])
            waited[0] += 1

    halo = (rows - slab_rows) // 2
    stream = finish()
    for layer in range(layers):
        stream = res_block(
            stream, rows, width, layer, (gain, shift_by, bias), cols, weights,
            tile_corner(slab_rows, tile_cols, halo), height, need,
        )
        rows, halo = rows - 4, halo - 2
    need(n_res + up_ref.shape[0])
    first_row, first_col = tile_corner(slab_rows, tile_cols, halo)
    framed = (stream * inside(rows, width, first_row, first_col, height)).astype(jnp.bfloat16)
    outs = up_bias.shape[1]
    products = []
    for pair in range(up_ref.shape[0]):
        both = jnp.dot(framed, weights[n_res + pair], preferred_element_type=jnp.float32)
        products += [both[:, :outs], both[:, outs:]]
    cells = rows * width
    even, odd = [], []
    for row_tap in range(3):
        left, mid, right = products[3 * row_tap : 3 * row_tap + 3]
        even.append(pltpu.roll(left, 1, 0) + mid + right)
        odd.append(left + mid + pltpu.roll(right, cells - 1, 0))
    share = outs // chans
    for row in range(slab_rows):
        for low in range(2):
            for parity, parts in ((0, even), (1, odd)):
                total = up_bias[...]
                for row_tap in range(3):
                    at = (row + 1 + (low + row_tap - 1) // 2) * width + HALO
                    total = total + parts[row_tap][at : at + tile_cols]
                for tile in range(woven.shape[0]):
                    lanes = total[:, 128 * tile : 128 * tile + 128]
                    if lanes.shape[1] < 128:
                        blank = jnp.zeros((tile_cols, 128 - lanes.shape[1]), jnp.float32)
                        lanes = jnp.concatenate([lanes, blank], 1)
                    woven[tile, pl.ds(parity, tile_cols, 2), :] = lanes
            turned = jnp.concatenate([woven[tile].T for tile in range(woven.shape[0])], 0)
            for owner in range(chans):
                out_ref[owner, 2 * row + low] = turned[owner * share : (owner + 1) * share].astype(jnp.bfloat16)


def body(
    latent, in_weight, in_bias, norm_gain, norm_shift, res_weight, res_bias, up_weight, up_bias
):
    seqs, chans = lax.axis_size("seq"), lax.axis_size("chan")
    layers, _, taps, depth, ch = res_weight.shape
    outs = up_weight.shape[2]
    tokens, lat = latent.shape
    slab_rows = tokens * chans // LAT_W
    height = slab_rows * seqs
    tile_cols = LAT_W // chans
    width = -(-(tile_cols + 2 * HALO) // 16) * 16

    norms = [a.reshape(2 * layers, depth) for a in (norm_gain, norm_shift, res_bias)]
    ends = jnp.zeros((2 * layers, depth), jnp.float32)
    ends = ends.at[0].set(in_bias).at[1, : outs // chans].set(up_bias)
    smalls = [*thirds(jnp.concatenate(norms + [ends], 1)), in_weight.reshape(-1, ch)]
    smalls = jnp.concatenate(smalls, 0)
    n_small = smalls.shape[0]
    smalls = [smalls[:, at : at + tokens] for at in range(0, ch, tokens)]
    smalls = jnp.concatenate([*smalls, gather_frame(latent.T[None]).reshape(-1, tokens)], 0)

    def small_args(packed):
        n_lanes = ch // tokens
        frame = packed[:, n_small * n_lanes :].reshape(chans, seqs, lat, tokens).transpose(1, 0, 2, 3)
        frame = frame.reshape(seqs * chans, lat, tokens)
        packed = jnp.concatenate([packed[:, n_small * i : n_small * (i + 1)] for i in range(n_lanes)], 2)
        params = sum(packed[:, 2 * layers * i : 2 * layers * (i + 1)].astype(jnp.float32) for i in range(3))
        params = params.reshape(chans, 2 * layers, 4, depth).transpose(2, 1, 0, 3)
        gain, shift_by, bias = (params[i].reshape(2 * layers, ch) for i in range(3))
        in_b = params[3, 0].reshape(1, ch)
        up_b = params[3, 1, :, : outs // chans].reshape(1, outs)
        in_w = packed[:, 6 * layers :].reshape(chans, 3, taps // 3, lat // chans, ch)
        in_w = in_w.transpose(1, 2, 0, 3, 4).reshape(3, taps // 3 * lat, ch)
        return gain, shift_by, bias, in_w, in_b, up_b, frame

    res_units = res_weight.reshape(layers * 2 * taps, depth, ch)
    up_units = jnp.pad(up_weight, ((0, 1), (0, 0), (0, 0))).reshape(-1, 2, depth, outs)
    up_units = up_units.transpose(0, 2, 1, 3).reshape(-1, depth, 2 * outs)
    units = jnp.concatenate([res_units, up_units], 0)
    per_chip = -(-units.shape[0] // 4)
    units = jnp.pad(units, ((0, 4 * per_chip - units.shape[0]), (0, 0), (0, 0)))
    metas, pieces, small = spread(own_slice(units, per_chip), smalls, small_args)

    rows = slab_rows + 2 * (HALO - 1)
    in_vmem = small[:-1]
    in_any = [small[-1], res_units, up_units, *pieces]
    vmem = pl.BlockSpec(memory_space=pltpu.VMEM)
    cells = sum(rows - 2 * i for i in range(1, 2 * layers + 1)) * width
    shares = pl.pallas_call(
        functools.partial(
            tile_kernel, (chans, layers, rows, width, slab_rows, height, metas, per_chip)
        ),
        out_shape=jax.ShapeDtypeStruct((chans, 2 * slab_rows, outs // chans, 2 * tile_cols), jnp.bfloat16),
        in_specs=[vmem] * len(in_vmem) + [pl.BlockSpec(memory_space=pl.ANY)] * len(in_any),
        out_specs=vmem,
        scratch_shapes=[
            pltpu.VMEM((4 * per_chip, ch, ch), jnp.bfloat16),
            pltpu.VMEM((rows * width, 3 * ch), jnp.bfloat16),
            pltpu.VMEM((rows + 2, LAT_W // tokens, lat, tokens), jnp.bfloat16),
            pltpu.VMEM((rows + 2, LAT_W + 4 * HALO, lat), jnp.float32),
            pltpu.VMEM(((rows + 2) * width, 3 * lat), jnp.bfloat16),
            pltpu.VMEM((-(-outs // 128), 2 * tile_cols, 128), jnp.float32),
            pltpu.SemaphoreType.DMA((rows + 2,)),
            pltpu.SemaphoreType.DMA((4, 2 * chans - 1)),
        ],
        compiler_params=pltpu.CompilerParams(vmem_limit_bytes=VMEM_BYTES),
        cost_estimate=pl.CostEstimate(
            flops=2 * taps * ch * ch * cells, bytes_accessed=4 * per_chip * ch * ch * 2, transcendentals=0
        ),
    )(*in_vmem, *in_any)
    turned = lax.all_to_all(shares, "chan", 0, 0, tiled=True)
    return turned.transpose(2, 1, 0, 3).reshape(outs // chans, 2 * slab_rows, 2 * LAT_W)


def solution(mesh):
    placed = (
        P(("seq", "chan"), None),
        P(None, "chan", None),
        P("chan"),
        P(None, None, "chan"),
        P(None, None, "chan"),
        P(None, None, None, "chan", None),
        P(None, None, "chan"),
        P(None, "chan", None),
        P("chan"),
    )
    return jax.shard_map(
        body, mesh=mesh, in_specs=placed, out_specs=P("chan", "seq", None), check_vma=False
    )
```

time: 214 us -> 156 us (0.73)
  local copies, waits for them, and re-layouts: 52.7 us -> 11.1 us
  waiting for transfers between devices: 44.4 us -> 76.4 us
  blocking collectives: 39.2 us -> 11.4 us
  starting transfers between devices: 41.2 us -> 21.3 us
  matrix products: 2.54 us -> 0 us
  Pallas kernels: 31 us -> 33.5 us
    all_gather x2 -> x0, blocking collectives: 26.2 us -> none  [the longest x1 15.3 us: body(): packed = lax.all_gather(flat, 'chan')]
    ppermute x6, waiting for transfers between devices: 17.5 us -> 39.8 us  [shift(): return lax.ppermute(array, ('seq', 'chan'), pairs)]
    ppermute x54 -> x28, starting transfers between devices: 35.8 us -> 17.3 us  [swap(): return lax.ppermute(array, ('seq', 'chan'), pairs)]
    unnamed x94 -> x48, local copies, waits for them, and re-layouts: 20.5 us -> 2.95 us
    slice x23 -> x9, local copies, waits for them, and re-layouts: 12.6 us -> 0.33 us  [the longest x1 0.12 us: small_args(): gain, shift_by, bias = (params[i].reshape(2 * layers, ch) for i in range(3))]
    ppermute x54 -> x28, waiting for transfers between devices: 26.9 us -> 36.6 us  [swap(): return lax.ppermute(array, ('seq', 'chan'), pairs)]
    convert_element_type x4 -> x0, local copies, waits for them, and re-layouts: 5.51 us -> none  [the longest x3 4.72 us: body(): found[0].transpose(1, 0, 2, 3).reshape(taps * lat_share * chans, ch)]
    concatenate x2 -> x0, local copies, waits for them, and re-layouts: 5.11 us -> none  [the longest x1 4.21 us: body(): jnp.concatenate([region[p:p + rows, r:r + width] for p in range(3) for r...]
  transfers between devices with their start and end apart: 60 -> 34, of which waited for: 12 -> 14; matrix products, arithmetic and copies ran while one was open for 15% -> 6% of each run, Pallas kernels for 11% -> 0%
where the time goes in v2:
time: 156 us
  waiting for transfers between devices  76.4 us (49%)
  Pallas kernels  33.5 us (21%)
  starting transfers between devices  21.3 us (14%)
  blocking collectives  11.4 us (7%)
  local copies, waits for them, and re-layouts  11.1 us (7%)
  other arithmetic  1.81 us (1%)
    ppermute x6, waiting for transfers between devices, shift(): return lax.ppermute(array, ('seq', 'chan'), pairs)  39.8 us
    ppermute x28, waiting for transfers between devices, swap(): return lax.ppermute(array, ('seq', 'chan'), pairs)  36.6 us
    pallas_call x1, Pallas kernels, body(): pl.pallas_call(functools.partial(tile_kernel, (chans, layers, rows, width...  33.5 us
    ppermute x28, starting transfers between devices, swap(): return lax.ppermute(array, ('seq', 'chan'), pairs)  17.3 us
    all_to_all x1, blocking collectives, body(): turned = lax.all_to_all(shares, 'chan', 0, 0, tiled=True)  11.4 us
    ppermute x6, starting transfers between devices, shift(): return lax.ppermute(array, ('seq', 'chan'), pairs)  3.98 us
  transfers between devices with their start and end apart: 34, of which 14 were waited for; matrix products, arithmetic and copies ran while one was open for 6% of the time, Pallas kernels for 0%

profile of v2, /device:TPU:0, one launch (start us, length us, event | category | flops | bytes accessed | tf_op | source)
XLA Modules:
  0.0 155.9 jit_solution(17333825484046664099)
XLA Ops:
  0.5 1.1 pad.14
  2.4 1.5 fusion.2
  4.0 2.6 %collective-permute-start = (bf16[15,48,384]{2,1,0:T(8,128)(2,1)S(1)}, bf16[15,48,384]{2,1,0:T(8,128)(2,1)S(1)}, u32[]{:S(2)}, u32[]{:S(2)}) collective-permute-start(bf16[15,48,384]{2,1,0:T(8,128)(2,1)S(1)} %fusion.2), channel_id=1, source_target_pairs={{0,1},{1,2},{2,3},{3,0},{4,5},{5,6},{6,7},{7,4},{8,9},{9,10},{10,1... | collective-permute-start | bytes 1658888 | tf_op jit(solution)/shard_map/ppermute | solution.py:31
  7.0 1.6 collective-permute-start.2
  8.6 2.1 %collective-permute-done.2 = bf16[2,16,128]{2,1,0:T(8,128)(2,1)S(1)} collective-permute-done((bf16[2,16,128]{2,1,0:T(8,128)(2,1)S(1)}, bf16[2,16,128]{2,1,0:T(8,128)(2,1)S(1)}, u32[]{:S(2)}, u32[]{:S(2)}) %collective-permute-start.2) | collective-permute-done | bytes 8224 | tf_op jit(solution)/shard_map/ppermute | solution.py:25
  10.7 1.5 collective-permute-start.3
  12.3 2.2 %collective-permute-done.3 = bf16[4,16,128]{2,1,0:T(8,128)(2,1)S(1)} collective-permute-done((bf16[4,16,128]{2,1,0:T(8,128)(2,1)S(1)}, bf16[4,16,128]{2,1,0:T(8,128)(2,1)S(1)}, u32[]{:S(2)}, u32[]{:S(2)}) %collective-permute-start.3) | collective-permute-done | bytes 16416 | tf_op jit(solution)/shard_map/ppermute | solution.py:25
  14.5 7.3 %collective-permute-done.refs_9_ = bf16[15,48,384]{2,1,0:T(8,128)(2,1)S(1)} collective-permute-done((bf16[15,48,384]{2,1,0:T(8,128)(2,1)S(1)}, bf16[15,48,384]{2,1,0:T(8,128)(2,1)S(1)}, u32[]{:S(2)}, u32[]{:S(2)}) %collective-permute-start) | collective-permute-done | bytes 552992 | tf_op jit(solution)/shard_map/ppermute | solution.py:31
  21.8 1.5 collective-permute-start.13
  23.3 1.4 collective-permute-start.11
  24.8 1.3 collective-permute-start.5
  26.1 13.6 %collective-permute-done.5 = bf16[290,128]{1,0:T(8,128)(2,1)S(1)} collective-permute-done((bf16[290,128]{1,0:T(8,128)(2,1)S(1)}, bf16[290,128]{1,0:T(8,128)(2,1)S(1)}, u32[]{:S(2)}, u32[]{:S(2)}) %collective-permute-start.5) | collective-permute-done | bytes 74272 | tf_op jit(solution)/shard_map/ppermute | solution.py:31
  39.6 1.4 collective-permute-start.22
  41.1 1.5 collective-permute-start.15
  42.6 0.9 copy-done.13
  44.2 14.8 %collective-permute-done.7 = bf16[290,128]{1,0:T(8,128)(2,1)S(1)} collective-permute-done((bf16[290,128]{1,0:T(8,128)(2,1)S(1)}, bf16[290,128]{1,0:T(8,128)(2,1)S(1)}, u32[]{:S(2)}, u32[]{:S(2)}) %collective-permute-start.7) | collective-permute-done | bytes 74272 | tf_op jit(solution)/shard_map/ppermute | solution.py:31
  59.7 6.1 %collective-permute-done.17.refs_17_ = bf16[8,48,384]{2,1,0:T(8,128)(2,1)S(1)} collective-permute-done((bf16[8,48,384]{2,1,0:T(8,128)(2,1)S(1)}, bf16[8,48,384]{2,1,0:T(8,128)(2,1)S(1)}, u32[]{:S(2)}, u32[]{:S(2)}) %collective-permute-start.17) | collective-permute-done | bytes 294944 | tf_op jit(solution)/shard_map/ppermute | solution.py:25
  66.4 0.7 copy-done.14
  67.2 1.2 collective-permute-done.16.refs_16_
  69.2 4.1 %collective-permute-done.9 = bf16[290,128]{1,0:T(8,128)(2,1)S(1)} collective-permute-done((bf16[290,128]{1,0:T(8,128)(2,1)S(1)}, bf16[290,128]{1,0:T(8,128)(2,1)S(1)}, u32[]{:S(2)}, u32[]{:S(2)}) %collective-permute-start.9) | collective-permute-done | bytes 74272 | tf_op jit(solution)/shard_map/ppermute | solution.py:31
  74.0 0.8 collective-permute-start.26
  75.0 2.2 %collective-permute-start.32 = (bf16[15,48,384]{2,1,0:T(8,128)(2,1)}, bf16[15,48,384]{2,1,0:T(8,128)(2,1)}, u32[]{:S(2)}, u32[]{:S(2)}) collective-permute-start(bf16[15,48,384]{2,1,0:T(8,128)(2,1)} %copy-done.14), channel_id=1, source_target_pairs={{0,24},{1,25},{2,26},{3,27},{4,28},{5,29},{6,30},{7,31},{8,16},{9,... | collective-permute-start | bytes 1658888 | tf_op jit(solution)/shard_map/ppermute | solution.py:25
  78.0 6.0 %collective-permute-done.26.refs_27_ = bf16[8,48,384]{2,1,0:T(8,128)(2,1)S(1)} collective-permute-done((bf16[8,48,384]{2,1,0:T(8,128)(2,1)S(1)}, bf16[8,48,384]{2,1,0:T(8,128)(2,1)S(1)}, u32[]{:S(2)}, u32[]{:S(2)}) %collective-permute-start.26) | collective-permute-done | bytes 294944 | tf_op jit(solution)/shard_map/ppermute | solution.py:25
  84.1 5.5 %collective-permute-done.8.refs_31_ = bf16[15,48,384]{2,1,0:T(8,128)(2,1)} collective-permute-done((bf16[15,48,384]{2,1,0:T(8,128)(2,1)}, bf16[15,48,384]{2,1,0:T(8,128)(2,1)}, u32[]{:S(2)}, u32[]{:S(2)}) %collective-permute-start.8) | collective-permute-done | bytes 552992 | tf_op jit(solution)/shard_map/ppermute | solution.py:25
  91.6 0.7 reshape_squeeze.16.refs_1_
  95.0 6.0 %collective-permute-done.32.refs_35_ = bf16[15,48,384]{2,1,0:T(8,128)(2,1)} collective-permute-done((bf16[15,48,384]{2,1,0:T(8,128)(2,1)}, bf16[15,48,384]{2,1,0:T(8,128)(2,1)}, u32[]{:S(2)}, u32[]{:S(2)}) %collective-permute-start.32) | collective-permute-done | bytes 552992 | tf_op jit(solution)/shard_map/ppermute | solution.py:25
  101.0 4.5 %collective-permute-done.30.refs_33_ = bf16[15,48,384]{2,1,0:T(8,128)(2,1)} collective-permute-done((bf16[15,48,384]{2,1,0:T(8,128)(2,1)}, bf16[15,48,384]{2,1,0:T(8,128)(2,1)}, u32[]{:S(2)}, u32[]{:S(2)}) %collective-permute-start.30) | collective-permute-done | bytes 552992 | tf_op jit(solution)/shard_map/ppermute | solution.py:25
  106.2 2.2 %collective-permute-done.27.refs_28_ = bf16[8,48,384]{2,1,0:T(8,128)(2,1)S(1)} collective-permute-done((bf16[8,48,384]{2,1,0:T(8,128)(2,1)S(1)}, bf16[8,48,384]{2,1,0:T(8,128)(2,1)S(1)}, u32[]{:S(2)}, u32[]{:S(2)}) %collective-permute-start.27) | collective-permute-done | bytes 294944 | tf_op jit(solution)/shard_map/ppermute | solution.py:25
  109.3 0.8 copy-done.19
  110.1 33.5 %shard_map.91 = bf16[4,4,48,128]{3,2,1,0:T(8,128)(2,1)} custom-call(f32[6,384]{1,0:T(8,128)} %reshape_squeeze.15.refs_0_, f32[6,384]{1,0:T(8,128)} %reshape_squeeze.16.refs_1_, f32[6,384]{1,0:T(8,128)} %reshape_squeeze.17.refs_2_, bf16[3,48,384]{2,1,0:T(8,128)(2,1)} %reshape.111.refs_3_, f32[1,384]{1,0:T(1,128)} %reshape_squeeze.18.refs_4_, ...), custom_call_target="tpu_custom_call" | custom-call | flops 11466178560 | bytes 17694720 | tf_op jit(solution)/shard_map/pallas_call | solution.py:320
  143.7 11.4 %all_to_all.5 = bf16[4,4,48,128]{3,2,1,0:T(8,128)(2,1)S(1)} all-to-all(bf16[4,4,48,128]{3,2,1,0:T(8,128)(2,1)} %shard_map.91), channel_id=1, replica_groups=mesh['seq'=8,'chan'=4] {'chan'}, dimensions={0} | all-to-all | bytes 393216 | tf_op jit(solution)/shard_map/all_to_all | solution.py:342
  155.2 0.8 reshape.115
  (128 shorter events, 12.5 us)
Async XLA Ops:
  0.0 7.0 %collective-permute-start.1 = (bf16[1,16,128]{2,1,0:T(8,128)(2,1)}, bf16[1,16,128]{2,1,0:T(8,128)(2,1)S(1)}, u32[]{:S(2)}, u32[]{:S(2)}) collective-permute-start(bf16[1,16,128]{2,1,0:T(8,128)(2,1)} %bitcast.42), channel_id=1, source_target_pairs={{0,4},{1,5},{2,6},{3,7},{4,0},{5,1},{6,2},{7,3},{8,12},{9,13},{10,... | collective-permute-start | bytes 12296 | tf_op jit(solution)/shard_map/ppermute | solution.py:25
  4.0 17.9 %collective-permute-start = (bf16[15,48,384]{2,1,0:T(8,128)(2,1)S(1)}, bf16[15,48,384]{2,1,0:T(8,128)(2,1)S(1)}, u32[]{:S(2)}, u32[]{:S(2)}) collective-permute-start(bf16[15,48,384]{2,1,0:T(8,128)(2,1)S(1)} %fusion.2), channel_id=1, source_target_pairs={{0,1},{1,2},{2,3},{3,0},{4,5},{5,6},{6,7},{7,4},{8,9},{9,10},{10,1... | collective-permute-start | bytes 1658888 | tf_op jit(solution)/shard_map/ppermute | solution.py:31
  7.0 3.7 %collective-permute-start.2 = (bf16[2,16,128]{2,1,0:T(8,128)(2,1)S(1)}, bf16[2,16,128]{2,1,0:T(8,128)(2,1)S(1)}, u32[]{:S(2)}, u32[]{:S(2)}) collective-permute-start(bf16[2,16,128]{2,1,0:T(8,128)(2,1)S(1)} %pad_maximum_fusion.18), channel_id=1, source_target_pairs={{0,8},{1,9},{2,10},{3,11},{4,12},{5,13},{6,14},{7,15},{8,0},{9,1},... | collective-permute-start | bytes 24584 | tf_op jit(solution)/shard_map/ppermute | solution.py:25
  10.7 3.7 %collective-permute-start.3 = (bf16[4,16,128]{2,1,0:T(8,128)(2,1)S(1)}, bf16[4,16,128]{2,1,0:T(8,128)(2,1)S(1)}, u32[]{:S(2)}, u32[]{:S(2)}) collective-permute-start(bf16[4,16,128]{2,1,0:T(8,128)(2,1)S(1)} %pad_maximum_fusion.16), channel_id=1, source_target_pairs={{0,16},{1,17},{2,18},{3,19},{4,20},{5,21},{6,22},{7,23},{8,24},{9,... | collective-permute-start | bytes 49160 | tf_op jit(solution)/shard_map/ppermute | solution.py:25
  21.8 17.8 %collective-permute-start.4 = (bf16[15,48,384]{2,1,0:T(8,128)(2,1)S(1)}, bf16[15,48,384]{2,1,0:T(8,128)(2,1)}, u32[]{:S(2)}, u32[]{:S(2)}) collective-permute-start(bf16[15,48,384]{2,1,0:T(8,128)(2,1)S(1)} %collective-permute-done.refs_9_), channel_id=1, source_target_pairs={{0,1},{1,2},{2,3},{3,0},{4,5},{5,6},{6,7},{7,4},{8,9},{9,10},{10,1... | collective-permute-start | bytes 1658888 | tf_op jit(solution)/shard_map/ppermute | solution.py:31
  21.8 19.2 %collective-permute-start.13 = (bf16[15,48,384]{2,1,0:T(8,128)(2,1)S(1)}, bf16[15,48,384]{2,1,0:T(8,128)(2,1)S(1)}, u32[]{:S(2)}, u32[]{:S(2)}) collective-permute-start(bf16[15,48,384]{2,1,0:T(8,128)(2,1)S(1)} %collective-permute-done.refs_9_), channel_id=1, source_target_pairs={{0,16},{1,17},{2,18},{3,19},{4,20},{5,21},{6,22},{7,23},{8,24},{9,... | collective-permute-start | bytes 1658888 | tf_op jit(solution)/shard_map/ppermute | solution.py:25
  23.3 19.2 %collective-permute-start.11 = (bf16[15,48,384]{2,1,0:T(8,128)(2,1)S(1)}, bf16[15,48,384]{2,1,0:T(8,128)(2,1)S(1)}, u32[]{:S(2)}, u32[]{:S(2)}) collective-permute-start(bf16[15,48,384]{2,1,0:T(8,128)(2,1)S(1)} %collective-permute-done.refs_9_), channel_id=1, source_target_pairs={{0,8},{1,9},{2,10},{3,11},{4,12},{5,13},{6,14},{7,15},{8,0},{9,1},... | collective-permute-start | bytes 1658888 | tf_op jit(solution)/shard_map/ppermute | solution.py:25
  24.8 17.9 %collective-permute-start.10 = (bf16[15,48,384]{2,1,0:T(8,128)(2,1)S(1)}, bf16[15,48,384]{2,1,0:T(8,128)(2,1)S(1)}, u32[]{:S(2)}, u32[]{:S(2)}) collective-permute-start(bf16[15,48,384]{2,1,0:T(8,128)(2,1)S(1)} %collective-permute-done.refs_9_), channel_id=1, source_target_pairs={{0,4},{1,5},{2,6},{3,7},{4,0},{5,1},{6,2},{7,3},{8,12},{9,13},{10,... | collective-permute-start | bytes 1658888 | tf_op jit(solution)/shard_map/ppermute | solution.py:25
  24.8 14.9 %collective-permute-start.5 = (bf16[290,128]{1,0:T(8,128)(2,1)S(1)}, bf16[290,128]{1,0:T(8,128)(2,1)S(1)}, u32[]{:S(2)}, u32[]{:S(2)}) collective-permute-start(bf16[290,128]{1,0:T(8,128)(2,1)S(1)} %get-tuple-element.44), channel_id=1, source_target_pairs={{0,1},{1,2},{2,3},{3,0},{4,5},{5,6},{6,7},{7,4},{8,9},{9,10},{10,1... | collective-permute-start | bytes 222728 | tf_op jit(solution)/shard_map/ppermute | solution.py:31
  39.6 26.2 %collective-permute-start.22 = (bf16[15,48,384]{2,1,0:T(8,128)(2,1)}, bf16[15,48,384]{2,1,0:T(8,128)(2,1)S(1)}, u32[]{:S(2)}, u32[]{:S(2)}) collective-permute-start(bf16[15,48,384]{2,1,0:T(8,128)(2,1)} %collective-permute-done.4.refs_19_), channel_id=1, source_target_pairs={{0,16},{1,17},{2,18},{3,19},{4,20},{5,21},{6,22},{7,23},{8,24},{9,... | collective-permute-start | bytes 1658888 | tf_op jit(solution)/shard_map/ppermute | solution.py:25
  41.1 18.6 %collective-permute-start.15 = (bf16[7,48,384]{2,1,0:T(8,128)(2,1)S(1)}, bf16[7,48,384]{2,1,0:T(8,128)(2,1)}, u32[]{:S(2)}, u32[]{:S(2)}) collective-permute-start(bf16[7,48,384]{2,1,0:T(8,128)(2,1)S(1)} %slice.121), channel_id=1, source_target_pairs={{0,8},{1,9},{2,10},{3,11},{4,12},{5,13},{6,14},{7,15},{8,0},{9,1},... | collective-permute-start | bytes 774152 | tf_op jit(solution)/shard_map/ppermute | solution.py:25
  42.5 23.8 %collective-permute-start.6 = (bf16[15,48,384]{2,1,0:T(8,128)(2,1)}, bf16[15,48,384]{2,1,0:T(8,128)(2,1)S(1)}, u32[]{:S(2)}, u32[]{:S(2)}) collective-permute-start(bf16[15,48,384]{2,1,0:T(8,128)(2,1)} %collective-permute-done.4.refs_19_), channel_id=1, source_target_pairs={{0,1},{1,2},{2,3},{3,0},{4,5},{5,6},{6,7},{7,4},{8,9},{9,10},{10,1... | collective-permute-start | bytes 1658888 | tf_op jit(solution)/shard_map/ppermute | solution.py:31
  42.5 16.5 %collective-permute-start.7 = (bf16[290,128]{1,0:T(8,128)(2,1)S(1)}, bf16[290,128]{1,0:T(8,128)(2,1)S(1)}, u32[]{:S(2)}, u32[]{:S(2)}) collective-permute-start(bf16[290,128]{1,0:T(8,128)(2,1)S(1)} %collective-permute-done.5), channel_id=1, source_target_pairs={{0,1},{1,2},{2,3},{3,0},{4,5},{5,6},{6,7},{7,4},{8,9},{9,10},{10,1... | collective-permute-start | bytes 222728 | tf_op jit(solution)/shard_map/ppermute | solution.py:31
  43.6 22.8 %collective-permute-start.20 = (bf16[15,48,384]{2,1,0:T(8,128)(2,1)}, bf16[15,48,384]{2,1,0:T(8,128)(2,1)S(1)}, u32[]{:S(2)}, u32[]{:S(2)}) collective-permute-start(bf16[15,48,384]{2,1,0:T(8,128)(2,1)} %collective-permute-done.4.refs_19_), channel_id=1, source_target_pairs={{0,8},{1,9},{2,10},{3,11},{4,12},{5,13},{6,14},{7,15},{8,0},{9,1},... | collective-permute-start | bytes 1658888 | tf_op jit(solution)/shard_map/ppermute | solution.py:25
  59.1 6.7 %collective-permute-start.17 = (bf16[8,48,384]{2,1,0:T(8,128)(2,1)S(1)}, bf16[8,48,384]{2,1,0:T(8,128)(2,1)S(1)}, u32[]{:S(2)}, u32[]{:S(2)}) collective-permute-start(bf16[8,48,384]{2,1,0:T(8,128)(2,1)S(1)} %slice.122), channel_id=1, source_target_pairs={{0,16},{1,17},{2,18},{3,19},{4,20},{5,21},{6,22},{7,23},{8,24},{9,... | collective-permute-start | bytes 884744 | tf_op jit(solution)/shard_map/ppermute | solution.py:25
  59.7 8.9 %collective-permute-start.14 = (bf16[15,48,384]{2,1,0:T(8,128)(2,1)S(1)}, bf16[15,48,384]{2,1,0:T(8,128)(2,1)}, u32[]{:S(2)}, u32[]{:S(2)}) collective-permute-start(bf16[15,48,384]{2,1,0:T(8,128)(2,1)S(1)} %collective-permute-done.13.refs_13_), channel_id=1, source_target_pairs={{0,4},{1,5},{2,6},{3,7},{4,0},{5,1},{6,2},{7,3},{8,12},{9,13},{10,... | collective-permute-start | bytes 1658888 | tf_op jit(solution)/shard_map/ppermute | solution.py:25
  65.8 8.2 %collective-permute-start.12 = (bf16[15,48,384]{2,1,0:T(8,128)(2,1)S(1)}, bf16[15,48,384]{2,1,0:T(8,128)(2,1)}, u32[]{:S(2)}, u32[]{:S(2)}) collective-permute-start(bf16[15,48,384]{2,1,0:T(8,128)(2,1)S(1)} %collective-permute-done.11.refs_11_), channel_id=1, source_target_pairs={{0,4},{1,5},{2,6},{3,7},{4,0},{5,1},{6,2},{7,3},{8,12},{9,13},{10,... | collective-permute-start | bytes 1658888 | tf_op jit(solution)/shard_map/ppermute | solution.py:25
  66.3 8.7 %collective-permute-start.19 = (bf16[15,48,384]{2,1,0:T(8,128)(2,1)}, bf16[15,48,384]{2,1,0:T(8,128)(2,1)}, u32[]{:S(2)}, u32[]{:S(2)}) collective-permute-start(bf16[15,48,384]{2,1,0:T(8,128)(2,1)} %collective-permute-done.4.refs_19_), channel_id=1, source_target_pairs={{0,4},{1,5},{2,6},{3,7},{4,0},{5,1},{6,2},{7,3},{8,12},{9,13},{10,... | collective-permute-start | bytes 1658888 | tf_op jit(solution)/shard_map/ppermute | solution.py:25
  67.1 6.2 %collective-permute-start.9 = (bf16[290,128]{1,0:T(8,128)(2,1)S(1)}, bf16[290,128]{1,0:T(8,128)(2,1)S(1)}, u32[]{:S(2)}, u32[]{:S(2)}) collective-permute-start(bf16[290,128]{1,0:T(8,128)(2,1)S(1)} %collective-permute-done.7), channel_id=1, source_target_pairs={{0,1},{1,2},{2,3},{3,0},{4,5},{5,6},{6,7},{7,4},{8,9},{9,10},{10,1... | collective-permute-start | bytes 222728 | tf_op jit(solution)/shard_map/ppermute | solution.py:31
  68.5 8.7 %collective-permute-start.18 = (bf16[8,48,384]{2,1,0:T(8,128)(2,1)S(1)}, bf16[8,48,384]{2,1,0:T(8,128)(2,1)}, u32[]{:S(2)}, u32[]{:S(2)}) collective-permute-start(bf16[8,48,384]{2,1,0:T(8,128)(2,1)S(1)} %collective-permute-done.17.refs_17_), channel_id=1, source_target_pairs={{0,4},{1,5},{2,6},{3,7},{4,0},{5,1},{6,2},{7,3},{8,12},{9,13},{10,... | collective-permute-start | bytes 884744 | tf_op jit(solution)/shard_map/ppermute | solution.py:25
  68.6 9.2 %collective-permute-start.24 = (bf16[7,48,384]{2,1,0:T(8,128)(2,1)S(1)}, bf16[7,48,384]{2,1,0:T(8,128)(2,1)}, u32[]{:S(2)}, u32[]{:S(2)}) collective-permute-start(bf16[7,48,384]{2,1,0:T(8,128)(2,1)S(1)} %slice.123), channel_id=1, source_target_pairs={{0,8},{1,9},{2,10},{3,11},{4,12},{5,13},{6,14},{7,15},{8,0},{9,1},... | collective-permute-start | bytes 774152 | tf_op jit(solution)/shard_map/ppermute | solution.py:25
  73.3 16.3 %collective-permute-start.8 = (bf16[15,48,384]{2,1,0:T(8,128)(2,1)}, bf16[15,48,384]{2,1,0:T(8,128)(2,1)}, u32[]{:S(2)}, u32[]{:S(2)}) collective-permute-start(bf16[15,48,384]{2,1,0:T(8,128)(2,1)} %copy-done.14), channel_id=1, source_target_pairs={{0,8},{1,9},{2,10},{3,11},{4,12},{5,13},{6,14},{7,15},{8,0},{9,1},... | collective-permute-start | bytes 1658888 | tf_op jit(solution)/shard_map/ppermute | solution.py:25
  74.0 10.0 %collective-permute-start.26 = (bf16[8,48,384]{2,1,0:T(8,128)(2,1)S(1)}, bf16[8,48,384]{2,1,0:T(8,128)(2,1)S(1)}, u32[]{:S(2)}, u32[]{:S(2)}) collective-permute-start(bf16[8,48,384]{2,1,0:T(8,128)(2,1)S(1)} %slice.124), channel_id=1, source_target_pairs={{0,16},{1,17},{2,18},{3,19},{4,20},{5,21},{6,22},{7,23},{8,24},{9,... | collective-permute-start | bytes 884744 | tf_op jit(solution)/shard_map/ppermute | solution.py:25
  75.0 26.0 %collective-permute-start.32 = (bf16[15,48,384]{2,1,0:T(8,128)(2,1)}, bf16[15,48,384]{2,1,0:T(8,128)(2,1)}, u32[]{:S(2)}, u32[]{:S(2)}) collective-permute-start(bf16[15,48,384]{2,1,0:T(8,128)(2,1)} %copy-done.14), channel_id=1, source_target_pairs={{0,24},{1,25},{2,26},{3,27},{4,28},{5,29},{6,30},{7,31},{8,16},{9,... | collective-permute-start | bytes 1658888 | tf_op jit(solution)/shard_map/ppermute | solution.py:25
  77.2 28.3 %collective-permute-start.30 = (bf16[15,48,384]{2,1,0:T(8,128)(2,1)}, bf16[15,48,384]{2,1,0:T(8,128)(2,1)}, u32[]{:S(2)}, u32[]{:S(2)}) collective-permute-start(bf16[15,48,384]{2,1,0:T(8,128)(2,1)} %copy-done.14), channel_id=1, source_target_pairs={{0,16},{1,17},{2,18},{3,19},{4,20},{5,21},{6,22},{7,23},{8,24},{9,... | collective-permute-start | bytes 1658888 | tf_op jit(solution)/shard_map/ppermute | solution.py:25
  77.8 27.7 %collective-permute-start.23 = (bf16[15,48,384]{2,1,0:T(8,128)(2,1)S(1)}, bf16[15,48,384]{2,1,0:T(8,128)(2,1)S(1)}, u32[]{:S(2)}, u32[]{:S(2)}) collective-permute-start(bf16[15,48,384]{2,1,0:T(8,128)(2,1)S(1)} %collective-permute-done.22.refs_23_), channel_id=1, source_target_pairs={{0,4},{1,5},{2,6},{3,7},{4,0},{5,1},{6,2},{7,3},{8,12},{9,13},{10,... | collective-permute-start | bytes 1658888 | tf_op jit(solution)/shard_map/ppermute | solution.py:25
  84.1 22.0 %collective-permute-start.21 = (bf16[15,48,384]{2,1,0:T(8,128)(2,1)S(1)}, bf16[15,48,384]{2,1,0:T(8,128)(2,1)}, u32[]{:S(2)}, u32[]{:S(2)}) collective-permute-start(bf16[15,48,384]{2,1,0:T(8,128)(2,1)S(1)} %collective-permute-done.20.refs_21_), channel_id=1, source_target_pairs={{0,4},{1,5},{2,6},{3,7},{4,0},{5,1},{6,2},{7,3},{8,12},{9,13},{10,... | collective-permute-start | bytes 1658888 | tf_op jit(solution)/shard_map/ppermute | solution.py:25
  89.6 4.9 %collective-permute-start.25 = (bf16[7,48,384]{2,1,0:T(8,128)(2,1)}, bf16[7,48,384]{2,1,0:T(8,128)(2,1)}, u32[]{:S(2)}, u32[]{:S(2)}) collective-permute-start(bf16[7,48,384]{2,1,0:T(8,128)(2,1)} %collective-permute-done.24.refs_25_), channel_id=1, source_target_pairs={{0,4},{1,5},{2,6},{3,7},{4,0},{5,1},{6,2},{7,3},{8,12},{9,13},{10,... | collective-permute-start | bytes 774152 | tf_op jit(solution)/shard_map/ppermute | solution.py:25
  94.5 11.7 %collective-permute-start.28 = (bf16[15,48,384]{2,1,0:T(8,128)(2,1)S(1)}, bf16[15,48,384]{2,1,0:T(8,128)(2,1)S(1)}, u32[]{:S(2)}, u32[]{:S(2)}) collective-permute-start(bf16[15,48,384]{2,1,0:T(8,128)(2,1)S(1)} %copy-done.15), channel_id=1, source_target_pairs={{0,4},{1,5},{2,6},{3,7},{4,0},{5,1},{6,2},{7,3},{8,12},{9,13},{10,... | collective-permute-start | bytes 1658888 | tf_op jit(solution)/shard_map/ppermute | solution.py:25
  101.0 7.3 %collective-permute-start.33 = (bf16[15,48,384]{2,1,0:T(8,128)(2,1)}, bf16[15,48,384]{2,1,0:T(8,128)(2,1)S(1)}, u32[]{:S(2)}, u32[]{:S(2)}) collective-permute-start(bf16[15,48,384]{2,1,0:T(8,128)(2,1)} %collective-permute-done.32.refs_35_), channel_id=1, source_target_pairs={{0,4},{1,5},{2,6},{3,7},{4,0},{5,1},{6,2},{7,3},{8,12},{9,13},{10,... | collective-permute-start | bytes 1658888 | tf_op jit(solution)/shard_map/ppermute | solution.py:25
  105.5 2.8 %collective-permute-start.31 = (bf16[15,48,384]{2,1,0:T(8,128)(2,1)}, bf16[15,48,384]{2,1,0:T(8,128)(2,1)}, u32[]{:S(2)}, u32[]{:S(2)}) collective-permute-start(bf16[15,48,384]{2,1,0:T(8,128)(2,1)} %collective-permute-done.30.refs_33_), channel_id=1, source_target_pairs={{0,4},{1,5},{2,6},{3,7},{4,0},{5,1},{6,2},{7,3},{8,12},{9,13},{10,... | collective-permute-start | bytes 1658888 | tf_op jit(solution)/shard_map/ppermute | solution.py:25
  105.6 3.4 %collective-permute-start.29 = (bf16[15,48,384]{2,1,0:T(8,128)(2,1)}, bf16[15,48,384]{2,1,0:T(8,128)(2,1)S(1)}, u32[]{:S(2)}, u32[]{:S(2)}) collective-permute-start(bf16[15,48,384]{2,1,0:T(8,128)(2,1)} %collective-permute-done.8.refs_31_), channel_id=1, source_target_pairs={{0,4},{1,5},{2,6},{3,7},{4,0},{5,1},{6,2},{7,3},{8,12},{9,13},{10,... | collective-permute-start | bytes 1658888 | tf_op jit(solution)/shard_map/ppermute | solution.py:25
  (26 other events, 208.4 us)

commit v3 on v2

v3 whole, which is shorter than its diff:
```python
import functools
import jax
import jax.numpy as jnp
from jax import lax
from jax.experimental import pallas as pl
from jax.experimental.pallas import tpu as pltpu
from jax.sharding import PartitionSpec as P

LAT_W = 256
EPS = 1e-06
HALO = 8
CHUNK = 3
VMEM_BYTES = 60 * 1024 * 1024
ENTER_VMEM = 16 * 1024 * 1024

CORE, NEAR, FAR = 1, 2, 4


def place():
    seq = lax.axis_index("seq")
    return lax.rem(seq, 2), lax.rem(lax.div(seq, 2), 4)


def swap(array, mask, chan_mask=0):
    seqs, chans = lax.axis_size("seq"), lax.axis_size("chan")
    pairs = [(s * chans + c, (s ^ mask) * chans + (c ^ chan_mask)) for s in range(seqs) for c in range(chans)]
    return lax.ppermute(array, ("seq", "chan"), pairs)


def shift(array, steps=1):
    seqs, chans = lax.axis_size("seq"), lax.axis_size("chan")
    pairs = [(s * chans + c, s * chans + (c + steps) % chans) for s in range(seqs) for c in range(chans)]
    return lax.ppermute(array, ("seq", "chan"), pairs)


def in_order(found):
    chans, chan = lax.axis_size("chan"), lax.axis_index("chan")
    found = jnp.stack(found)
    return jnp.stack(
        [lax.dynamic_index_in_dim(found, lax.rem(chan + chans - c, chans), 0, False) for c in range(chans)]
    )


def gather_frame(held):
    mask = 1
    while mask < lax.axis_size("seq"):
        held = jnp.concatenate([held, swap(held, mask)], 0)
        mask *= 2
    return held


def thirds(values):
    parts = []
    for _ in range(3):
        part = lax.reduce_precision(values, 8, 7)
        parts.append(part.astype(jnp.bfloat16))
        values = values - part
    return parts


def spread(own, small, finish, early):
    units = own.shape[0]
    cut, third = units // 2, (units - early) // 3
    mid, end = early + third, early + 2 * third
    x, y, across = NEAR // 2, FAR // 2, (NEAR | FAR) // 2
    settle = lax.optimization_barrier
    pieces = []

    def add(array, *parts):
        twin = swap(array, CORE)
        pieces.extend([(0, parts, array), (1, parts, twin)])
        return twin

    held_1, small_1 = settle((shift(own), shift(small)))
    held_2, small_2 = shift(held_1), shift(small_1)
    near_1, far_1 = swap(held_1, NEAR), swap(held_1, FAR)
    twin = add(held_1, (0, 1, 0, units))
    held_2, small_2, near_1, far_1, twin = settle((held_2, small_2, near_1, far_1, twin))
    held_3, small_3 = shift(held_2), shift(small_2)
    near_2 = swap(jnp.concatenate([held_2, far_1[:cut]], 0), NEAR)
    far_2 = swap(jnp.concatenate([held_2, near_1[cut:]], 0), FAR)
    twins = [
        add(near_1, (x, 1, 0, units)), add(far_1, (y, 1, 0, units)), add(held_2, (0, 2, 0, units)),
    ]
    held_3, small_3, near_2, far_2, twins = settle((held_3, small_3, near_2, far_2, twins))
    across_2 = shift(jnp.concatenate([near_2[units:], far_2[units:]], 0))
    near_3, far_3, first_3 = swap(held_3, NEAR), swap(held_3, FAR), swap(held_3[:early], NEAR | FAR)
    twins = [
        add(near_2, (x, 2, 0, units), (across, 1, 0, cut)),
        add(far_2, (y, 2, 0, units), (across, 1, cut, units - cut)),
        add(held_3, (0, 3, 0, units)),
    ]
    across_2, near_3, far_3, first_3, twins, extra = settle(
        (across_2, near_3, far_3, first_3, twins, finish(in_order([small, small_1, small_2, small_3])))
    )
    add(near_3, (x, 3, 0, units))
    add(far_3, (y, 3, 0, units))
    add(across_2, (across, 2, 0, units))
    add(first_3, (across, 3, 0, early))
    late = [
        (swap(far_3[early:mid], NEAR), (across, 3, early, third)),
        (swap(near_3[mid:end], FAR), (across, 3, mid, third)),
        (shift(across_2[end:]), (across, 3, end, units - end)),
    ]

    def last(gate):
        for array, part in late:
            add(settle((array, gate))[0], part)
        return pieces

    return pieces, last, extra


def groups_of(low, high, per_early, per_late):
    found = []
    for begin, per_chip, at in ((0, per_early, 0), (4 * per_early, per_late, per_early)):
        for chip in range(4):
            first = begin + chip * per_chip
            lowest, highest = max(first, low), min(first + per_chip, high)
            if lowest < highest:
                found.append((chip, at + lowest - first, lowest, highest - lowest))
    return tuple(found)


def own_slice(units, per_chip):
    core, chip = place()
    rows = units.shape[1] // 2
    return lax.dynamic_slice(units, (chip * per_chip, core * rows, 0), (per_chip, rows, units.shape[2]))


def load_weights(groups, metas, chans, own, pieces, weights, sems):
    core, chip = place()
    chan = lax.axis_index("chan")
    base = groups[0][2]
    depth = own[0][0].shape[1]
    half = depth // 2

    def start_own(group, unit, units):
        at = pl.multiple_of(chan * depth, 16)
        for ref, begin in own:
            first, end = max(unit, begin), min(unit + units, begin + ref.shape[0])
            if first < end:
                dst = weights.at[pl.ds(first - base, end - first), pl.ds(at, depth), :]
                src = ref.at[pl.ds(first - begin, end - first)]
                pltpu.make_async_copy(src, dst, sems.at[group, 0]).start()

    def start_others(group, place_in, unit, units, chip_mask):
        for (core_mask, parts), ref in zip(metas, pieces):
            at = 0
            for mask, step, first, count in parts:
                low, high = max(first, place_in), min(first + count, place_in + units)
                if mask == chip_mask and low < high:
                    shard = lax.rem(chan + chans - step, chans)
                    row = pl.multiple_of(shard * depth + (core ^ core_mask) * half, 16)
                    to = unit - base + low - place_in
                    dst = weights.at[pl.ds(to, high - low), pl.ds(row, half), :]
                    src = ref.at[pl.ds(at + low - first, high - low)]
                    pltpu.make_async_copy(src, dst, sems.at[group, 2 * step - 1 + core_mask]).start()
                at += count

    for here in range(4):

        @pl.when(chip == here)
        def _():
            for group, (owner, place_in, unit, units) in enumerate(groups):
                start_own(group, unit, units)
                start_others(group, place_in, unit, units, here ^ owner)

    left = list(enumerate(groups))

    def need(end):
        while left and left[0][1][2] < end:
            group, (_, _, unit, units) = left.pop(0)
            taken = sum(
                max(0, min(unit + units, begin + ref.shape[0]) - max(unit, begin)) for ref, begin in own
            )
            mine = weights.at[pl.ds(unit - base, taken), pl.ds(0, depth), :]
            pltpu.make_async_copy(mine, mine, sems.at[group, 0]).wait()
            slice_of = weights.at[pl.ds(unit - base, units), pl.ds(0, half), :]
            for i in range(1, 2 * chans - 1):
                pltpu.make_async_copy(slice_of, slice_of, sems.at[group, i]).wait()

    return need


def inside(rows, width, first_row, first_col, height):
    row = first_row + lax.broadcasted_iota(jnp.int32, (rows, width, 1), 0)
    col = first_col + lax.broadcasted_iota(jnp.int32, (rows, width, 1), 1)
    ok = (row >= 0) & (row < height) & (col >= 0) & (col < LAT_W)
    return jnp.where(ok, 1.0, 0.0).astype(jnp.float32).reshape(rows * width, 1)


def norm_act(values, gain, shift_by, mask):
    mean_sq = jnp.mean(values * values, axis=1, keepdims=True)
    scaled = values * lax.rsqrt(mean_sq + EPS) * gain + shift_by
    half = 0.5 * scaled * mask
    return half + half * jnp.tanh(0.5 * scaled)


def set_columns(cols, values, at=0):
    cells, chans = values.shape
    cols[at : at + cells, :chans] = pltpu.roll(values, 1, 0).astype(jnp.bfloat16)
    cols[at : at + cells, chans : 2 * chans] = values.astype(jnp.bfloat16)
    cols[at : at + cells, 2 * chans :] = pltpu.roll(values, cells - 1, 0).astype(jnp.bfloat16)


def conv(cols, weights, unit, row, rows, width):
    chans = weights.shape[1]
    total = None
    for row_tap in range(3):
        taps = weights[unit + 3 * row_tap : unit + 3 * row_tap + 3].reshape(3 * chans, chans)
        at = (row + row_tap - 1) * width
        part = jnp.dot(cols[at : at + rows * width, :], taps, preferred_element_type=jnp.float32)
        total = part if total is None else total + part
    return total


def chunks(low, high):
    count = max(1, (high - low) // CHUNK)
    cuts = [low + (high - low) * i // count for i in range(count + 1)]
    return list(zip(cuts[:-1], cuts[1:]))


def tile_corner(slab_rows, tile_cols, halo):
    return (
        lax.axis_index("seq") * slab_rows - halo,
        lax.axis_index("chan") * tile_cols - HALO,
    )


def enter_kernel(static, params, in_weight, frame, out_ref, slab, wide, in_cols, sems):
    chans, rows, width, slab_rows, height = static
    tile_cols = LAT_W // chans
    lat, tokens = frame.shape[1:]
    blocks = LAT_W // tokens
    first_row, first_col = tile_corner(slab_rows, tile_cols, HALO)
    fetches = []
    for row in range(rows + 2):
        held = (first_row + row >= 0) & (first_row + row < height)
        at = jnp.clip(first_row + row, 0, height - 1)
        owner = lax.div(at, slab_rows) ^ lax.axis_index("seq")
        start = (owner * slab_rows + lax.rem(at, slab_rows)) * blocks
        fetch = pltpu.make_async_copy(frame.at[pl.ds(start, blocks)], slab.at[row], sems.at[row])
        pl.when(held)(fetch.start)
        fetches.append((held, fetch))
    for held, fetch in fetches:
        pl.when(held)(fetch.wait)
    for row in range(rows + 2):
        for block in range(blocks):
            at = 2 * HALO + block * tokens
            wide[row, at : at + tokens, :] = slab[row, block].astype(jnp.float32).T
    left = pl.multiple_of(lax.axis_index("chan") * tile_cols + HALO, 8)
    region = wide[:, pl.ds(left, width), :].reshape((rows + 2) * width, lat)
    mask = inside(rows + 2, width, first_row, first_col, height)
    set_columns(in_cols, jnp.where(mask > 0.0, region, 0.0))
    total = params[3, 0][None]
    for row_tap in range(3):
        part = in_cols[row_tap * width : (row_tap + rows) * width, :]
        total = total + jnp.dot(part, in_weight[row_tap], preferred_element_type=jnp.float32)
    out_ref[...] = total.astype(jnp.bfloat16)


def tile_kernel(static, *refs):
    chans, layers, begin, end, width, rows, slab_rows, height, groups, metas = static
    upsamples = end == layers
    params, up_bias, entered, res_ref, up_ref = refs[:5]
    pieces = refs[5 : 5 + len(metas)]
    n_outs = chans if upsamples else 1
    outs = refs[5 + len(metas) : 5 + len(metas) + n_outs]
    weights, held, cols_a, cols_b, last, woven, sems = refs[5 + len(metas) + n_outs :]
    gain, shift_by, bias = params[0], params[1], params[2]
    tile_cols = LAT_W // chans
    n_res = res_ref.shape[0]
    need = load_weights(groups, metas, chans, ((res_ref, 0), (up_ref, n_res)), pieces, weights, sems)
    base = groups[0][2]
    corner = tile_corner(slab_rows, tile_cols, (rows - slab_rows) // 2)

    def norm(values, index, row, stop):
        mask = inside(stop - row, width, corner[0] + row, corner[1], height)
        return norm_act(values, gain[index][None], shift_by[index][None], mask)

    held[...] = entered[...].astype(jnp.float32)
    for low, high in chunks(0, rows):
        set_columns(cols_a, norm(held[low * width : high * width, :], 2 * begin, low, high), low * width)
    for layer in range(begin, end):
        margin, unit = 2 * (layer - begin) + 1, 18 * layer
        need(unit + 9)
        for low, high in chunks(margin, rows - margin):
            middle = conv(cols_a, weights, unit - base, low, high - low, width) + bias[2 * layer][None]
            set_columns(cols_b, norm(middle, 2 * layer + 1, low, high), low * width)
        need(unit + 18)
        for low, high in chunks(margin + 1, rows - margin - 1):
            branch = conv(cols_b, weights, unit + 9 - base, low, high - low, width) + bias[2 * layer + 1][None]
            cells = slice(low * width, high * width)
            out_cells = slice((low - margin - 1) * width, (high - margin - 1) * width)
            stream = (held[cells, :] + branch).astype(jnp.bfloat16)
            if layer < end - 1:
                held[cells, :] = stream.astype(jnp.float32)
                set_columns(cols_a, norm(held[cells, :], 2 * layer + 2, low, high), low * width)
            elif upsamples:
                mask = inside(high - low, width, corner[0] + low, corner[1], height)
                last[out_cells, :] = (stream.astype(jnp.float32) * mask).astype(jnp.bfloat16)
            else:
                outs[0][out_cells, :] = stream
    need(n_res + up_ref.shape[0])
    if not upsamples:
        return
    framed = last[...]
    rows = framed.shape[0] // width
    n_out = up_bias.shape[1]
    products = []
    for pair in range(up_ref.shape[0]):
        both = jnp.dot(framed, weights[n_res - base + pair], preferred_element_type=jnp.float32)
        products += [both[:, :n_out], both[:, n_out:]]
    cells = rows * width
    even, odd = [], []
    for row_tap in range(3):
        left, mid, right = products[3 * row_tap : 3 * row_tap + 3]
        even.append(pltpu.roll(left, 1, 0) + mid + right)
        odd.append(left + mid + pltpu.roll(right, cells - 1, 0))
    share = n_out // chans
    chan = lax.axis_index("chan")
    for row in range(slab_rows):
        for low in range(2):
            for parity, parts in ((0, even), (1, odd)):
                total = up_bias[...]
                for row_tap in range(3):
                    at = (row + 1 + (low + row_tap - 1) // 2) * width + HALO
                    total = total + parts[row_tap][at : at + tile_cols]
                for tile in range(woven.shape[0]):
                    lanes = total[:, 128 * tile : 128 * tile + 128]
                    if lanes.shape[1] < 128:
                        blank = jnp.zeros((tile_cols, 128 - lanes.shape[1]), jnp.float32)
                        lanes = jnp.concatenate([lanes, blank], 1)
                    woven[tile, pl.ds(parity, tile_cols, 2), :] = lanes
            turned = jnp.concatenate([woven[tile].T for tile in range(woven.shape[0])], 0)
            for owner in range(chans):
                part = turned[owner * share : (owner + 1) * share].astype(jnp.bfloat16)
                for step in range(chans):

                    @pl.when(lax.rem(chan + step, chans) == owner)
                    def _():
                        outs[step][2 * row + low] = part


def body(
    latent, in_weight, in_bias, norm_gain, norm_shift, res_weight, res_bias, up_weight, up_bias
):
    seqs, chans = lax.axis_size("seq"), lax.axis_size("chan")
    layers, _, taps, depth, ch = res_weight.shape
    outs = up_weight.shape[2]
    tokens, lat = latent.shape
    slab_rows = tokens * chans // LAT_W
    height = slab_rows * seqs
    tile_cols = LAT_W // chans
    width = -(-(tile_cols + 2 * HALO) // 16) * 16
    rows = slab_rows + 2 * (HALO - 1)
    vmem = pl.BlockSpec(memory_space=pltpu.VMEM)

    norms = [a.reshape(2 * layers, depth) for a in (norm_gain, norm_shift, res_bias)]
    ends = jnp.zeros((2 * layers, depth), jnp.float32)
    ends = ends.at[0].set(in_bias).at[1, : outs // chans].set(up_bias)
    smalls = [*thirds(jnp.concatenate(norms + [ends], 1)), in_weight.reshape(-1, ch)]
    smalls = jnp.concatenate(smalls, 0)
    n_small = smalls.shape[0]
    smalls = [smalls[:, at : at + tokens] for at in range(0, ch, tokens)]
    smalls = jnp.concatenate([*smalls, gather_frame(latent.T[None]).reshape(-1, tokens)], 0)

    def small_args(packed):
        n_lanes = ch // tokens
        frame = packed[:, n_small * n_lanes :].reshape(chans, seqs, lat, tokens).transpose(1, 0, 2, 3)
        frame = frame.reshape(seqs * chans, lat, tokens)
        packed = jnp.concatenate([packed[:, n_small * i : n_small * (i + 1)] for i in range(n_lanes)], 2)
        params = sum(packed[:, 2 * layers * i : 2 * layers * (i + 1)].astype(jnp.float32) for i in range(3))
        params = params.reshape(chans, 2 * layers, 4, depth).transpose(2, 1, 0, 3)
        up_b = params[3, 1, :, : outs // chans].reshape(1, outs)
        params = params.reshape(4, 2 * layers, ch)
        in_w = packed[:, 6 * layers :].reshape(chans, 3, taps // 3, lat // chans, ch)
        in_w = in_w.transpose(1, 2, 0, 3, 4).reshape(3, taps // 3 * lat, ch)
        entered = pl.pallas_call(
            functools.partial(enter_kernel, (chans, rows, width, slab_rows, height)),
            out_shape=jax.ShapeDtypeStruct((rows * width, ch), jnp.bfloat16),
            in_specs=[vmem, vmem, pl.BlockSpec(memory_space=pl.ANY)],
            out_specs=vmem,
            scratch_shapes=[
                pltpu.VMEM((rows + 2, LAT_W // tokens, lat, tokens), jnp.bfloat16),
                pltpu.VMEM((rows + 2, LAT_W + 4 * HALO, lat), jnp.float32),
                pltpu.VMEM(((rows + 2) * width, 3 * lat), jnp.bfloat16),
                pltpu.SemaphoreType.DMA((rows + 2,)),
            ],
            compiler_params=pltpu.CompilerParams(vmem_limit_bytes=ENTER_VMEM),
        )(params, in_w, frame)
        return params, up_b, entered

    res_units = res_weight.reshape(layers * 2 * taps, depth, ch)
    up_units = jnp.pad(up_weight, ((0, 1), (0, 0), (0, 0))).reshape(-1, 2, depth, outs)
    up_units = up_units.transpose(0, 2, 1, 3).reshape(-1, depth, 2 * outs)
    n_units = res_units.shape[0] + up_units.shape[0]
    per_early = -(-2 * taps // 4)
    per_late = -(-(n_units - 4 * per_early) // 4)
    late_units = jnp.concatenate([res_units[4 * per_early :], up_units], 0)
    late_units = jnp.pad(late_units, ((0, 4 * per_late - late_units.shape[0]), (0, 0), (0, 0)))
    mine = [own_slice(res_units[: 4 * per_early], per_early), own_slice(late_units, per_late)]
    pieces, last_pieces, small = spread(jnp.concatenate(mine, 0), smalls, small_args, per_early)
    params, up_b, stream = small

    def run(begin, end, rows, stream, pieces):
        first, stop = 2 * taps * begin, 2 * taps * end
        if end == layers:
            stop = 4 * (per_early + per_late)
            out_shape, n_out = (2 * slab_rows, outs // chans, 2 * tile_cols), chans
        else:
            out_shape, n_out = ((rows - 4 * (end - begin)) * width, ch), 1
        groups = groups_of(first, stop, per_early, per_late)
        metas = tuple((core, parts) for core, parts, _ in pieces)
        in_vmem = [params, up_b, stream]
        in_any = [res_units, up_units] + [array for _, _, array in pieces]
        cells = sum(rows - 2 * i for i in range(1, 2 * (end - begin) + 1)) * width
        return pl.pallas_call(
            functools.partial(
                tile_kernel, (chans, layers, begin, end, width, rows, slab_rows, height, groups, metas)
            ),
            out_shape=[jax.ShapeDtypeStruct(out_shape, jnp.bfloat16)] * n_out,
            in_specs=[vmem] * len(in_vmem) + [pl.BlockSpec(memory_space=pl.ANY)] * len(in_any),
            out_specs=[vmem] * n_out,
            scratch_shapes=[
                pltpu.VMEM((stop - first, ch, ch), jnp.bfloat16),
                pltpu.VMEM((rows * width, ch), jnp.float32),
                pltpu.VMEM((rows * width, 3 * ch), jnp.bfloat16),
                pltpu.VMEM((rows * width, 3 * ch), jnp.bfloat16),
                pltpu.VMEM(((slab_rows + 2) * width, ch), jnp.bfloat16),
                pltpu.VMEM((-(-outs // 128), 2 * tile_cols, 128), jnp.float32),
                pltpu.SemaphoreType.DMA((len(groups), 2 * chans - 1)),
            ],
            compiler_params=pltpu.CompilerParams(vmem_limit_bytes=VMEM_BYTES),
            cost_estimate=pl.CostEstimate(
                flops=4 * taps * ch * ch * cells, bytes_accessed=(stop - first) * ch * ch * 2, transcendentals=0
            ),
        )(*in_vmem, *in_any)

    [stream] = run(0, 1, rows, stream, pieces)
    shares = run(1, layers, rows - 4, stream, last_pieces(stream))
    shares = in_order([shares[0]] + [shift(shares[step], step) for step in range(1, chans)])
    return shares.transpose(2, 1, 0, 3).reshape(outs // chans, 2 * slab_rows, 2 * LAT_W)


def solution(mesh):
    placed = (
        P(("seq", "chan"), None),
        P(None, "chan", None),
        P("chan"),
        P(None, None, "chan"),
        P(None, None, "chan"),
        P(None, None, None, "chan", None),
        P(None, None, "chan"),
        P(None, "chan", None),
        P("chan"),
    )
    return jax.shard_map(
        body, mesh=mesh, in_specs=placed, out_specs=P("chan", "seq", None), check_vma=False
    )
```

time: 156 us -> 139 us (0.89)
  waiting for transfers between devices: 76.4 us -> 57.7 us
  blocking collectives: 11.4 us -> 0 us
  starting transfers between devices: 21.3 us -> 31.1 us
  local copies, waits for them, and re-layouts: 11.1 us -> 16 us
  Pallas kernels: 33.5 us -> 31.7 us
    ppermute x28 -> x26, waiting for transfers between devices: 36.6 us -> 17.1 us  [swap(): return lax.ppermute(array, ('seq', 'chan'), pairs)]
    all_to_all x1 -> x0, blocking collectives: 11.4 us -> none  [body(): turned = lax.all_to_all(shares, 'chan', 0, 0, tiled=True)]
    ppermute x6 -> x11, starting transfers between devices: 3.98 us -> 13.2 us  [shift(): return lax.ppermute(array, ('seq', 'chan'), pairs)]
    slice x6 -> x10, local copies, waits for them, and re-layouts: 0.26 us -> 7 us  [the longest x1 2.73 us: body(): res_units[:4 * per_early]]
    another operation x4 -> x0, local copies, waits for them, and re-layouts: 2.69 us -> none  [the longest x3 2.02 us: small_args(): gain, shift_by, bias = (params[i].reshape(2 * layers, ch) for i in range(3))]
    pallas_call x1 -> x3, Pallas kernels: 33.5 us -> 31.7 us  [the longest x2 29.8 us: run(): pl.pallas_call(functools.partial(tile_kernel, (chans, layers, begin, end,...]
    unnamed x48 -> x62, local copies, waits for them, and re-layouts: 2.95 us -> 4.19 us
    ppermute x6 -> x11, waiting for transfers between devices: 39.8 us -> 40.6 us  [shift(): return lax.ppermute(array, ('seq', 'chan'), pairs)]
  transfers between devices with their start and end apart: 34 -> 37, of which waited for: 14 -> 16; matrix products, arithmetic and copies ran while one was open for 6% -> 2% of each run, Pallas kernels for 0% -> 11%
where the time goes in v3:
time: 139 us
  waiting for transfers between devices  57.7 us (42%)
  Pallas kernels  31.7 us (23%)
  starting transfers between devices  31.1 us (22%)
  local copies, waits for them, and re-layouts  16 us (12%)
  other arithmetic  1.68 us (1%)
    ppermute x11, waiting for transfers between devices, shift(): return lax.ppermute(array, ('seq', 'chan'), pairs)  40.6 us
    pallas_call x2, Pallas kernels, run(): pl.pallas_call(functools.partial(tile_kernel, (chans, layers, begin, end,...  29.8 us
    ppermute x26, starting transfers between devices, swap(): return lax.ppermute(array, ('seq', 'chan'), pairs)  17.9 us
    ppermute x26, waiting for transfers between devices, swap(): return lax.ppermute(array, ('seq', 'chan'), pairs)  17.1 us
    ppermute x11, starting transfers between devices, shift(): return lax.ppermute(array, ('seq', 'chan'), pairs)  13.2 us
    unnamed x62, local copies, waits for them, and re-layouts  4.19 us
  transfers between devices with their start and end apart: 37, of which 16 were waited for; matrix products, arithmetic and copies ran while one was open for 2% of the time, Pallas kernels for 11%

profile of v3, /device:TPU:0, one launch (start us, length us, event | category | flops | bytes accessed | tf_op | source)
XLA Modules:
  0.0 138.9 jit_solution(7447494114644710404)
XLA Ops:
  0.0 2.0 %slice.122 = bf16[34,96,384]{2,1,0:T(8,128)(2,1)S(1)} slice(bf16[54,96,384]{2,1,0:T(8,128)(2,1)} %bitcast.35), slice={[20:54], [0:96], [0:384]} | slice | bytes 5013504 | tf_op jit(solution)/shard_map/slice | solution.py:401
  2.0 2.7 %slice.121 = bf16[20,96,384]{2,1,0:T(8,128)(2,1)} slice(bf16[54,96,384]{2,1,0:T(8,128)(2,1)} %bitcast.36), slice={[0:20], [0:96], [0:384]} | slice | bytes 2949120 | tf_op jit(solution)/shard_map/slice | solution.py:403
  5.7 1.1 constant_dynamic-slice_fusion.8
  7.0 3.1 %collective-permute-start = (bf16[15,48,384]{2,1,0:T(8,128)(2,1)S(1)}, bf16[15,48,384]{2,1,0:T(8,128)(2,1)S(1)}, u32[]{:S(2)}, u32[]{:S(2)}) collective-permute-start(bf16[15,48,384]{2,1,0:T(8,128)(2,1)S(1)} %pad_maximum_fusion.2), channel_id=1, source_target_pairs={{0,1},{1,2},{2,3},{3,0},{4,5},{5,6},{6,7},{7,4},{8,9},{9,10},{10,1... | collective-permute-start | bytes 1658888 | tf_op jit(solution)/shard_map/ppermute | solution.py:33
  11.3 1.5 %collective-permute-start.2 = (bf16[2,16,128]{2,1,0:T(8,128)(2,1)S(1)}, bf16[2,16,128]{2,1,0:T(8,128)(2,1)S(1)}, u32[]{:S(2)}, u32[]{:S(2)}) collective-permute-start(bf16[2,16,128]{2,1,0:T(8,128)(2,1)S(1)} %pad_maximum_fusion.23), channel_id=1, source_target_pairs={{0,8},{1,9},{2,10},{3,11},{4,12},{5,13},{6,14},{7,15},{8,0},{9,1},... | collective-permute-start | bytes 24584 | tf_op jit(solution)/shard_map/ppermute | solution.py:27
  12.8 2.1 %collective-permute-done.2 = bf16[2,16,128]{2,1,0:T(8,128)(2,1)S(1)} collective-permute-done((bf16[2,16,128]{2,1,0:T(8,128)(2,1)S(1)}, bf16[2,16,128]{2,1,0:T(8,128)(2,1)S(1)}, u32[]{:S(2)}, u32[]{:S(2)}) %collective-permute-start.2) | collective-permute-done | bytes 8224 | tf_op jit(solution)/shard_map/ppermute | solution.py:27
  15.0 1.5 %collective-permute-start.3 = (bf16[4,16,128]{2,1,0:T(8,128)(2,1)S(1)}, bf16[4,16,128]{2,1,0:T(8,128)(2,1)S(1)}, u32[]{:S(2)}, u32[]{:S(2)}) collective-permute-start(bf16[4,16,128]{2,1,0:T(8,128)(2,1)S(1)} %pad_maximum_fusion.21), channel_id=1, source_target_pairs={{0,16},{1,17},{2,18},{3,19},{4,20},{5,21},{6,22},{7,23},{8,24},{9,... | collective-permute-start | bytes 49160 | tf_op jit(solution)/shard_map/ppermute | solution.py:27
  16.5 2.2 %collective-permute-done.3 = bf16[4,16,128]{2,1,0:T(8,128)(2,1)S(1)} collective-permute-done((bf16[4,16,128]{2,1,0:T(8,128)(2,1)S(1)}, bf16[4,16,128]{2,1,0:T(8,128)(2,1)S(1)}, u32[]{:S(2)}, u32[]{:S(2)}) %collective-permute-start.3) | collective-permute-done | bytes 16416 | tf_op jit(solution)/shard_map/ppermute | solution.py:27
  18.7 1.6 %collective-permute-start.4 = (bf16[290,128]{1,0:T(8,128)(2,1)S(1)}, bf16[290,128]{1,0:T(8,128)(2,1)S(1)}, u32[]{:S(2)}, u32[]{:S(2)}) collective-permute-start(bf16[290,128]{1,0:T(8,128)(2,1)S(1)} %get-tuple-element.86), channel_id=1, source_target_pairs={{0,1},{1,2},{2,3},{3,0},{4,5},{5,6},{6,7},{7,4},{8,9},{9,10},{10,1... | collective-permute-start | bytes 222728 | tf_op jit(solution)/shard_map/ppermute | solution.py:33
  20.4 6.0 %collective-permute-done.4 = bf16[290,128]{1,0:T(8,128)(2,1)S(1)} collective-permute-done((bf16[290,128]{1,0:T(8,128)(2,1)S(1)}, bf16[290,128]{1,0:T(8,128)(2,1)S(1)}, u32[]{:S(2)}, u32[]{:S(2)}) %collective-permute-start.4) | collective-permute-done | bytes 74272 | tf_op jit(solution)/shard_map/ppermute | solution.py:33
  26.3 1.6 %collective-permute-start.7 = (bf16[15,48,384]{2,1,0:T(8,128)(2,1)S(1)}, bf16[15,48,384]{2,1,0:T(8,128)(2,1)S(1)}, u32[]{:S(2)}, u32[]{:S(2)}) collective-permute-start(bf16[15,48,384]{2,1,0:T(8,128)(2,1)S(1)} %collective-permute-done.refs_5_), channel_id=1, source_target_pairs={{0,8},{1,9},{2,10},{3,11},{4,12},{5,13},{6,14},{7,15},{8,0},{9,1},... | collective-permute-start | bytes 1658888 | tf_op jit(solution)/shard_map/ppermute | solution.py:27
  27.9 1.5 %collective-permute-start.8 = (bf16[15,48,384]{2,1,0:T(8,128)(2,1)S(1)}, bf16[15,48,384]{2,1,0:T(8,128)(2,1)S(1)}, u32[]{:S(2)}, u32[]{:S(2)}) collective-permute-start(bf16[15,48,384]{2,1,0:T(8,128)(2,1)S(1)} %collective-permute-done.refs_5_), channel_id=1, source_target_pairs={{0,16},{1,17},{2,18},{3,19},{4,20},{5,21},{6,22},{7,23},{8,24},{9,... | collective-permute-start | bytes 1658888 | tf_op jit(solution)/shard_map/ppermute | solution.py:27
  29.4 1.2 collective-permute-start.6
  30.6 12.8 %collective-permute-done.6 = bf16[290,128]{1,0:T(8,128)(2,1)S(1)} collective-permute-done((bf16[290,128]{1,0:T(8,128)(2,1)S(1)}, bf16[290,128]{1,0:T(8,128)(2,1)S(1)}, u32[]{:S(2)}, u32[]{:S(2)}) %collective-permute-start.6) | collective-permute-done | bytes 74272 | tf_op jit(solution)/shard_map/ppermute | solution.py:33
  44.5 1.3 collective-permute-start.13
  46.0 1.6 %collective-permute-start.12 = (bf16[22,48,384]{2,1,0:T(8,128)(2,1)S(1)}, bf16[22,48,384]{2,1,0:T(8,128)(2,1)}, u32[]{:S(2)}, u32[]{:S(2)}) collective-permute-start(bf16[22,48,384]{2,1,0:T(8,128)(2,1)S(1)} %pad_maximum_fusion.1), channel_id=1, source_target_pairs={{0,8},{1,9},{2,10},{3,11},{4,12},{5,13},{6,14},{7,15},{8,0},{9,1},... | collective-permute-start | bytes 2433032 | tf_op jit(solution)/shard_map/ppermute | solution.py:27
  47.6 13.0 %collective-permute-done.11 = bf16[290,128]{1,0:T(8,128)(2,1)S(1)} collective-permute-done((bf16[290,128]{1,0:T(8,128)(2,1)S(1)}, bf16[290,128]{1,0:T(8,128)(2,1)S(1)}, u32[]{:S(2)}, u32[]{:S(2)}) %collective-permute-start.11) | collective-permute-done | bytes 74272 | tf_op jit(solution)/shard_map/ppermute | solution.py:33
  61.1 1.4 %collective-permute-done.15.refs_10_ = bf16[15,48,384]{2,1,0:T(8,128)(2,1)S(1)} collective-permute-done((bf16[15,48,384]{2,1,0:T(8,128)(2,1)S(1)}, bf16[15,48,384]{2,1,0:T(8,128)(2,1)S(1)}, u32[]{:S(2)}, u32[]{:S(2)}) %collective-permute-start.15) | collective-permute-done | bytes 552992 | tf_op jit(solution)/shard_map/ppermute | solution.py:27
  64.2 1.3 slice.106
  66.3 2.0 %collective-permute-start.20 = (bf16[5,48,384]{2,1,0:T(8,128)(2,1)S(1)}, bf16[5,48,384]{2,1,0:T(8,128)(2,1)}, u32[]{:S(2)}, u32[]{:S(2)}) collective-permute-start(bf16[5,48,384]{2,1,0:T(8,128)(2,1)S(1)} %slice.108), channel_id=1, source_target_pairs={{0,24},{1,25},{2,26},{3,27},{4,28},{5,29},{6,30},{7,31},{8,16},{9,... | collective-permute-start | bytes 552968 | tf_op jit(solution)/shard_map/ppermute | solution.py:27
  68.9 6.0 %collective-permute-done.20.refs_25_ = bf16[5,48,384]{2,1,0:T(8,128)(2,1)} collective-permute-done((bf16[5,48,384]{2,1,0:T(8,128)(2,1)S(1)}, bf16[5,48,384]{2,1,0:T(8,128)(2,1)}, u32[]{:S(2)}, u32[]{:S(2)}) %collective-permute-start.20) | collective-permute-done | bytes 184352 | tf_op jit(solution)/shard_map/ppermute | solution.py:27
  74.8 1.0 collective-permute-start.19
  75.8 6.2 %collective-permute-done.17.refs_23_ = bf16[15,48,384]{2,1,0:T(8,128)(2,1)S(1)} collective-permute-done((bf16[15,48,384]{2,1,0:T(8,128)(2,1)S(1)}, bf16[15,48,384]{2,1,0:T(8,128)(2,1)S(1)}, u32[]{:S(2)}, u32[]{:S(2)}) %collective-permute-start.17) | collective-permute-done | bytes 552992 | tf_op jit(solution)/shard_map/ppermute | solution.py:33
  83.3 1.9 %shard_map.91.refs_2_ = bf16[1280,384]{1,0:T(8,128)(2,1)S(1)} custom-call(f32[4,6,384]{2,1,0:T(8,128)S(1)} %copy.17.params, bf16[3,48,384]{2,1,0:T(8,128)(2,1)S(1)} %reshape.115.in_weight, bf16[32,16,128]{2,1,0:T(8,128)(2,1)S(1)} %bitcast.34), custom_call_target="tpu_custom_call" | custom-call | tf_op jit(solution)/shard_map/pallas_call | solution.py:380
  86.3 1.6 %collective-permute-done.19.refs_21_ = bf16[15,48,384]{2,1,0:T(8,128)(2,1)} collective-permute-done((bf16[15,48,384]{2,1,0:T(8,128)(2,1)S(1)}, bf16[15,48,384]{2,1,0:T(8,128)(2,1)}, u32[]{:S(2)}, u32[]{:S(2)}) %collective-permute-start.19) | collective-permute-done | bytes 552992 | tf_op jit(solution)/shard_map/ppermute | solution.py:27
  93.0 1.5 %collective-permute-start.28 = (bf16[3,48,384]{2,1,0:T(8,128)(2,1)S(1)}, bf16[3,48,384]{2,1,0:T(8,128)(2,1)S(1)}, u32[]{:S(2)}, u32[]{:S(2)}) collective-permute-start(bf16[3,48,384]{2,1,0:T(8,128)(2,1)S(1)} %slice.118), channel_id=1, source_target_pairs={{0,8},{1,9},{2,10},{3,11},{4,12},{5,13},{6,14},{7,15},{8,0},{9,1},... | collective-permute-start | bytes 331784 | tf_op jit(solution)/shard_map/ppermute | solution.py:27
  95.3 13.4 %shard_map.92.refs_2_ = bf16[960,384]{1,0:T(8,128)(2,1)} custom-call(f32[4,6,384]{2,1,0:T(8,128)} %copy.19.refs_0_, f32[1,192]{1,0:T(1,128)} %reshape_squeeze.3.refs_1_, bf16[1280,384]{1,0:T(8,128)(2,1)} %copy-done, bf16[54,96,384]{2,1,0:T(8,128)(2,1)} %bitcast.37, bf16[5,96,384]{2,1,0:T(8,128)(2,1)} %copy-done.2, bf16[15,48,384]{2,1,0:T(8,128)(2,1)} %copy-done.17, ...), custom_call_target="tpu_custom_call" | custom-call | flops 11041505280 | bytes 5308416 | tf_op jit(solution)/shard_map/pallas_call | solution.py:419
  111.9 16.4 %shard_map.93 = (bf16[4,48,128]{2,1,0:T(8,128)(2,1)}, bf16[4,48,128]{2,1,0:T(8,128)(2,1)}, bf16[4,48,128]{2,1,0:T(8,128)(2,1)}, bf16[4,48,128]{2,1,0:T(8,128)(2,1)}) custom-call(f32[4,6,384]{2,1,0:T(8,128)} %copy.19.refs_0_, f32[1,192]{1,0:T(1,128)} %reshape_squeeze.3.refs_1_, bf16[960,384]{1,0:T(8,128)(2,1)} %shard_map.92.refs_2_, ...), custom_call_target="tpu_custom_call" | custom-call | flops 11890851840 | bytes 12386304 | tf_op jit(solution)/shard_map/pallas_call | solution.py:419
  128.3 2.5 %collective-permute-start.34 = (bf16[4,48,128]{2,1,0:T(8,128)(2,1)}, bf16[4,48,128]{2,1,0:T(8,128)(2,1)S(1)}, u32[]{:S(2)}, u32[]{:S(2)}) collective-permute-start(bf16[4,48,128]{2,1,0:T(8,128)(2,1)} %get-tuple-element.74), channel_id=1, source_target_pairs={{0,1},{1,2},{2,3},{3,0},{4,5},{5,6},{6,7},{7,4},{8,9},{9,10},{10,1... | collective-permute-start | bytes 147464 | tf_op jit(solution)/shard_map/ppermute | solution.py:33
  130.8 1.6 %collective-permute-start.35 = (bf16[4,48,128]{2,1,0:T(8,128)(2,1)}, bf16[4,48,128]{2,1,0:T(8,128)(2,1)S(1)}, u32[]{:S(2)}, u32[]{:S(2)}) collective-permute-start(bf16[4,48,128]{2,1,0:T(8,128)(2,1)} %get-tuple-element.75), channel_id=1, source_target_pairs={{0,2},{1,3},{2,0},{3,1},{4,6},{5,7},{6,4},{7,5},{8,10},{9,11},{10,... | collective-permute-start | bytes 147464 | tf_op jit(solution)/shard_map/ppermute | solution.py:33
  132.4 2.2 %collective-permute-start.36 = (bf16[4,48,128]{2,1,0:T(8,128)(2,1)}, bf16[4,48,128]{2,1,0:T(8,128)(2,1)S(1)}, u32[]{:S(2)}, u32[]{:S(2)}) collective-permute-start(bf16[4,48,128]{2,1,0:T(8,128)(2,1)} %get-tuple-element.76), channel_id=1, source_target_pairs={{0,3},{1,0},{2,1},{3,2},{4,7},{5,4},{6,5},{7,6},{8,11},{9,8},{10,9... | collective-permute-start | bytes 147464 | tf_op jit(solution)/shard_map/ppermute | solution.py:33
  134.5 2.5 %collective-permute-done.35 = bf16[4,48,128]{2,1,0:T(8,128)(2,1)S(1)} collective-permute-done((bf16[4,48,128]{2,1,0:T(8,128)(2,1)}, bf16[4,48,128]{2,1,0:T(8,128)(2,1)S(1)}, u32[]{:S(2)}, u32[]{:S(2)}) %collective-permute-start.35) | collective-permute-done | bytes 49184 | tf_op jit(solution)/shard_map/ppermute | solution.py:33
  (161 shorter events, 19.9 us)
Async XLA Ops:
  7.0 19.3 %collective-permute-start = (bf16[15,48,384]{2,1,0:T(8,128)(2,1)S(1)}, bf16[15,48,384]{2,1,0:T(8,128)(2,1)S(1)}, u32[]{:S(2)}, u32[]{:S(2)}) collective-permute-start(bf16[15,48,384]{2,1,0:T(8,128)(2,1)S(1)} %pad_maximum_fusion.2), channel_id=1, source_target_pairs={{0,1},{1,2},{2,3},{3,0},{4,5},{5,6},{6,7},{7,4},{8,9},{9,10},{10,1... | collective-permute-start | bytes 1658888 | tf_op jit(solution)/shard_map/ppermute | solution.py:33
  11.3 3.7 %collective-permute-start.2 = (bf16[2,16,128]{2,1,0:T(8,128)(2,1)S(1)}, bf16[2,16,128]{2,1,0:T(8,128)(2,1)S(1)}, u32[]{:S(2)}, u32[]{:S(2)}) collective-permute-start(bf16[2,16,128]{2,1,0:T(8,128)(2,1)S(1)} %pad_maximum_fusion.23), channel_id=1, source_target_pairs={{0,8},{1,9},{2,10},{3,11},{4,12},{5,13},{6,14},{7,15},{8,0},{9,1},... | collective-permute-start | bytes 24584 | tf_op jit(solution)/shard_map/ppermute | solution.py:27
  15.0 3.7 %collective-permute-start.3 = (bf16[4,16,128]{2,1,0:T(8,128)(2,1)S(1)}, bf16[4,16,128]{2,1,0:T(8,128)(2,1)S(1)}, u32[]{:S(2)}, u32[]{:S(2)}) collective-permute-start(bf16[4,16,128]{2,1,0:T(8,128)(2,1)S(1)} %pad_maximum_fusion.21), channel_id=1, source_target_pairs={{0,16},{1,17},{2,18},{3,19},{4,20},{5,21},{6,22},{7,23},{8,24},{9,... | collective-permute-start | bytes 49160 | tf_op jit(solution)/shard_map/ppermute | solution.py:27
  18.7 7.6 %collective-permute-start.4 = (bf16[290,128]{1,0:T(8,128)(2,1)S(1)}, bf16[290,128]{1,0:T(8,128)(2,1)S(1)}, u32[]{:S(2)}, u32[]{:S(2)}) collective-permute-start(bf16[290,128]{1,0:T(8,128)(2,1)S(1)} %get-tuple-element.86), channel_id=1, source_target_pairs={{0,1},{1,2},{2,3},{3,0},{4,5},{5,6},{6,7},{7,4},{8,9},{9,10},{10,1... | collective-permute-start | bytes 222728 | tf_op jit(solution)/shard_map/ppermute | solution.py:33
  26.3 17.2 %collective-permute-start.5 = (bf16[15,48,384]{2,1,0:T(8,128)(2,1)S(1)}, bf16[15,48,384]{2,1,0:T(8,128)(2,1)S(1)}, u32[]{:S(2)}, u32[]{:S(2)}) collective-permute-start(bf16[15,48,384]{2,1,0:T(8,128)(2,1)S(1)} %collective-permute-done.refs_5_), channel_id=1, source_target_pairs={{0,1},{1,2},{2,3},{3,0},{4,5},{5,6},{6,7},{7,4},{8,9},{9,10},{10,1... | collective-permute-start | bytes 1658888 | tf_op jit(solution)/shard_map/ppermute | solution.py:33
  26.3 17.1 %collective-permute-start.7 = (bf16[15,48,384]{2,1,0:T(8,128)(2,1)S(1)}, bf16[15,48,384]{2,1,0:T(8,128)(2,1)S(1)}, u32[]{:S(2)}, u32[]{:S(2)}) collective-permute-start(bf16[15,48,384]{2,1,0:T(8,128)(2,1)S(1)} %collective-permute-done.refs_5_), channel_id=1, source_target_pairs={{0,8},{1,9},{2,10},{3,11},{4,12},{5,13},{6,14},{7,15},{8,0},{9,1},... | collective-permute-start | bytes 1658888 | tf_op jit(solution)/shard_map/ppermute | solution.py:27
  27.9 15.6 %collective-permute-start.8 = (bf16[15,48,384]{2,1,0:T(8,128)(2,1)S(1)}, bf16[15,48,384]{2,1,0:T(8,128)(2,1)S(1)}, u32[]{:S(2)}, u32[]{:S(2)}) collective-permute-start(bf16[15,48,384]{2,1,0:T(8,128)(2,1)S(1)} %collective-permute-done.refs_5_), channel_id=1, source_target_pairs={{0,16},{1,17},{2,18},{3,19},{4,20},{5,21},{6,22},{7,23},{8,24},{9,... | collective-permute-start | bytes 1658888 | tf_op jit(solution)/shard_map/ppermute | solution.py:27
  29.4 14.1 %collective-permute-start.9 = (bf16[15,48,384]{2,1,0:T(8,128)(2,1)S(1)}, bf16[15,48,384]{2,1,0:T(8,128)(2,1)S(1)}, u32[]{:S(2)}, u32[]{:S(2)}) collective-permute-start(bf16[15,48,384]{2,1,0:T(8,128)(2,1)S(1)} %collective-permute-done.refs_5_), channel_id=1, source_target_pairs={{0,4},{1,5},{2,6},{3,7},{4,0},{5,1},{6,2},{7,3},{8,12},{9,13},{10,... | collective-permute-start | bytes 1658888 | tf_op jit(solution)/shard_map/ppermute | solution.py:27
  29.4 14.1 %collective-permute-start.6 = (bf16[290,128]{1,0:T(8,128)(2,1)S(1)}, bf16[290,128]{1,0:T(8,128)(2,1)S(1)}, u32[]{:S(2)}, u32[]{:S(2)}) collective-permute-start(bf16[290,128]{1,0:T(8,128)(2,1)S(1)} %collective-permute-done.4), channel_id=1, source_target_pairs={{0,1},{1,2},{2,3},{3,0},{4,5},{5,6},{6,7},{7,4},{8,9},{9,10},{10,1... | collective-permute-start | bytes 222728 | tf_op jit(solution)/shard_map/ppermute | solution.py:33
  44.4 16.2 %collective-permute-start.10 = (bf16[15,48,384]{2,1,0:T(8,128)(2,1)S(1)}, bf16[15,48,384]{2,1,0:T(8,128)(2,1)S(1)}, u32[]{:S(2)}, u32[]{:S(2)}) collective-permute-start(bf16[15,48,384]{2,1,0:T(8,128)(2,1)S(1)} %collective-permute-done.5.refs_11_), channel_id=1, source_target_pairs={{0,1},{1,2},{2,3},{3,0},{4,5},{5,6},{6,7},{7,4},{8,9},{9,10},{10,1... | collective-permute-start | bytes 1658888 | tf_op jit(solution)/shard_map/ppermute | solution.py:33
  44.5 19.6 %collective-permute-start.13 = (bf16[23,48,384]{2,1,0:T(8,128)(2,1)S(1)}, bf16[23,48,384]{2,1,0:T(8,128)(2,1)S(1)}, u32[]{:S(2)}, u32[]{:S(2)}) collective-permute-start(bf16[23,48,384]{2,1,0:T(8,128)(2,1)S(1)} %pad_maximum_fusion), channel_id=1, source_target_pairs={{0,16},{1,17},{2,18},{3,19},{4,20},{5,21},{6,22},{7,23},{8,24},{9,... | collective-permute-start | bytes 2543624 | tf_op jit(solution)/shard_map/ppermute | solution.py:27
  46.0 18.0 %collective-permute-start.12 = (bf16[22,48,384]{2,1,0:T(8,128)(2,1)S(1)}, bf16[22,48,384]{2,1,0:T(8,128)(2,1)}, u32[]{:S(2)}, u32[]{:S(2)}) collective-permute-start(bf16[22,48,384]{2,1,0:T(8,128)(2,1)S(1)} %pad_maximum_fusion.1), channel_id=1, source_target_pairs={{0,8},{1,9},{2,10},{3,11},{4,12},{5,13},{6,14},{7,15},{8,0},{9,1},... | collective-permute-start | bytes 2433032 | tf_op jit(solution)/shard_map/ppermute | solution.py:27
  47.6 13.0 %collective-permute-start.11 = (bf16[290,128]{1,0:T(8,128)(2,1)S(1)}, bf16[290,128]{1,0:T(8,128)(2,1)S(1)}, u32[]{:S(2)}, u32[]{:S(2)}) collective-permute-start(bf16[290,128]{1,0:T(8,128)(2,1)S(1)} %collective-permute-done.6), channel_id=1, source_target_pairs={{0,1},{1,2},{2,3},{3,0},{4,5},{5,6},{6,7},{7,4},{8,9},{9,10},{10,1... | collective-permute-start | bytes 222728 | tf_op jit(solution)/shard_map/ppermute | solution.py:33
  47.6 13.6 %collective-permute-start.14 = (bf16[15,48,384]{2,1,0:T(8,128)(2,1)S(1)}, bf16[15,48,384]{2,1,0:T(8,128)(2,1)S(1)}, u32[]{:S(2)}, u32[]{:S(2)}) collective-permute-start(bf16[15,48,384]{2,1,0:T(8,128)(2,1)S(1)} %collective-permute-done.7.refs_7_), channel_id=1, source_target_pairs={{0,4},{1,5},{2,6},{3,7},{4,0},{5,1},{6,2},{7,3},{8,12},{9,13},{10,... | collective-permute-start | bytes 1658888 | tf_op jit(solution)/shard_map/ppermute | solution.py:27
  60.6 2.7 %collective-permute-start.16 = (bf16[15,48,384]{2,1,0:T(8,128)(2,1)S(1)}, bf16[15,48,384]{2,1,0:T(8,128)(2,1)S(1)}, u32[]{:S(2)}, u32[]{:S(2)}) collective-permute-start(bf16[15,48,384]{2,1,0:T(8,128)(2,1)S(1)} %collective-permute-done.5.refs_11_), channel_id=1, source_target_pairs={{0,4},{1,5},{2,6},{3,7},{4,0},{5,1},{6,2},{7,3},{8,12},{9,13},{10,... | collective-permute-start | bytes 1658888 | tf_op jit(solution)/shard_map/ppermute | solution.py:27
  65.6 16.4 %collective-permute-start.17 = (bf16[15,48,384]{2,1,0:T(8,128)(2,1)S(1)}, bf16[15,48,384]{2,1,0:T(8,128)(2,1)S(1)}, u32[]{:S(2)}, u32[]{:S(2)}) collective-permute-start(bf16[15,48,384]{2,1,0:T(8,128)(2,1)S(1)} %pad_maximum_fusion.3), channel_id=1, source_target_pairs={{0,1},{1,2},{2,3},{3,0},{4,5},{5,6},{6,7},{7,4},{8,9},{9,10},{10,1... | collective-permute-start | bytes 1658888 | tf_op jit(solution)/shard_map/ppermute | solution.py:33
  65.7 22.2 %collective-permute-start.22 = (bf16[23,48,384]{2,1,0:T(8,128)(2,1)S(1)}, bf16[23,48,384]{2,1,0:T(8,128)(2,1)}, u32[]{:S(2)}, u32[]{:S(2)}) collective-permute-start(bf16[23,48,384]{2,1,0:T(8,128)(2,1)S(1)} %collective-permute-done.13.refs_15_), channel_id=1, source_target_pairs={{0,4},{1,5},{2,6},{3,7},{4,0},{5,1},{6,2},{7,3},{8,12},{9,13},{10,... | collective-permute-start | bytes 2543624 | tf_op jit(solution)/shard_map/ppermute | solution.py:27
  65.9 22.0 %collective-permute-start.21 = (bf16[22,48,384]{2,1,0:T(8,128)(2,1)}, bf16[22,48,384]{2,1,0:T(8,128)(2,1)}, u32[]{:S(2)}, u32[]{:S(2)}) collective-permute-start(bf16[22,48,384]{2,1,0:T(8,128)(2,1)} %collective-permute-done.12.refs_13_), channel_id=1, source_target_pairs={{0,4},{1,5},{2,6},{3,7},{4,0},{5,1},{6,2},{7,3},{8,12},{9,13},{10,... | collective-permute-start | bytes 2433032 | tf_op jit(solution)/shard_map/ppermute | solution.py:27
  66.3 8.6 %collective-permute-start.20 = (bf16[5,48,384]{2,1,0:T(8,128)(2,1)S(1)}, bf16[5,48,384]{2,1,0:T(8,128)(2,1)}, u32[]{:S(2)}, u32[]{:S(2)}) collective-permute-start(bf16[5,48,384]{2,1,0:T(8,128)(2,1)S(1)} %slice.108), channel_id=1, source_target_pairs={{0,24},{1,25},{2,26},{3,27},{4,28},{5,29},{6,30},{7,31},{8,16},{9,... | collective-permute-start | bytes 552968 | tf_op jit(solution)/shard_map/ppermute | solution.py:27
  68.3 18.0 %collective-permute-start.18 = (bf16[15,48,384]{2,1,0:T(8,128)(2,1)S(1)}, bf16[15,48,384]{2,1,0:T(8,128)(2,1)S(1)}, u32[]{:S(2)}, u32[]{:S(2)}) collective-permute-start(bf16[15,48,384]{2,1,0:T(8,128)(2,1)S(1)} %collective-permute-done.10.refs_17_), channel_id=1, source_target_pairs={{0,8},{1,9},{2,10},{3,11},{4,12},{5,13},{6,14},{7,15},{8,0},{9,1},... | collective-permute-start | bytes 1658888 | tf_op jit(solution)/shard_map/ppermute | solution.py:27
  74.8 13.1 %collective-permute-start.19 = (bf16[15,48,384]{2,1,0:T(8,128)(2,1)S(1)}, bf16[15,48,384]{2,1,0:T(8,128)(2,1)}, u32[]{:S(2)}, u32[]{:S(2)}) collective-permute-start(bf16[15,48,384]{2,1,0:T(8,128)(2,1)S(1)} %collective-permute-done.10.refs_17_), channel_id=1, source_target_pairs={{0,16},{1,17},{2,18},{3,19},{4,20},{5,21},{6,22},{7,23},{8,24},{9,... | collective-permute-start | bytes 1658888 | tf_op jit(solution)/shard_map/ppermute | solution.py:27
  82.0 5.8 %collective-permute-start.23 = (bf16[15,48,384]{2,1,0:T(8,128)(2,1)S(1)}, bf16[15,48,384]{2,1,0:T(8,128)(2,1)}, u32[]{:S(2)}, u32[]{:S(2)}) collective-permute-start(bf16[15,48,384]{2,1,0:T(8,128)(2,1)S(1)} %collective-permute-done.10.refs_17_), channel_id=1, source_target_pairs={{0,4},{1,5},{2,6},{3,7},{4,0},{5,1},{6,2},{7,3},{8,12},{9,13},{10,... | collective-permute-start | bytes 1658888 | tf_op jit(solution)/shard_map/ppermute | solution.py:27
  87.9 5.1 %collective-permute-start.24 = (bf16[15,48,384]{2,1,0:T(8,128)(2,1)S(1)}, bf16[15,48,384]{2,1,0:T(8,128)(2,1)S(1)}, u32[]{:S(2)}, u32[]{:S(2)}) collective-permute-start(bf16[15,48,384]{2,1,0:T(8,128)(2,1)S(1)} %collective-permute-done.18.refs_19_), channel_id=1, source_target_pairs={{0,4},{1,5},{2,6},{3,7},{4,0},{5,1},{6,2},{7,3},{8,12},{9,13},{10,... | collective-permute-start | bytes 1658888 | tf_op jit(solution)/shard_map/ppermute | solution.py:27
  88.0 6.5 %collective-permute-start.25 = (bf16[15,48,384]{2,1,0:T(8,128)(2,1)}, bf16[15,48,384]{2,1,0:T(8,128)(2,1)S(1)}, u32[]{:S(2)}, u32[]{:S(2)}) collective-permute-start(bf16[15,48,384]{2,1,0:T(8,128)(2,1)} %collective-permute-done.19.refs_21_), channel_id=1, source_target_pairs={{0,4},{1,5},{2,6},{3,7},{4,0},{5,1},{6,2},{7,3},{8,12},{9,13},{10,... | collective-permute-start | bytes 1658888 | tf_op jit(solution)/shard_map/ppermute | solution.py:27
  88.5 6.0 %collective-permute-start.26 = (bf16[15,48,384]{2,1,0:T(8,128)(2,1)S(1)}, bf16[15,48,384]{2,1,0:T(8,128)(2,1)}, u32[]{:S(2)}, u32[]{:S(2)}) collective-permute-start(bf16[15,48,384]{2,1,0:T(8,128)(2,1)S(1)} %collective-permute-done.17.refs_23_), channel_id=1, source_target_pairs={{0,4},{1,5},{2,6},{3,7},{4,0},{5,1},{6,2},{7,3},{8,12},{9,13},{10,... | collective-permute-start | bytes 1658888 | tf_op jit(solution)/shard_map/ppermute | solution.py:27
  88.5 3.4 %collective-permute-start.27 = (bf16[5,48,384]{2,1,0:T(8,128)(2,1)}, bf16[5,48,384]{2,1,0:T(8,128)(2,1)S(1)}, u32[]{:S(2)}, u32[]{:S(2)}) collective-permute-start(bf16[5,48,384]{2,1,0:T(8,128)(2,1)} %collective-permute-done.20.refs_25_), channel_id=1, source_target_pairs={{0,4},{1,5},{2,6},{3,7},{4,0},{5,1},{6,2},{7,3},{8,12},{9,13},{10,... | collective-permute-start | bytes 552968 | tf_op jit(solution)/shard_map/ppermute | solution.py:27
  90.6 18.1 %collective-permute-start.32 = (bf16[4,48,384]{2,1,0:T(8,128)(2,1)S(1)}, bf16[4,48,384]{2,1,0:T(8,128)(2,1)S(1)}, u32[]{:S(2)}, u32[]{:S(2)}) collective-permute-start(bf16[4,48,384]{2,1,0:T(8,128)(2,1)S(1)} %slice.120), channel_id=1, source_target_pairs={{0,1},{1,2},{2,3},{3,0},{4,5},{5,6},{6,7},{7,4},{8,9},{9,10},{10,1... | collective-permute-start | bytes 442376 | tf_op jit(solution)/shard_map/ppermute | solution.py:33
  92.0 16.8 %collective-permute-start.30 = (bf16[3,48,384]{2,1,0:T(8,128)(2,1)S(1)}, bf16[3,48,384]{2,1,0:T(8,128)(2,1)S(1)}, u32[]{:S(2)}, u32[]{:S(2)}) collective-permute-start(bf16[3,48,384]{2,1,0:T(8,128)(2,1)S(1)} %slice.119), channel_id=1, source_target_pairs={{0,16},{1,17},{2,18},{3,19},{4,20},{5,21},{6,22},{7,23},{8,24},{9,... | collective-permute-start | bytes 331784 | tf_op jit(solution)/shard_map/ppermute | solution.py:27
  93.0 16.3 %collective-permute-start.28 = (bf16[3,48,384]{2,1,0:T(8,128)(2,1)S(1)}, bf16[3,48,384]{2,1,0:T(8,128)(2,1)S(1)}, u32[]{:S(2)}, u32[]{:S(2)}) collective-permute-start(bf16[3,48,384]{2,1,0:T(8,128)(2,1)S(1)} %slice.118), channel_id=1, source_target_pairs={{0,8},{1,9},{2,10},{3,11},{4,12},{5,13},{6,14},{7,15},{8,0},{9,1},... | collective-permute-start | bytes 331784 | tf_op jit(solution)/shard_map/ppermute | solution.py:27
  128.3 6.2 %collective-permute-start.34 = (bf16[4,48,128]{2,1,0:T(8,128)(2,1)}, bf16[4,48,128]{2,1,0:T(8,128)(2,1)S(1)}, u32[]{:S(2)}, u32[]{:S(2)}) collective-permute-start(bf16[4,48,128]{2,1,0:T(8,128)(2,1)} %get-tuple-element.74), channel_id=1, source_target_pairs={{0,1},{1,2},{2,3},{3,0},{4,5},{5,6},{6,7},{7,4},{8,9},{9,10},{10,1... | collective-permute-start | bytes 147464 | tf_op jit(solution)/shard_map/ppermute | solution.py:33
  130.8 6.3 %collective-permute-start.35 = (bf16[4,48,128]{2,1,0:T(8,128)(2,1)}, bf16[4,48,128]{2,1,0:T(8,128)(2,1)S(1)}, u32[]{:S(2)}, u32[]{:S(2)}) collective-permute-start(bf16[4,48,128]{2,1,0:T(8,128)(2,1)} %get-tuple-element.75), channel_id=1, source_target_pairs={{0,2},{1,3},{2,0},{3,1},{4,6},{5,7},{6,4},{7,5},{8,10},{9,11},{10,... | collective-permute-start | bytes 147464 | tf_op jit(solution)/shard_map/ppermute | solution.py:33
  132.4 4.7 %collective-permute-start.36 = (bf16[4,48,128]{2,1,0:T(8,128)(2,1)}, bf16[4,48,128]{2,1,0:T(8,128)(2,1)S(1)}, u32[]{:S(2)}, u32[]{:S(2)}) collective-permute-start(bf16[4,48,128]{2,1,0:T(8,128)(2,1)} %get-tuple-element.76), channel_id=1, source_target_pairs={{0,3},{1,0},{2,1},{3,2},{4,7},{5,4},{6,5},{7,6},{8,11},{9,8},{10,9... | collective-permute-start | bytes 147464 | tf_op jit(solution)/shard_map/ppermute | solution.py:33
  (36 other events, 211.6 us)

commit v4 on v3

--- a/solution.py
+++ b/solution.py
@@ -9,7 +9,8 @@
 LAT_W = 256
 EPS = 1e-06
 HALO = 8
-CHUNK = 3
+CHUNK = 2
+AHEAD = 2
 VMEM_BYTES = 60 * 1024 * 1024
 ENTER_VMEM = 16 * 1024 * 1024
 
@@ -66,8 +67,8 @@
     settle = lax.optimization_barrier
     pieces = []
 
-    def add(array, *parts):
-        twin = swap(array, CORE)
+    def add(array, *parts, behind=None):
+        twin = swap(array if behind is None else settle((array, behind))[0], CORE)
         pieces.extend([(0, parts, array), (1, parts, twin)])
         return twin
 
@@ -85,11 +86,9 @@
     held_3, small_3, near_2, far_2, twins = settle((held_3, small_3, near_2, far_2, twins))
     across_2 = shift(jnp.concatenate([near_2[units:], far_2[units:]], 0))
     near_3, far_3, first_3 = swap(held_3, NEAR), swap(held_3, FAR), swap(held_3[:early], NEAR | FAR)
-    twins = [
-        add(near_2, (x, 2, 0, units), (across, 1, 0, cut)),
-        add(far_2, (y, 2, 0, units), (across, 1, cut, units - cut)),
-        add(held_3, (0, 3, 0, units)),
-    ]
+    twins = add(near_2, (x, 2, 0, units), (across, 1, 0, cut))
+    twins = add(far_2, (y, 2, 0, units), (across, 1, cut, units - cut), behind=twins)
+    twins = add(held_3, (0, 3, 0, units), behind=twins)
     across_2, near_3, far_3, first_3, twins, extra = settle(
         (across_2, near_3, far_3, first_3, twins, finish(in_order([small, small_1, small_2, small_3])))
     )
@@ -122,10 +121,9 @@
     return tuple(found)
 
 
-def own_slice(units, per_chip):
-    core, chip = place()
+def own_slice(units, first, count, core):
     rows = units.shape[1] // 2
-    return lax.dynamic_slice(units, (chip * per_chip, core * rows, 0), (per_chip, rows, units.shape[2]))
+    return lax.dynamic_slice(units, (first, core * rows, 0), (count, rows, units.shape[2]))
 
 
 def load_weights(groups, metas, chans, own, pieces, weights, sems):
@@ -158,13 +156,17 @@
                     pltpu.make_async_copy(src, dst, sems.at[group, 2 * step - 1 + core_mask]).start()
                 at += count
 
-    for here in range(4):
-
-        @pl.when(chip == here)
-        def _():
-            for group, (owner, place_in, unit, units) in enumerate(groups):
-                start_own(group, unit, units)
+    def start(group):
+        owner, place_in, unit, units = groups[group]
+        start_own(group, unit, units)
+        for here in range(4):
+
+            @pl.when(chip == here)
+            def _():
                 start_others(group, place_in, unit, units, here ^ owner)
+
+    for group in range(min(AHEAD, len(groups))):
+        start(group)
 
     left = list(enumerate(groups))
 
@@ -179,6 +181,8 @@
             slice_of = weights.at[pl.ds(unit - base, units), pl.ds(0, half), :]
             for i in range(1, 2 * chans - 1):
                 pltpu.make_async_copy(slice_of, slice_of, sems.at[group, i]).wait()
+            if group + AHEAD < len(groups):
+                start(group + AHEAD)
 
     return need
 
@@ -190,35 +194,46 @@
     return jnp.where(ok, 1.0, 0.0).astype(jnp.float32).reshape(rows * width, 1)
 
 
-def norm_act(values, gain, shift_by, mask):
+def norm_act(values, half_gain, half_shift, mask):
     mean_sq = jnp.mean(values * values, axis=1, keepdims=True)
-    scaled = values * lax.rsqrt(mean_sq + EPS) * gain + shift_by
-    half = 0.5 * scaled * mask
-    return half + half * jnp.tanh(0.5 * scaled)
-
-
-def set_columns(cols, values, at=0):
+    half = (values * lax.rsqrt(mean_sq + EPS) * half_gain + half_shift) * mask
+    return half + half * jnp.tanh(half)
+
+
+def set_rows(cols, values, low, width, rows):
     cells, chans = values.shape
-    cols[at : at + cells, :chans] = pltpu.roll(values, 1, 0).astype(jnp.bfloat16)
-    cols[at : at + cells, chans : 2 * chans] = values.astype(jnp.bfloat16)
-    cols[at : at + cells, 2 * chans :] = pltpu.roll(values, cells - 1, 0).astype(jnp.bfloat16)
+    values = values.astype(jnp.bfloat16)
+    high = low + cells // width
+    for tap in range(3):
+        first, end = max(low + 1 - tap, 0), min(high + 1 - tap, rows)
+        skip = first - (low + 1 - tap)
+        part = values[skip * width : (skip + end - first) * width]
+        cols[first * width : end * width, tap * chans : (tap + 1) * chans] = part
 
 
 def conv(cols, weights, unit, row, rows, width):
     chans = weights.shape[1]
-    total = None
-    for row_tap in range(3):
-        taps = weights[unit + 3 * row_tap : unit + 3 * row_tap + 3].reshape(3 * chans, chans)
-        at = (row + row_tap - 1) * width
-        part = jnp.dot(cols[at : at + rows * width, :], taps, preferred_element_type=jnp.float32)
-        total = part if total is None else total + part
-    return total
+    taps = [
+        jnp.concatenate([weights[unit + tap + 3 * i] for i in range(3)], 0)
+        for tap in range(3)
+    ]
+    window = cols[row * width : (row + rows) * width, :]
+    every = jnp.dot(window, jnp.concatenate(taps, 1), preferred_element_type=jnp.float32)
+    left, mid, right = (every[:, i * chans : (i + 1) * chans] for i in range(3))
+    return pltpu.roll(left, 1, 0) + mid + pltpu.roll(right, rows * width - 1, 0)
 
 
 def chunks(low, high):
     count = max(1, (high - low) // CHUNK)
     cuts = [low + (high - low) * i // count for i in range(count + 1)]
     return list(zip(cuts[:-1], cuts[1:]))
+
+
+def set_columns(cols, values):
+    cells, chans = values.shape
+    cols[:cells, :chans] = pltpu.roll(values, 1, 0).astype(jnp.bfloat16)
+    cols[:cells, chans : 2 * chans] = values.astype(jnp.bfloat16)
+    cols[:cells, 2 * chans :] = pltpu.roll(values, cells - 1, 0).astype(jnp.bfloat16)
 
 
 def tile_corner(slab_rows, tile_cols, halo):
@@ -268,7 +283,7 @@
     n_outs = chans if upsamples else 1
     outs = refs[5 + len(metas) : 5 + len(metas) + n_outs]
     weights, held, cols_a, cols_b, last, woven, sems = refs[5 + len(metas) + n_outs :]
-    gain, shift_by, bias = params[0], params[1], params[2]
+    gain, shift_by, bias = 0.5 * params[0], 0.5 * params[1], params[2]
     tile_cols = LAT_W // chans
     n_res = res_ref.shape[0]
     need = load_weights(groups, metas, chans, ((res_ref, 0), (up_ref, n_res)), pieces, weights, sems)
@@ -281,13 +296,13 @@
 
     held[...] = entered[...].astype(jnp.float32)
     for low, high in chunks(0, rows):
-        set_columns(cols_a, norm(held[low * width : high * width, :], 2 * begin, low, high), low * width)
+        set_rows(cols_a, norm(held[low * width : high * width, :], 2 * begin, low, high), low, width, rows)
     for layer in range(begin, end):
         margin, unit = 2 * (layer - begin) + 1, 18 * layer
         need(unit + 9)
         for low, high in chunks(margin, rows - margin):
             middle = conv(cols_a, weights, unit - base, low, high - low, width) + bias[2 * layer][None]
-            set_columns(cols_b, norm(middle, 2 * layer + 1, low, high), low * width)
+            set_rows(cols_b, norm(middle, 2 * layer + 1, low, high), low, width, rows)
         need(unit + 18)
         for low, high in chunks(margin + 1, rows - margin - 1):
             branch = conv(cols_b, weights, unit + 9 - base, low, high - low, width) + bias[2 * layer + 1][None]
@@ -296,7 +311,7 @@
             stream = (held[cells, :] + branch).astype(jnp.bfloat16)
             if layer < end - 1:
                 held[cells, :] = stream.astype(jnp.float32)
-                set_columns(cols_a, norm(held[cells, :], 2 * layer + 2, low, high), low * width)
+                set_rows(cols_a, norm(held[cells, :], 2 * layer + 2, low, high), low, width, rows)
             elif upsamples:
                 mask = inside(high - low, width, corner[0] + low, corner[1], height)
                 last[out_cells, :] = (stream.astype(jnp.float32) * mask).astype(jnp.bfloat16)
@@ -398,9 +413,18 @@
     n_units = res_units.shape[0] + up_units.shape[0]
     per_early = -(-2 * taps // 4)
     per_late = -(-(n_units - 4 * per_early) // 4)
-    late_units = jnp.concatenate([res_units[4 * per_early :], up_units], 0)
-    late_units = jnp.pad(late_units, ((0, 4 * per_late - late_units.shape[0]), (0, 0), (0, 0)))
-    mine = [own_slice(res_units[: 4 * per_early], per_early), own_slice(late_units, per_late)]
+    begin = 4 * per_early + 3 * per_late
+    tail = jnp.concatenate([res_units[begin:], up_units], 0)
+    tail = jnp.pad(tail, ((0, per_late - tail.shape[0]), (0, 0), (0, 0)))
+    core, chip = place()
+    mine = [
+        own_slice(res_units, chip * per_early, per_early, core),
+        jnp.where(
+            chip == 3,
+            own_slice(tail, 0, per_late, core),
+            own_slice(res_units, 4 * per_early + jnp.minimum(chip, 2) * per_late, per_late, core),
+        ),
+    ]
     pieces, last_pieces, small = spread(jnp.concatenate(mine, 0), smalls, small_args, per_early)
     params, up_b, stream = small
 

time: 139 us -> 136 us (0.978)
  Pallas kernels: 31.7 us -> 29 us
  starting transfers between devices: 31.1 us -> 29.5 us
    ppermute x11, waiting for transfers between devices: 40.6 us -> 33.9 us  [shift(): return lax.ppermute(array, ('seq', 'chan'), pairs)]
    ppermute x26, waiting for transfers between devices: 17.1 us -> 22.9 us  [swap(): return lax.ppermute(array, ('seq', 'chan'), pairs)]
    slice x2 -> x1, local copies, waits for them, and re-layouts: 4.69 us -> 1.04 us  [body(): tail = jnp.concatenate([res_units[begin:], up_units], 0)]
    pallas_call x2, Pallas kernels: 29.8 us -> 27.1 us  [run(): pl.pallas_call(functools.partial(tile_kernel, (chans, layers, begin, end,...]
    unnamed x62 -> x64, local copies, waits for them, and re-layouts: 4.19 us -> 5.7 us
  transfers between devices with their start and end apart: 37 -> 37, of which waited for: 16 -> 17; matrix products, arithmetic and copies ran while one was open for 2% -> 5% of each run, Pallas kernels for 11% -> 10%
where the time goes in v4:
time: 136 us; the launch traced here: 135 us
  waiting for transfers between devices  56.8 us (42%)
  starting transfers between devices  29.5 us (22%)
  Pallas kernels  29 us (21%)
  local copies, waits for them, and re-layouts  16.4 us (12%)
  other arithmetic  2.56 us (2%)
    ppermute x11, waiting for transfers between devices, shift(): return lax.ppermute(array, ('seq', 'chan'), pairs)  33.9 us
    pallas_call x2, Pallas kernels, run(): pl.pallas_call(functools.partial(tile_kernel, (chans, layers, begin, end,...  27.1 us
    ppermute x26, waiting for transfers between devices, swap(): return lax.ppermute(array, ('seq', 'chan'), pairs)  22.9 us
    ppermute x26, starting transfers between devices, swap(): return lax.ppermute(array, ('seq', 'chan'), pairs)  16.8 us
    ppermute x11, starting transfers between devices, shift(): return lax.ppermute(array, ('seq', 'chan'), pairs)  12.7 us
    unnamed x64, local copies, waits for them, and re-layouts  5.7 us
  transfers between devices with their start and end apart: 37, of which 17 were waited for; matrix products, arithmetic and copies ran while one was open for 5% of the time, Pallas kernels for 10%

profile of v4, /device:TPU:0, one launch (start us, length us, event | category | flops | bytes accessed | tf_op | source)
XLA Modules:
  0.0 135.1 jit_solution(1901468463481716937)
XLA Ops:
  0.1 1.0 slice.117
  1.1 1.1 pad.14
  3.0 1.1 constant_dynamic-slice_fusion.8
  4.1 1.1 fusion.3
  5.2 3.1 %collective-permute-start = (bf16[15,48,384]{2,1,0:T(8,128)(2,1)S(1)}, bf16[15,48,384]{2,1,0:T(8,128)(2,1)S(1)}, u32[]{:S(2)}, u32[]{:S(2)}) collective-permute-start(bf16[15,48,384]{2,1,0:T(8,128)(2,1)S(1)} %pad_maximum_fusion.2), channel_id=1, source_target_pairs={{0,1},{1,2},{2,3},{3,0},{4,5},{5,6},{6,7},{7,4},{8,9},{9,10},{10,1... | collective-permute-start | bytes 1658888 | tf_op jit(solution)/shard_map/ppermute | solution.py:34
  9.5 1.5 %collective-permute-start.2 = (bf16[2,16,128]{2,1,0:T(8,128)(2,1)S(1)}, bf16[2,16,128]{2,1,0:T(8,128)(2,1)S(1)}, u32[]{:S(2)}, u32[]{:S(2)}) collective-permute-start(bf16[2,16,128]{2,1,0:T(8,128)(2,1)S(1)} %pad_maximum_fusion.23), channel_id=1, source_target_pairs={{0,8},{1,9},{2,10},{3,11},{4,12},{5,13},{6,14},{7,15},{8,0},{9,1},... | collective-permute-start | bytes 24584 | tf_op jit(solution)/shard_map/ppermute | solution.py:28
  11.0 2.1 %collective-permute-done.2 = bf16[2,16,128]{2,1,0:T(8,128)(2,1)S(1)} collective-permute-done((bf16[2,16,128]{2,1,0:T(8,128)(2,1)S(1)}, bf16[2,16,128]{2,1,0:T(8,128)(2,1)S(1)}, u32[]{:S(2)}, u32[]{:S(2)}) %collective-permute-start.2) | collective-permute-done | bytes 8224 | tf_op jit(solution)/shard_map/ppermute | solution.py:28
  13.1 1.5 %collective-permute-start.3 = (bf16[4,16,128]{2,1,0:T(8,128)(2,1)S(1)}, bf16[4,16,128]{2,1,0:T(8,128)(2,1)S(1)}, u32[]{:S(2)}, u32[]{:S(2)}) collective-permute-start(bf16[4,16,128]{2,1,0:T(8,128)(2,1)S(1)} %pad_maximum_fusion.21), channel_id=1, source_target_pairs={{0,16},{1,17},{2,18},{3,19},{4,20},{5,21},{6,22},{7,23},{8,24},{9,... | collective-permute-start | bytes 49160 | tf_op jit(solution)/shard_map/ppermute | solution.py:28
  14.7 2.2 %collective-permute-done.3 = bf16[4,16,128]{2,1,0:T(8,128)(2,1)S(1)} collective-permute-done((bf16[4,16,128]{2,1,0:T(8,128)(2,1)S(1)}, bf16[4,16,128]{2,1,0:T(8,128)(2,1)S(1)}, u32[]{:S(2)}, u32[]{:S(2)}) %collective-permute-start.3) | collective-permute-done | bytes 16416 | tf_op jit(solution)/shard_map/ppermute | solution.py:28
  16.9 1.6 %collective-permute-start.4 = (bf16[290,128]{1,0:T(8,128)(2,1)S(1)}, bf16[290,128]{1,0:T(8,128)(2,1)S(1)}, u32[]{:S(2)}, u32[]{:S(2)}) collective-permute-start(bf16[290,128]{1,0:T(8,128)(2,1)S(1)} %get-tuple-element.90), channel_id=1, source_target_pairs={{0,1},{1,2},{2,3},{3,0},{4,5},{5,6},{6,7},{7,4},{8,9},{9,10},{10,1... | collective-permute-start | bytes 222728 | tf_op jit(solution)/shard_map/ppermute | solution.py:34
  18.5 6.0 %collective-permute-done.4 = bf16[290,128]{1,0:T(8,128)(2,1)S(1)} collective-permute-done((bf16[290,128]{1,0:T(8,128)(2,1)S(1)}, bf16[290,128]{1,0:T(8,128)(2,1)S(1)}, u32[]{:S(2)}, u32[]{:S(2)}) %collective-permute-start.4) | collective-permute-done | bytes 74272 | tf_op jit(solution)/shard_map/ppermute | solution.py:34
  24.5 1.6 %collective-permute-start.7 = (bf16[15,48,384]{2,1,0:T(8,128)(2,1)S(1)}, bf16[15,48,384]{2,1,0:T(8,128)(2,1)S(1)}, u32[]{:S(2)}, u32[]{:S(2)}) collective-permute-start(bf16[15,48,384]{2,1,0:T(8,128)(2,1)S(1)} %collective-permute-done.refs_5_), channel_id=1, source_target_pairs={{0,8},{1,9},{2,10},{3,11},{4,12},{5,13},{6,14},{7,15},{8,0},{9,1},... | collective-permute-start | bytes 1658888 | tf_op jit(solution)/shard_map/ppermute | solution.py:28
  26.1 1.5 %collective-permute-start.8 = (bf16[15,48,384]{2,1,0:T(8,128)(2,1)S(1)}, bf16[15,48,384]{2,1,0:T(8,128)(2,1)S(1)}, u32[]{:S(2)}, u32[]{:S(2)}) collective-permute-start(bf16[15,48,384]{2,1,0:T(8,128)(2,1)S(1)} %collective-permute-done.refs_5_), channel_id=1, source_target_pairs={{0,16},{1,17},{2,18},{3,19},{4,20},{5,21},{6,22},{7,23},{8,24},{9,... | collective-permute-start | bytes 1658888 | tf_op jit(solution)/shard_map/ppermute | solution.py:28
  27.6 1.2 collective-permute-start.6
  28.8 12.8 %collective-permute-done.6 = bf16[290,128]{1,0:T(8,128)(2,1)S(1)} collective-permute-done((bf16[290,128]{1,0:T(8,128)(2,1)S(1)}, bf16[290,128]{1,0:T(8,128)(2,1)S(1)}, u32[]{:S(2)}, u32[]{:S(2)}) %collective-permute-start.6) | collective-permute-done | bytes 74272 | tf_op jit(solution)/shard_map/ppermute | solution.py:34
  42.7 1.3 collective-permute-start.13
  44.2 1.6 %collective-permute-start.12 = (bf16[22,48,384]{2,1,0:T(8,128)(2,1)S(1)}, bf16[22,48,384]{2,1,0:T(8,128)(2,1)S(1)}, u32[]{:S(2)}, u32[]{:S(2)}) collective-permute-start(bf16[22,48,384]{2,1,0:T(8,128)(2,1)S(1)} %pad_maximum_fusion.1), channel_id=1, source_target_pairs={{0,8},{1,9},{2,10},{3,11},{4,12},{5,13},{6,14},{7,15},{8,0},{9,1},... | collective-permute-start | bytes 2433032 | tf_op jit(solution)/shard_map/ppermute | solution.py:28
  45.8 13.0 %collective-permute-done.11 = bf16[290,128]{1,0:T(8,128)(2,1)S(1)} collective-permute-done((bf16[290,128]{1,0:T(8,128)(2,1)S(1)}, bf16[290,128]{1,0:T(8,128)(2,1)S(1)}, u32[]{:S(2)}, u32[]{:S(2)}) %collective-permute-start.11) | collective-permute-done | bytes 74272 | tf_op jit(solution)/shard_map/ppermute | solution.py:34
  59.3 1.4 %collective-permute-done.15.refs_10_ = bf16[15,48,384]{2,1,0:T(8,128)(2,1)S(1)} collective-permute-done((bf16[15,48,384]{2,1,0:T(8,128)(2,1)S(1)}, bf16[15,48,384]{2,1,0:T(8,128)(2,1)S(1)}, u32[]{:S(2)}, u32[]{:S(2)}) %collective-permute-start.15) | collective-permute-done | bytes 552992 | tf_op jit(solution)/shard_map/ppermute | solution.py:28
  62.2 2.3 %collective-permute-done.21.refs_14_ = bf16[22,48,384]{2,1,0:T(8,128)(2,1)S(1)} collective-permute-done((bf16[22,48,384]{2,1,0:T(8,128)(2,1)S(1)}, bf16[22,48,384]{2,1,0:T(8,128)(2,1)S(1)}, u32[]{:S(2)}, u32[]{:S(2)}) %collective-permute-start.21) | collective-permute-done | bytes 811040 | tf_op jit(solution)/shard_map/ppermute | solution.py:28
  65.5 1.0 slice.103
  66.6 1.6 %collective-permute-start.18 = (bf16[15,48,384]{2,1,0:T(8,128)(2,1)}, bf16[15,48,384]{2,1,0:T(8,128)(2,1)}, u32[]{:S(2)}, u32[]{:S(2)}) collective-permute-start(bf16[15,48,384]{2,1,0:T(8,128)(2,1)} %copy-done.6), channel_id=1, source_target_pairs={{0,8},{1,9},{2,10},{3,11},{4,12},{5,13},{6,14},{7,15},{8,0},{9,1},... | collective-permute-start | bytes 1658888 | tf_op jit(solution)/shard_map/ppermute | solution.py:28
  69.0 1.0 slice.104
  70.6 1.2 collective-permute-start.20
  72.8 1.9 %shard_map.91.refs_2_ = bf16[1280,384]{1,0:T(8,128)(2,1)S(1)} custom-call(f32[4,6,384]{2,1,0:T(8,128)S(1)} %copy.17.params, bf16[3,48,384]{2,1,0:T(8,128)(2,1)S(1)} %reshape.115.in_weight, bf16[32,16,128]{2,1,0:T(8,128)(2,1)S(1)} %bitcast.34), custom_call_target="tpu_custom_call" | custom-call | tf_op jit(solution)/shard_map/pallas_call | solution.py:395
  74.7 1.0 copy-done
  75.7 10.4 %collective-permute-done.20.refs_25_ = bf16[5,48,384]{2,1,0:T(8,128)(2,1)S(1)} collective-permute-done((bf16[5,48,384]{2,1,0:T(8,128)(2,1)S(1)}, bf16[5,48,384]{2,1,0:T(8,128)(2,1)S(1)}, u32[]{:S(2)}, u32[]{:S(2)}) %collective-permute-start.20) | collective-permute-done | bytes 184352 | tf_op jit(solution)/shard_map/ppermute | solution.py:28
  94.1 12.1 %shard_map.92.refs_2_ = bf16[960,384]{1,0:T(8,128)(2,1)} custom-call(f32[4,6,384]{2,1,0:T(8,128)} %copy.19.refs_0_, f32[1,192]{1,0:T(1,128)} %reshape_squeeze.3.refs_1_, bf16[1280,384]{1,0:T(8,128)(2,1)} %copy-done, bf16[54,96,384]{2,1,0:T(8,128)(2,1)} %bitcast.44, bf16[5,96,384]{2,1,0:T(8,128)(2,1)} %copy-done.2, bf16[15,48,384]{2,1,0:T(8,128)(2,1)} %copy-done.16, ...), custom_call_target="tpu_custom_call" | custom-call | flops 11041505280 | bytes 5308416 | tf_op jit(solution)/shard_map/pallas_call | solution.py:443
  109.5 15.0 %shard_map.93 = (bf16[4,48,128]{2,1,0:T(8,128)(2,1)}, bf16[4,48,128]{2,1,0:T(8,128)(2,1)}, bf16[4,48,128]{2,1,0:T(8,128)(2,1)}, bf16[4,48,128]{2,1,0:T(8,128)(2,1)}) custom-call(f32[4,6,384]{2,1,0:T(8,128)} %copy.19.refs_0_, f32[1,192]{1,0:T(1,128)} %reshape_squeeze.3.refs_1_, bf16[960,384]{1,0:T(8,128)(2,1)} %shard_map.92.refs_2_, ...), custom_call_target="tpu_custom_call" | custom-call | flops 11890851840 | bytes 12386304 | tf_op jit(solution)/shard_map/pallas_call | solution.py:443
  125.4 3.2 %collective-permute-start.35 = (bf16[4,48,128]{2,1,0:T(8,128)(2,1)}, bf16[4,48,128]{2,1,0:T(8,128)(2,1)S(1)}, u32[]{:S(2)}, u32[]{:S(2)}) collective-permute-start(bf16[4,48,128]{2,1,0:T(8,128)(2,1)} %get-tuple-element.79), channel_id=1, source_target_pairs={{0,2},{1,3},{2,0},{3,1},{4,6},{5,7},{6,4},{7,5},{8,10},{9,11},{10,... | collective-permute-start | bytes 147464 | tf_op jit(solution)/shard_map/ppermute | solution.py:34
  128.6 2.6 %collective-permute-start.36 = (bf16[4,48,128]{2,1,0:T(8,128)(2,1)}, bf16[4,48,128]{2,1,0:T(8,128)(2,1)S(1)}, u32[]{:S(2)}, u32[]{:S(2)}) collective-permute-start(bf16[4,48,128]{2,1,0:T(8,128)(2,1)} %get-tuple-element.80), channel_id=1, source_target_pairs={{0,3},{1,0},{2,1},{3,2},{4,7},{5,4},{6,5},{7,6},{8,11},{9,8},{10,9... | collective-permute-start | bytes 147464 | tf_op jit(solution)/shard_map/ppermute | solution.py:34
  131.7 1.6 %collective-permute-done.36 = bf16[4,48,128]{2,1,0:T(8,128)(2,1)S(1)} collective-permute-done((bf16[4,48,128]{2,1,0:T(8,128)(2,1)}, bf16[4,48,128]{2,1,0:T(8,128)(2,1)S(1)}, u32[]{:S(2)}, u32[]{:S(2)}) %collective-permute-start.36) | collective-permute-done | bytes 49184 | tf_op jit(solution)/shard_map/ppermute | solution.py:34
  (162 shorter events, 22.7 us)
Async XLA Ops:
  5.2 19.3 %collective-permute-start = (bf16[15,48,384]{2,1,0:T(8,128)(2,1)S(1)}, bf16[15,48,384]{2,1,0:T(8,128)(2,1)S(1)}, u32[]{:S(2)}, u32[]{:S(2)}) collective-permute-start(bf16[15,48,384]{2,1,0:T(8,128)(2,1)S(1)} %pad_maximum_fusion.2), channel_id=1, source_target_pairs={{0,1},{1,2},{2,3},{3,0},{4,5},{5,6},{6,7},{7,4},{8,9},{9,10},{10,1... | collective-permute-start | bytes 1658888 | tf_op jit(solution)/shard_map/ppermute | solution.py:34
  9.5 3.7 %collective-permute-start.2 = (bf16[2,16,128]{2,1,0:T(8,128)(2,1)S(1)}, bf16[2,16,128]{2,1,0:T(8,128)(2,1)S(1)}, u32[]{:S(2)}, u32[]{:S(2)}) collective-permute-start(bf16[2,16,128]{2,1,0:T(8,128)(2,1)S(1)} %pad_maximum_fusion.23), channel_id=1, source_target_pairs={{0,8},{1,9},{2,10},{3,11},{4,12},{5,13},{6,14},{7,15},{8,0},{9,1},... | collective-permute-start | bytes 24584 | tf_op jit(solution)/shard_map/ppermute | solution.py:28
  13.1 3.7 %collective-permute-start.3 = (bf16[4,16,128]{2,1,0:T(8,128)(2,1)S(1)}, bf16[4,16,128]{2,1,0:T(8,128)(2,1)S(1)}, u32[]{:S(2)}, u32[]{:S(2)}) collective-permute-start(bf16[4,16,128]{2,1,0:T(8,128)(2,1)S(1)} %pad_maximum_fusion.21), channel_id=1, source_target_pairs={{0,16},{1,17},{2,18},{3,19},{4,20},{5,21},{6,22},{7,23},{8,24},{9,... | collective-permute-start | bytes 49160 | tf_op jit(solution)/shard_map/ppermute | solution.py:28
  16.9 7.6 %collective-permute-start.4 = (bf16[290,128]{1,0:T(8,128)(2,1)S(1)}, bf16[290,128]{1,0:T(8,128)(2,1)S(1)}, u32[]{:S(2)}, u32[]{:S(2)}) collective-permute-start(bf16[290,128]{1,0:T(8,128)(2,1)S(1)} %get-tuple-element.90), channel_id=1, source_target_pairs={{0,1},{1,2},{2,3},{3,0},{4,5},{5,6},{6,7},{7,4},{8,9},{9,10},{10,1... | collective-permute-start | bytes 222728 | tf_op jit(solution)/shard_map/ppermute | solution.py:34
  24.5 17.2 %collective-permute-start.5 = (bf16[15,48,384]{2,1,0:T(8,128)(2,1)S(1)}, bf16[15,48,384]{2,1,0:T(8,128)(2,1)S(1)}, u32[]{:S(2)}, u32[]{:S(2)}) collective-permute-start(bf16[15,48,384]{2,1,0:T(8,128)(2,1)S(1)} %collective-permute-done.refs_5_), channel_id=1, source_target_pairs={{0,1},{1,2},{2,3},{3,0},{4,5},{5,6},{6,7},{7,4},{8,9},{9,10},{10,1... | collective-permute-start | bytes 1658888 | tf_op jit(solution)/shard_map/ppermute | solution.py:34
  24.5 17.1 %collective-permute-start.7 = (bf16[15,48,384]{2,1,0:T(8,128)(2,1)S(1)}, bf16[15,48,384]{2,1,0:T(8,128)(2,1)S(1)}, u32[]{:S(2)}, u32[]{:S(2)}) collective-permute-start(bf16[15,48,384]{2,1,0:T(8,128)(2,1)S(1)} %collective-permute-done.refs_5_), channel_id=1, source_target_pairs={{0,8},{1,9},{2,10},{3,11},{4,12},{5,13},{6,14},{7,15},{8,0},{9,1},... | collective-permute-start | bytes 1658888 | tf_op jit(solution)/shard_map/ppermute | solution.py:28
  26.1 15.6 %collective-permute-start.8 = (bf16[15,48,384]{2,1,0:T(8,128)(2,1)S(1)}, bf16[15,48,384]{2,1,0:T(8,128)(2,1)S(1)}, u32[]{:S(2)}, u32[]{:S(2)}) collective-permute-start(bf16[15,48,384]{2,1,0:T(8,128)(2,1)S(1)} %collective-permute-done.refs_5_), channel_id=1, source_target_pairs={{0,16},{1,17},{2,18},{3,19},{4,20},{5,21},{6,22},{7,23},{8,24},{9,... | collective-permute-start | bytes 1658888 | tf_op jit(solution)/shard_map/ppermute | solution.py:28
  27.6 14.1 %collective-permute-start.9 = (bf16[15,48,384]{2,1,0:T(8,128)(2,1)S(1)}, bf16[15,48,384]{2,1,0:T(8,128)(2,1)S(1)}, u32[]{:S(2)}, u32[]{:S(2)}) collective-permute-start(bf16[15,48,384]{2,1,0:T(8,128)(2,1)S(1)} %collective-permute-done.refs_5_), channel_id=1, source_target_pairs={{0,4},{1,5},{2,6},{3,7},{4,0},{5,1},{6,2},{7,3},{8,12},{9,13},{10,... | collective-permute-start | bytes 1658888 | tf_op jit(solution)/shard_map/ppermute | solution.py:28
  27.6 14.1 %collective-permute-start.6 = (bf16[290,128]{1,0:T(8,128)(2,1)S(1)}, bf16[290,128]{1,0:T(8,128)(2,1)S(1)}, u32[]{:S(2)}, u32[]{:S(2)}) collective-permute-start(bf16[290,128]{1,0:T(8,128)(2,1)S(1)} %collective-permute-done.4), channel_id=1, source_target_pairs={{0,1},{1,2},{2,3},{3,0},{4,5},{5,6},{6,7},{7,4},{8,9},{9,10},{10,1... | collective-permute-start | bytes 222728 | tf_op jit(solution)/shard_map/ppermute | solution.py:34
  42.6 16.2 %collective-permute-start.10 = (bf16[15,48,384]{2,1,0:T(8,128)(2,1)S(1)}, bf16[15,48,384]{2,1,0:T(8,128)(2,1)S(1)}, u32[]{:S(2)}, u32[]{:S(2)}) collective-permute-start(bf16[15,48,384]{2,1,0:T(8,128)(2,1)S(1)} %collective-permute-done.5.refs_11_), channel_id=1, source_target_pairs={{0,1},{1,2},{2,3},{3,0},{4,5},{5,6},{6,7},{7,4},{8,9},{9,10},{10,1... | collective-permute-start | bytes 1658888 | tf_op jit(solution)/shard_map/ppermute | solution.py:34
  42.7 19.4 %collective-permute-start.13 = (bf16[23,48,384]{2,1,0:T(8,128)(2,1)S(1)}, bf16[23,48,384]{2,1,0:T(8,128)(2,1)}, u32[]{:S(2)}, u32[]{:S(2)}) collective-permute-start(bf16[23,48,384]{2,1,0:T(8,128)(2,1)S(1)} %pad_maximum_fusion), channel_id=1, source_target_pairs={{0,16},{1,17},{2,18},{3,19},{4,20},{5,21},{6,22},{7,23},{8,24},{9,... | collective-permute-start | bytes 2543624 | tf_op jit(solution)/shard_map/ppermute | solution.py:28
  44.2 17.9 %collective-permute-start.12 = (bf16[22,48,384]{2,1,0:T(8,128)(2,1)S(1)}, bf16[22,48,384]{2,1,0:T(8,128)(2,1)S(1)}, u32[]{:S(2)}, u32[]{:S(2)}) collective-permute-start(bf16[22,48,384]{2,1,0:T(8,128)(2,1)S(1)} %pad_maximum_fusion.1), channel_id=1, source_target_pairs={{0,8},{1,9},{2,10},{3,11},{4,12},{5,13},{6,14},{7,15},{8,0},{9,1},... | collective-permute-start | bytes 2433032 | tf_op jit(solution)/shard_map/ppermute | solution.py:28
  45.8 13.0 %collective-permute-start.11 = (bf16[290,128]{1,0:T(8,128)(2,1)S(1)}, bf16[290,128]{1,0:T(8,128)(2,1)S(1)}, u32[]{:S(2)}, u32[]{:S(2)}) collective-permute-start(bf16[290,128]{1,0:T(8,128)(2,1)S(1)} %collective-permute-done.6), channel_id=1, source_target_pairs={{0,1},{1,2},{2,3},{3,0},{4,5},{5,6},{6,7},{7,4},{8,9},{9,10},{10,1... | collective-permute-start | bytes 222728 | tf_op jit(solution)/shard_map/ppermute | solution.py:34
  45.8 13.6 %collective-permute-start.14 = (bf16[15,48,384]{2,1,0:T(8,128)(2,1)S(1)}, bf16[15,48,384]{2,1,0:T(8,128)(2,1)S(1)}, u32[]{:S(2)}, u32[]{:S(2)}) collective-permute-start(bf16[15,48,384]{2,1,0:T(8,128)(2,1)S(1)} %collective-permute-done.7.refs_7_), channel_id=1, source_target_pairs={{0,4},{1,5},{2,6},{3,7},{4,0},{5,1},{6,2},{7,3},{8,12},{9,13},{10,... | collective-permute-start | bytes 1658888 | tf_op jit(solution)/shard_map/ppermute | solution.py:28
  58.8 2.7 %collective-permute-start.16 = (bf16[15,48,384]{2,1,0:T(8,128)(2,1)S(1)}, bf16[15,48,384]{2,1,0:T(8,128)(2,1)S(1)}, u32[]{:S(2)}, u32[]{:S(2)}) collective-permute-start(bf16[15,48,384]{2,1,0:T(8,128)(2,1)S(1)} %collective-permute-done.5.refs_11_), channel_id=1, source_target_pairs={{0,4},{1,5},{2,6},{3,7},{4,0},{5,1},{6,2},{7,3},{8,12},{9,13},{10,... | collective-permute-start | bytes 1658888 | tf_op jit(solution)/shard_map/ppermute | solution.py:28
  62.1 2.4 %collective-permute-start.21 = (bf16[22,48,384]{2,1,0:T(8,128)(2,1)S(1)}, bf16[22,48,384]{2,1,0:T(8,128)(2,1)S(1)}, u32[]{:S(2)}, u32[]{:S(2)}) collective-permute-start(bf16[22,48,384]{2,1,0:T(8,128)(2,1)S(1)} %collective-permute-done.12.refs_13_), channel_id=1, source_target_pairs={{0,4},{1,5},{2,6},{3,7},{4,0},{5,1},{6,2},{7,3},{8,12},{9,13},{10,... | collective-permute-start | bytes 2433032 | tf_op jit(solution)/shard_map/ppermute | solution.py:28
  65.4 4.8 %collective-permute-start.22 = (bf16[23,48,384]{2,1,0:T(8,128)(2,1)}, bf16[23,48,384]{2,1,0:T(8,128)(2,1)}, u32[]{:S(2)}, u32[]{:S(2)}) collective-permute-start(bf16[23,48,384]{2,1,0:T(8,128)(2,1)} %collective-permute-done.13.refs_15_), channel_id=1, source_target_pairs={{0,4},{1,5},{2,6},{3,7},{4,0},{5,1},{6,2},{7,3},{8,12},{9,13},{10,... | collective-permute-start | bytes 2543624 | tf_op jit(solution)/shard_map/ppermute | solution.py:28
  66.6 19.6 %collective-permute-start.18 = (bf16[15,48,384]{2,1,0:T(8,128)(2,1)}, bf16[15,48,384]{2,1,0:T(8,128)(2,1)}, u32[]{:S(2)}, u32[]{:S(2)}) collective-permute-start(bf16[15,48,384]{2,1,0:T(8,128)(2,1)} %copy-done.6), channel_id=1, source_target_pairs={{0,8},{1,9},{2,10},{3,11},{4,12},{5,13},{6,14},{7,15},{8,0},{9,1},... | collective-permute-start | bytes 1658888 | tf_op jit(solution)/shard_map/ppermute | solution.py:28
  68.1 18.8 %collective-permute-start.19 = (bf16[15,48,384]{2,1,0:T(8,128)(2,1)}, bf16[15,48,384]{2,1,0:T(8,128)(2,1)}, u32[]{:S(2)}, u32[]{:S(2)}) collective-permute-start(bf16[15,48,384]{2,1,0:T(8,128)(2,1)} %copy-done.6), channel_id=1, source_target_pairs={{0,16},{1,17},{2,18},{3,19},{4,20},{5,21},{6,22},{7,23},{8,24},{9,... | collective-permute-start | bytes 1658888 | tf_op jit(solution)/shard_map/ppermute | solution.py:28
  70.1 16.1 %collective-permute-start.17 = (bf16[15,48,384]{2,1,0:T(8,128)(2,1)S(1)}, bf16[15,48,384]{2,1,0:T(8,128)(2,1)S(1)}, u32[]{:S(2)}, u32[]{:S(2)}) collective-permute-start(bf16[15,48,384]{2,1,0:T(8,128)(2,1)S(1)} %pad_maximum_fusion.3), channel_id=1, source_target_pairs={{0,1},{1,2},{2,3},{3,0},{4,5},{5,6},{6,7},{7,4},{8,9},{9,10},{10,1... | collective-permute-start | bytes 1658888 | tf_op jit(solution)/shard_map/ppermute | solution.py:34
  70.2 16.7 %collective-permute-start.23 = (bf16[15,48,384]{2,1,0:T(8,128)(2,1)}, bf16[15,48,384]{2,1,0:T(8,128)(2,1)}, u32[]{:S(2)}, u32[]{:S(2)}) collective-permute-start(bf16[15,48,384]{2,1,0:T(8,128)(2,1)} %copy-done.6), channel_id=1, source_target_pairs={{0,4},{1,5},{2,6},{3,7},{4,0},{5,1},{6,2},{7,3},{8,12},{9,13},{10,... | collective-permute-start | bytes 1658888 | tf_op jit(solution)/shard_map/ppermute | solution.py:28
  70.6 15.5 %collective-permute-start.20 = (bf16[5,48,384]{2,1,0:T(8,128)(2,1)S(1)}, bf16[5,48,384]{2,1,0:T(8,128)(2,1)S(1)}, u32[]{:S(2)}, u32[]{:S(2)}) collective-permute-start(bf16[5,48,384]{2,1,0:T(8,128)(2,1)S(1)} %slice.104), channel_id=1, source_target_pairs={{0,24},{1,25},{2,26},{3,27},{4,28},{5,29},{6,30},{7,31},{8,16},{9,... | collective-permute-start | bytes 552968 | tf_op jit(solution)/shard_map/ppermute | solution.py:28
  86.9 4.7 %collective-permute-start.24 = (bf16[15,48,384]{2,1,0:T(8,128)(2,1)}, bf16[15,48,384]{2,1,0:T(8,128)(2,1)S(1)}, u32[]{:S(2)}, u32[]{:S(2)}) collective-permute-start(bf16[15,48,384]{2,1,0:T(8,128)(2,1)} %collective-permute-done.18.refs_19_), channel_id=1, source_target_pairs={{0,4},{1,5},{2,6},{3,7},{4,0},{5,1},{6,2},{7,3},{8,12},{9,13},{10,... | collective-permute-start | bytes 1658888 | tf_op jit(solution)/shard_map/ppermute | solution.py:28
  86.9 5.5 %collective-permute-start.25 = (bf16[15,48,384]{2,1,0:T(8,128)(2,1)}, bf16[15,48,384]{2,1,0:T(8,128)(2,1)S(1)}, u32[]{:S(2)}, u32[]{:S(2)}) collective-permute-start(bf16[15,48,384]{2,1,0:T(8,128)(2,1)} %collective-permute-done.19.refs_21_), channel_id=1, source_target_pairs={{0,4},{1,5},{2,6},{3,7},{4,0},{5,1},{6,2},{7,3},{8,12},{9,13},{10,... | collective-permute-start | bytes 1658888 | tf_op jit(solution)/shard_map/ppermute | solution.py:28
  87.5 5.0 %collective-permute-start.26 = (bf16[15,48,384]{2,1,0:T(8,128)(2,1)S(1)}, bf16[15,48,384]{2,1,0:T(8,128)(2,1)S(1)}, u32[]{:S(2)}, u32[]{:S(2)}) collective-permute-start(bf16[15,48,384]{2,1,0:T(8,128)(2,1)S(1)} %collective-permute-done.17.refs_23_), channel_id=1, source_target_pairs={{0,4},{1,5},{2,6},{3,7},{4,0},{5,1},{6,2},{7,3},{8,12},{9,13},{10,... | collective-permute-start | bytes 1658888 | tf_op jit(solution)/shard_map/ppermute | solution.py:28
  87.5 3.3 %collective-permute-start.27 = (bf16[5,48,384]{2,1,0:T(8,128)(2,1)S(1)}, bf16[5,48,384]{2,1,0:T(8,128)(2,1)S(1)}, u32[]{:S(2)}, u32[]{:S(2)}) collective-permute-start(bf16[5,48,384]{2,1,0:T(8,128)(2,1)S(1)} %collective-permute-done.20.refs_25_), channel_id=1, source_target_pairs={{0,4},{1,5},{2,6},{3,7},{4,0},{5,1},{6,2},{7,3},{8,12},{9,13},{10,... | collective-permute-start | bytes 552968 | tf_op jit(solution)/shard_map/ppermute | solution.py:28
  90.4 15.8 %collective-permute-start.32 = (bf16[4,48,384]{2,1,0:T(8,128)(2,1)S(1)}, bf16[4,48,384]{2,1,0:T(8,128)(2,1)S(1)}, u32[]{:S(2)}, u32[]{:S(2)}) collective-permute-start(bf16[4,48,384]{2,1,0:T(8,128)(2,1)S(1)} %slice.116), channel_id=1, source_target_pairs={{0,1},{1,2},{2,3},{3,0},{4,5},{5,6},{6,7},{7,4},{8,9},{9,10},{10,1... | collective-permute-start | bytes 442376 | tf_op jit(solution)/shard_map/ppermute | solution.py:34
  90.7 15.6 %collective-permute-start.30 = (bf16[3,48,384]{2,1,0:T(8,128)(2,1)S(1)}, bf16[3,48,384]{2,1,0:T(8,128)(2,1)S(1)}, u32[]{:S(2)}, u32[]{:S(2)}) collective-permute-start(bf16[3,48,384]{2,1,0:T(8,128)(2,1)S(1)} %slice.115), channel_id=1, source_target_pairs={{0,16},{1,17},{2,18},{3,19},{4,20},{5,21},{6,22},{7,23},{8,24},{9,... | collective-permute-start | bytes 331784 | tf_op jit(solution)/shard_map/ppermute | solution.py:28
  91.6 15.2 %collective-permute-start.28 = (bf16[3,48,384]{2,1,0:T(8,128)(2,1)S(1)}, bf16[3,48,384]{2,1,0:T(8,128)(2,1)S(1)}, u32[]{:S(2)}, u32[]{:S(2)}) collective-permute-start(bf16[3,48,384]{2,1,0:T(8,128)(2,1)S(1)} %slice.114), channel_id=1, source_target_pairs={{0,8},{1,9},{2,10},{3,11},{4,12},{5,13},{6,14},{7,15},{8,0},{9,1},... | collective-permute-start | bytes 331784 | tf_op jit(solution)/shard_map/ppermute | solution.py:28
  124.5 6.7 %collective-permute-start.34 = (bf16[4,48,128]{2,1,0:T(8,128)(2,1)}, bf16[4,48,128]{2,1,0:T(8,128)(2,1)S(1)}, u32[]{:S(2)}, u32[]{:S(2)}) collective-permute-start(bf16[4,48,128]{2,1,0:T(8,128)(2,1)} %get-tuple-element.78), channel_id=1, source_target_pairs={{0,1},{1,2},{2,3},{3,0},{4,5},{5,6},{6,7},{7,4},{8,9},{9,10},{10,1... | collective-permute-start | bytes 147464 | tf_op jit(solution)/shard_map/ppermute | solution.py:34
  125.4 6.3 %collective-permute-start.35 = (bf16[4,48,128]{2,1,0:T(8,128)(2,1)}, bf16[4,48,128]{2,1,0:T(8,128)(2,1)S(1)}, u32[]{:S(2)}, u32[]{:S(2)}) collective-permute-start(bf16[4,48,128]{2,1,0:T(8,128)(2,1)} %get-tuple-element.79), channel_id=1, source_target_pairs={{0,2},{1,3},{2,0},{3,1},{4,6},{5,7},{6,4},{7,5},{8,10},{9,11},{10,... | collective-permute-start | bytes 147464 | tf_op jit(solution)/shard_map/ppermute | solution.py:34
  128.6 4.7 %collective-permute-start.36 = (bf16[4,48,128]{2,1,0:T(8,128)(2,1)}, bf16[4,48,128]{2,1,0:T(8,128)(2,1)S(1)}, u32[]{:S(2)}, u32[]{:S(2)}) collective-permute-start(bf16[4,48,128]{2,1,0:T(8,128)(2,1)} %get-tuple-element.80), channel_id=1, source_target_pairs={{0,3},{1,0},{2,1},{3,2},{4,7},{5,4},{6,5},{7,6},{8,11},{9,8},{10,9... | collective-permute-start | bytes 147464 | tf_op jit(solution)/shard_map/ppermute | solution.py:34
  (37 other events, 256.6 us)

commit v5 on v4

--- a/solution.py
+++ b/solution.py
@@ -59,7 +59,7 @@
     return parts
 
 
-def spread(own, small, finish, early):
+def spread(own, small, finish, early, beside):
     units = own.shape[0]
     cut, third = units // 2, (units - early) // 3
     mid, end = early + third, early + 2 * third
@@ -76,7 +76,7 @@
     held_2, small_2 = shift(held_1), shift(small_1)
     near_1, far_1 = swap(held_1, NEAR), swap(held_1, FAR)
     twin = add(held_1, (0, 1, 0, units))
-    held_2, small_2, near_1, far_1, twin = settle((held_2, small_2, near_1, far_1, twin))
+    held_2, small_2, near_1, far_1, twin, beside = settle((held_2, small_2, near_1, far_1, twin, beside))
     held_3, small_3 = shift(held_2), shift(small_2)
     near_2 = swap(jnp.concatenate([held_2, far_1[:cut]], 0), NEAR)
     far_2 = swap(jnp.concatenate([held_2, near_1[cut:]], 0), FAR)
@@ -107,7 +107,7 @@
             add(settle((array, gate))[0], part)
         return pieces
 
-    return pieces, last, extra
+    return pieces, last, extra, beside
 
 
 def groups_of(low, high, per_early, per_late):
@@ -372,10 +372,10 @@
     rows = slab_rows + 2 * (HALO - 1)
     vmem = pl.BlockSpec(memory_space=pltpu.VMEM)
 
-    norms = [a.reshape(2 * layers, depth) for a in (norm_gain, norm_shift, res_bias)]
-    ends = jnp.zeros((2 * layers, depth), jnp.float32)
-    ends = ends.at[0].set(in_bias).at[1, : outs // chans].set(up_bias)
-    smalls = [*thirds(jnp.concatenate(norms + [ends], 1)), in_weight.reshape(-1, ch)]
+    ends = jnp.concatenate([in_bias, up_bias, jnp.zeros(2 * depth - in_bias.size - up_bias.size, jnp.float32)])
+    ends = jnp.pad(ends.reshape(1, 2, depth), ((0, layers - 1), (0, 0), (0, 0)))
+    norms = jnp.concatenate([norm_gain, norm_shift, res_bias, ends], 2).reshape(2 * layers, ch)
+    smalls = [*thirds(norms), in_weight.reshape(-1, ch)]
     smalls = jnp.concatenate(smalls, 0)
     n_small = smalls.shape[0]
     smalls = [smalls[:, at : at + tokens] for at in range(0, ch, tokens)]
@@ -414,18 +414,22 @@
     per_early = -(-2 * taps // 4)
     per_late = -(-(n_units - 4 * per_early) // 4)
     begin = 4 * per_early + 3 * per_late
-    tail = jnp.concatenate([res_units[begin:], up_units], 0)
-    tail = jnp.pad(tail, ((0, per_late - tail.shape[0]), (0, 0), (0, 0)))
     core, chip = place()
+    half = own_slice(up_weight, 0, taps, core)
+    odd = jnp.pad(half[1::2], ((0, taps % 2), (0, 0), (0, 0)))
+    tail = [own_slice(res_units, begin, res_units.shape[0] - begin, core), jnp.concatenate([half[0::2], odd], 2)]
+    tail.append(jnp.zeros((begin + per_late - n_units,) + tail[1].shape[1:], tail[1].dtype))
     mine = [
         own_slice(res_units, chip * per_early, per_early, core),
         jnp.where(
             chip == 3,
-            own_slice(tail, 0, per_late, core),
+            jnp.concatenate(tail, 0),
             own_slice(res_units, 4 * per_early + jnp.minimum(chip, 2) * per_late, per_late, core),
         ),
     ]
-    pieces, last_pieces, small = spread(jnp.concatenate(mine, 0), smalls, small_args, per_early)
+    pieces, last_pieces, small, up_units = spread(
+        jnp.concatenate(mine, 0), smalls, small_args, per_early, up_units
+    )
     params, up_b, stream = small
 
     def run(begin, end, rows, stream, pieces):

time: 136 us -> 134 us (0.985)
  waiting for transfers between devices: 56.8 us -> 52 us
  other arithmetic: 2.56 us -> 4.8 us
    ppermute x11, waiting for transfers between devices: 33.9 us -> 28.9 us  [shift(): return lax.ppermute(array, ('seq', 'chan'), pairs)]
    dynamic_slice x1 -> x3, local copies, waits for them, and re-layouts: 1.07 us -> 2.91 us  [own_slice(): lax.dynamic_slice(units, (first, core * rows, 0), (count, rows, units.sha...]
    concatenate x0 -> x2, other arithmetic: none -> 1.54 us  [the longest x1 0.8 us: body(): jnp.concatenate([norm_gain, norm_shift, res_bias, ends], 2)]
    unnamed x64 -> x48, local copies, waits for them, and re-layouts: 5.7 us -> 4.82 us
  transfers between devices with their start and end apart: 37 -> 37, of which waited for: 17 -> 15; matrix products, arithmetic and copies ran while one was open for 5% -> 8% of each run, Pallas kernels for 10% -> 11%
where the time goes in v5:
time: 134 us; the launch traced here: 133 us
  waiting for transfers between devices  52 us (39%)
  starting transfers between devices  30.2 us (23%)
  Pallas kernels  29 us (22%)
  local copies, waits for them, and re-layouts  16.8 us (13%)
  other arithmetic  4.8 us (4%)
    ppermute x11, waiting for transfers between devices, shift(): return lax.ppermute(array, ('seq', 'chan'), pairs)  28.9 us
    pallas_call x2, Pallas kernels, run(): pl.pallas_call(functools.partial(tile_kernel, (chans, layers, begin, end,...  27.1 us
    ppermute x26, waiting for transfers between devices, swap(): return lax.ppermute(array, ('seq', 'chan'), pairs)  23.1 us
    ppermute x26, starting transfers between devices, swap(): return lax.ppermute(array, ('seq', 'chan'), pairs)  17.2 us
    ppermute x11, starting transfers between devices, shift(): return lax.ppermute(array, ('seq', 'chan'), pairs)  13.1 us
    unnamed x48, local copies, waits for them, and re-layouts  4.82 us
    dynamic_slice x3, local copies, waits for them, and re-layouts, own_slice(): lax.dynamic_slice(units, (first, core * rows, 0), (count, rows, units.sha...  2.91 us
  transfers between devices with their start and end apart: 37, of which 15 were waited for; matrix products, arithmetic and copies ran while one was open for 8% of the time, Pallas kernels for 11%

profile of v5, /device:TPU:0, one launch (start us, length us, event | category | flops | bytes accessed | tf_op | source)
XLA Modules:
  0.0 133.4 jit_solution(9390308409398624005)
XLA Ops:
  0.0 1.0 constant_dynamic-slice_fusion.8
  3.1 1.2 maximum_select_fusion
  4.3 3.1 %collective-permute-start = (bf16[15,48,384]{2,1,0:T(8,128)(2,1)S(1)}, bf16[15,48,384]{2,1,0:T(8,128)(2,1)S(1)}, u32[]{:S(2)}, u32[]{:S(2)}) collective-permute-start(bf16[15,48,384]{2,1,0:T(8,128)(2,1)S(1)} %pad_maximum_fusion.2), channel_id=1, source_target_pairs={{0,1},{1,2},{2,3},{3,0},{4,5},{5,6},{6,7},{7,4},{8,9},{9,10},{10,1... | collective-permute-start | bytes 1658888 | tf_op jit(solution)/shard_map/ppermute | solution.py:34
  10.5 1.5 %collective-permute-start.2 = (bf16[2,16,128]{2,1,0:T(8,128)(2,1)S(1)}, bf16[2,16,128]{2,1,0:T(8,128)(2,1)S(1)}, u32[]{:S(2)}, u32[]{:S(2)}) collective-permute-start(bf16[2,16,128]{2,1,0:T(8,128)(2,1)S(1)} %pad_maximum_fusion.22), channel_id=1, source_target_pairs={{0,8},{1,9},{2,10},{3,11},{4,12},{5,13},{6,14},{7,15},{8,0},{9,1},... | collective-permute-start | bytes 24584 | tf_op jit(solution)/shard_map/ppermute | solution.py:28
  12.1 2.1 %collective-permute-done.2 = bf16[2,16,128]{2,1,0:T(8,128)(2,1)S(1)} collective-permute-done((bf16[2,16,128]{2,1,0:T(8,128)(2,1)S(1)}, bf16[2,16,128]{2,1,0:T(8,128)(2,1)S(1)}, u32[]{:S(2)}, u32[]{:S(2)}) %collective-permute-start.2) | collective-permute-done | bytes 8224 | tf_op jit(solution)/shard_map/ppermute | solution.py:28
  14.2 1.6 %collective-permute-start.3 = (bf16[4,16,128]{2,1,0:T(8,128)(2,1)S(1)}, bf16[4,16,128]{2,1,0:T(8,128)(2,1)S(1)}, u32[]{:S(2)}, u32[]{:S(2)}) collective-permute-start(bf16[4,16,128]{2,1,0:T(8,128)(2,1)S(1)} %pad_maximum_fusion.21), channel_id=1, source_target_pairs={{0,16},{1,17},{2,18},{3,19},{4,20},{5,21},{6,22},{7,23},{8,24},{9,... | collective-permute-start | bytes 49160 | tf_op jit(solution)/shard_map/ppermute | solution.py:28
  15.8 2.2 %collective-permute-done.3 = bf16[4,16,128]{2,1,0:T(8,128)(2,1)S(1)} collective-permute-done((bf16[4,16,128]{2,1,0:T(8,128)(2,1)S(1)}, bf16[4,16,128]{2,1,0:T(8,128)(2,1)S(1)}, u32[]{:S(2)}, u32[]{:S(2)}) %collective-permute-start.3) | collective-permute-done | bytes 16416 | tf_op jit(solution)/shard_map/ppermute | solution.py:28
  18.0 1.6 %collective-permute-start.4 = (bf16[290,128]{1,0:T(8,128)(2,1)S(1)}, bf16[290,128]{1,0:T(8,128)(2,1)S(1)}, u32[]{:S(2)}, u32[]{:S(2)}) collective-permute-start(bf16[290,128]{1,0:T(8,128)(2,1)S(1)} %get-tuple-element.68), channel_id=1, source_target_pairs={{0,1},{1,2},{2,3},{3,0},{4,5},{5,6},{6,7},{7,4},{8,9},{9,10},{10,1... | collective-permute-start | bytes 222728 | tf_op jit(solution)/shard_map/ppermute | solution.py:34
  19.7 4.6 %collective-permute-done.4 = bf16[290,128]{1,0:T(8,128)(2,1)S(1)} collective-permute-done((bf16[290,128]{1,0:T(8,128)(2,1)S(1)}, bf16[290,128]{1,0:T(8,128)(2,1)S(1)}, u32[]{:S(2)}, u32[]{:S(2)}) %collective-permute-start.4) | collective-permute-done | bytes 74272 | tf_op jit(solution)/shard_map/ppermute | solution.py:34
  24.3 1.6 %collective-permute-start.7 = (bf16[15,48,384]{2,1,0:T(8,128)(2,1)S(1)}, bf16[15,48,384]{2,1,0:T(8,128)(2,1)S(1)}, u32[]{:S(2)}, u32[]{:S(2)}) collective-permute-start(bf16[15,48,384]{2,1,0:T(8,128)(2,1)S(1)} %collective-permute-done.refs_5_), channel_id=1, source_target_pairs={{0,8},{1,9},{2,10},{3,11},{4,12},{5,13},{6,14},{7,15},{8,0},{9,1},... | collective-permute-start | bytes 1658888 | tf_op jit(solution)/shard_map/ppermute | solution.py:28
  25.8 1.5 %collective-permute-start.8 = (bf16[15,48,384]{2,1,0:T(8,128)(2,1)S(1)}, bf16[15,48,384]{2,1,0:T(8,128)(2,1)S(1)}, u32[]{:S(2)}, u32[]{:S(2)}) collective-permute-start(bf16[15,48,384]{2,1,0:T(8,128)(2,1)S(1)} %collective-permute-done.refs_5_), channel_id=1, source_target_pairs={{0,16},{1,17},{2,18},{3,19},{4,20},{5,21},{6,22},{7,23},{8,24},{9,... | collective-permute-start | bytes 1658888 | tf_op jit(solution)/shard_map/ppermute | solution.py:28
  27.4 1.3 collective-permute-start.6
  29.2 1.0 reshape.48.refs_4_
  30.2 10.3 %collective-permute-done.6 = bf16[290,128]{1,0:T(8,128)(2,1)S(1)} collective-permute-done((bf16[290,128]{1,0:T(8,128)(2,1)S(1)}, bf16[290,128]{1,0:T(8,128)(2,1)S(1)}, u32[]{:S(2)}, u32[]{:S(2)}) %collective-permute-start.6) | collective-permute-done | bytes 74272 | tf_op jit(solution)/shard_map/ppermute | solution.py:34
  40.8 1.6 %collective-permute-start.13 = (bf16[23,48,384]{2,1,0:T(8,128)(2,1)S(1)}, bf16[23,48,384]{2,1,0:T(8,128)(2,1)}, u32[]{:S(2)}, u32[]{:S(2)}) collective-permute-start(bf16[23,48,384]{2,1,0:T(8,128)(2,1)S(1)} %pad_maximum_fusion), channel_id=1, source_target_pairs={{0,16},{1,17},{2,18},{3,19},{4,20},{5,21},{6,22},{7,23},{8,24},{9,... | collective-permute-start | bytes 2543624 | tf_op jit(solution)/shard_map/ppermute | solution.py:28
  42.5 1.6 %collective-permute-start.12 = (bf16[22,48,384]{2,1,0:T(8,128)(2,1)S(1)}, bf16[22,48,384]{2,1,0:T(8,128)(2,1)S(1)}, u32[]{:S(2)}, u32[]{:S(2)}) collective-permute-start(bf16[22,48,384]{2,1,0:T(8,128)(2,1)S(1)} %pad_maximum_fusion.1), channel_id=1, source_target_pairs={{0,8},{1,9},{2,10},{3,11},{4,12},{5,13},{6,14},{7,15},{8,0},{9,1},... | collective-permute-start | bytes 2433032 | tf_op jit(solution)/shard_map/ppermute | solution.py:28
  44.1 11.9 %collective-permute-done.11 = bf16[290,128]{1,0:T(8,128)(2,1)S(1)} collective-permute-done((bf16[290,128]{1,0:T(8,128)(2,1)S(1)}, bf16[290,128]{1,0:T(8,128)(2,1)S(1)}, u32[]{:S(2)}, u32[]{:S(2)}) %collective-permute-start.11) | collective-permute-done | bytes 74272 | tf_op jit(solution)/shard_map/ppermute | solution.py:34
  56.5 1.4 %collective-permute-done.15.refs_10_ = bf16[15,48,384]{2,1,0:T(8,128)(2,1)S(1)} collective-permute-done((bf16[15,48,384]{2,1,0:T(8,128)(2,1)S(1)}, bf16[15,48,384]{2,1,0:T(8,128)(2,1)S(1)}, u32[]{:S(2)}, u32[]{:S(2)}) %collective-permute-start.15) | collective-permute-done | bytes 552992 | tf_op jit(solution)/shard_map/ppermute | solution.py:28
  58.7 1.0 collective-permute-done.12.refs_13_
  59.9 2.3 %collective-permute-done.21.refs_14_ = bf16[22,48,384]{2,1,0:T(8,128)(2,1)S(1)} collective-permute-done((bf16[22,48,384]{2,1,0:T(8,128)(2,1)S(1)}, bf16[22,48,384]{2,1,0:T(8,128)(2,1)S(1)}, u32[]{:S(2)}, u32[]{:S(2)}) %collective-permute-start.21) | collective-permute-done | bytes 811040 | tf_op jit(solution)/shard_map/ppermute | solution.py:28
  63.2 1.0 slice.74
  64.2 1.6 %collective-permute-start.18 = (bf16[15,48,384]{2,1,0:T(8,128)(2,1)S(1)}, bf16[15,48,384]{2,1,0:T(8,128)(2,1)}, u32[]{:S(2)}, u32[]{:S(2)}) collective-permute-start(bf16[15,48,384]{2,1,0:T(8,128)(2,1)S(1)} %collective-permute-done.10.refs_17_), channel_id=1, source_target_pairs={{0,8},{1,9},{2,10},{3,11},{4,12},{5,13},{6,14},{7,15},{8,0},{9,1},... | collective-permute-start | bytes 1658888 | tf_op jit(solution)/shard_map/ppermute | solution.py:28
  67.3 1.2 collective-permute-start.20
  69.5 1.9 %shard_map.91.refs_2_ = bf16[1280,384]{1,0:T(8,128)(2,1)S(1)} custom-call(f32[4,6,384]{2,1,0:T(8,128)S(1)} %copy.17.params, bf16[3,48,384]{2,1,0:T(8,128)(2,1)S(1)} %reshape.52.in_weight, bf16[32,16,128]{2,1,0:T(8,128)(2,1)S(1)} %bitcast.33), custom_call_target="tpu_custom_call" | custom-call | tf_op jit(solution)/shard_map/pallas_call | solution.py:395
  71.4 1.0 copy-done
  72.4 11.1 %collective-permute-done.20.refs_25_ = bf16[5,48,384]{2,1,0:T(8,128)(2,1)S(1)} collective-permute-done((bf16[5,48,384]{2,1,0:T(8,128)(2,1)S(1)}, bf16[5,48,384]{2,1,0:T(8,128)(2,1)S(1)}, u32[]{:S(2)}, u32[]{:S(2)}) %collective-permute-start.20) | collective-permute-done | bytes 184352 | tf_op jit(solution)/shard_map/ppermute | solution.py:28
  92.2 12.1 %shard_map.92.refs_2_ = bf16[960,384]{1,0:T(8,128)(2,1)} custom-call(f32[4,6,384]{2,1,0:T(8,128)} %copy.19.refs_0_, f32[1,192]{1,0:T(1,128)} %reshape_squeeze.3.refs_1_, bf16[1280,384]{1,0:T(8,128)(2,1)} %copy-done, bf16[54,96,384]{2,1,0:T(8,128)(2,1)} %bitcast.44, bf16[5,96,384]{2,1,0:T(8,128)(2,1)} %reshape.48.refs_4_, bf16[15,48,384]{2,1,0:T(8,128)(2,1)} %copy-done.9, ...), custom_call_target="tpu_custom_call" | custom-call | flops 11041505280 | bytes 5308416 | tf_op jit(solution)/shard_map/pallas_call | solution.py:447
  107.6 15.0 %shard_map.93 = (bf16[4,48,128]{2,1,0:T(8,128)(2,1)}, bf16[4,48,128]{2,1,0:T(8,128)(2,1)}, bf16[4,48,128]{2,1,0:T(8,128)(2,1)}, bf16[4,48,128]{2,1,0:T(8,128)(2,1)}) custom-call(f32[4,6,384]{2,1,0:T(8,128)} %copy.19.refs_0_, f32[1,192]{1,0:T(1,128)} %reshape_squeeze.3.refs_1_, bf16[960,384]{1,0:T(8,128)(2,1)} %shard_map.92.refs_2_, ...), custom_call_target="tpu_custom_call" | custom-call | flops 11890851840 | bytes 12386304 | tf_op jit(solution)/shard_map/pallas_call | solution.py:447
  122.6 1.2 collective-permute-start.34
  123.8 3.1 %collective-permute-start.35 = (bf16[4,48,128]{2,1,0:T(8,128)(2,1)}, bf16[4,48,128]{2,1,0:T(8,128)(2,1)S(1)}, u32[]{:S(2)}, u32[]{:S(2)}) collective-permute-start(bf16[4,48,128]{2,1,0:T(8,128)(2,1)} %get-tuple-element.57), channel_id=1, source_target_pairs={{0,2},{1,3},{2,0},{3,1},{4,6},{5,7},{6,4},{7,5},{8,10},{9,11},{10,... | collective-permute-start | bytes 147464 | tf_op jit(solution)/shard_map/ppermute | solution.py:34
  126.9 2.6 %collective-permute-start.36 = (bf16[4,48,128]{2,1,0:T(8,128)(2,1)}, bf16[4,48,128]{2,1,0:T(8,128)(2,1)S(1)}, u32[]{:S(2)}, u32[]{:S(2)}) collective-permute-start(bf16[4,48,128]{2,1,0:T(8,128)(2,1)} %get-tuple-element.58), channel_id=1, source_target_pairs={{0,3},{1,0},{2,1},{3,2},{4,7},{5,4},{6,5},{7,6},{8,11},{9,8},{10,9... | collective-permute-start | bytes 147464 | tf_op jit(solution)/shard_map/ppermute | solution.py:34
  129.8 1.8 %collective-permute-done.36 = bf16[4,48,128]{2,1,0:T(8,128)(2,1)S(1)} collective-permute-done((bf16[4,48,128]{2,1,0:T(8,128)(2,1)}, bf16[4,48,128]{2,1,0:T(8,128)(2,1)S(1)}, u32[]{:S(2)}, u32[]{:S(2)}) %collective-permute-start.36) | collective-permute-done | bytes 49184 | tf_op jit(solution)/shard_map/ppermute | solution.py:34
  (150 shorter events, 24.9 us)
Async XLA Ops:
  4.3 20.0 %collective-permute-start = (bf16[15,48,384]{2,1,0:T(8,128)(2,1)S(1)}, bf16[15,48,384]{2,1,0:T(8,128)(2,1)S(1)}, u32[]{:S(2)}, u32[]{:S(2)}) collective-permute-start(bf16[15,48,384]{2,1,0:T(8,128)(2,1)S(1)} %pad_maximum_fusion.2), channel_id=1, source_target_pairs={{0,1},{1,2},{2,3},{3,0},{4,5},{5,6},{6,7},{7,4},{8,9},{9,10},{10,1... | collective-permute-start | bytes 1658888 | tf_op jit(solution)/shard_map/ppermute | solution.py:34
  7.4 2.5 %collective-permute-start.1 = (bf16[1,16,128]{2,1,0:T(8,128)(2,1)}, bf16[1,16,128]{2,1,0:T(8,128)(2,1)S(1)}, u32[]{:S(2)}, u32[]{:S(2)}) collective-permute-start(bf16[1,16,128]{2,1,0:T(8,128)(2,1)} %bitcast.53), channel_id=1, source_target_pairs={{0,4},{1,5},{2,6},{3,7},{4,0},{5,1},{6,2},{7,3},{8,12},{9,13},{10,... | collective-permute-start | bytes 12296 | tf_op jit(solution)/shard_map/ppermute | solution.py:28
  10.5 3.7 %collective-permute-start.2 = (bf16[2,16,128]{2,1,0:T(8,128)(2,1)S(1)}, bf16[2,16,128]{2,1,0:T(8,128)(2,1)S(1)}, u32[]{:S(2)}, u32[]{:S(2)}) collective-permute-start(bf16[2,16,128]{2,1,0:T(8,128)(2,1)S(1)} %pad_maximum_fusion.22), channel_id=1, source_target_pairs={{0,8},{1,9},{2,10},{3,11},{4,12},{5,13},{6,14},{7,15},{8,0},{9,1},... | collective-permute-start | bytes 24584 | tf_op jit(solution)/shard_map/ppermute | solution.py:28
  14.2 3.8 %collective-permute-start.3 = (bf16[4,16,128]{2,1,0:T(8,128)(2,1)S(1)}, bf16[4,16,128]{2,1,0:T(8,128)(2,1)S(1)}, u32[]{:S(2)}, u32[]{:S(2)}) collective-permute-start(bf16[4,16,128]{2,1,0:T(8,128)(2,1)S(1)} %pad_maximum_fusion.21), channel_id=1, source_target_pairs={{0,16},{1,17},{2,18},{3,19},{4,20},{5,21},{6,22},{7,23},{8,24},{9,... | collective-permute-start | bytes 49160 | tf_op jit(solution)/shard_map/ppermute | solution.py:28
  18.0 6.2 %collective-permute-start.4 = (bf16[290,128]{1,0:T(8,128)(2,1)S(1)}, bf16[290,128]{1,0:T(8,128)(2,1)S(1)}, u32[]{:S(2)}, u32[]{:S(2)}) collective-permute-start(bf16[290,128]{1,0:T(8,128)(2,1)S(1)} %get-tuple-element.68), channel_id=1, source_target_pairs={{0,1},{1,2},{2,3},{3,0},{4,5},{5,6},{6,7},{7,4},{8,9},{9,10},{10,1... | collective-permute-start | bytes 222728 | tf_op jit(solution)/shard_map/ppermute | solution.py:34
  24.3 16.3 %collective-permute-start.5 = (bf16[15,48,384]{2,1,0:T(8,128)(2,1)S(1)}, bf16[15,48,384]{2,1,0:T(8,128)(2,1)S(1)}, u32[]{:S(2)}, u32[]{:S(2)}) collective-permute-start(bf16[15,48,384]{2,1,0:T(8,128)(2,1)S(1)} %collective-permute-done.refs_5_), channel_id=1, source_target_pairs={{0,1},{1,2},{2,3},{3,0},{4,5},{5,6},{6,7},{7,4},{8,9},{9,10},{10,1... | collective-permute-start | bytes 1658888 | tf_op jit(solution)/shard_map/ppermute | solution.py:34
  24.3 16.3 %collective-permute-start.7 = (bf16[15,48,384]{2,1,0:T(8,128)(2,1)S(1)}, bf16[15,48,384]{2,1,0:T(8,128)(2,1)S(1)}, u32[]{:S(2)}, u32[]{:S(2)}) collective-permute-start(bf16[15,48,384]{2,1,0:T(8,128)(2,1)S(1)} %collective-permute-done.refs_5_), channel_id=1, source_target_pairs={{0,8},{1,9},{2,10},{3,11},{4,12},{5,13},{6,14},{7,15},{8,0},{9,1},... | collective-permute-start | bytes 1658888 | tf_op jit(solution)/shard_map/ppermute | solution.py:28
  25.8 14.7 %collective-permute-start.8 = (bf16[15,48,384]{2,1,0:T(8,128)(2,1)S(1)}, bf16[15,48,384]{2,1,0:T(8,128)(2,1)S(1)}, u32[]{:S(2)}, u32[]{:S(2)}) collective-permute-start(bf16[15,48,384]{2,1,0:T(8,128)(2,1)S(1)} %collective-permute-done.refs_5_), channel_id=1, source_target_pairs={{0,16},{1,17},{2,18},{3,19},{4,20},{5,21},{6,22},{7,23},{8,24},{9,... | collective-permute-start | bytes 1658888 | tf_op jit(solution)/shard_map/ppermute | solution.py:28
  27.4 13.2 %collective-permute-start.9 = (bf16[15,48,384]{2,1,0:T(8,128)(2,1)S(1)}, bf16[15,48,384]{2,1,0:T(8,128)(2,1)}, u32[]{:S(2)}, u32[]{:S(2)}) collective-permute-start(bf16[15,48,384]{2,1,0:T(8,128)(2,1)S(1)} %collective-permute-done.refs_5_), channel_id=1, source_target_pairs={{0,4},{1,5},{2,6},{3,7},{4,0},{5,1},{6,2},{7,3},{8,12},{9,13},{10,... | collective-permute-start | bytes 1658888 | tf_op jit(solution)/shard_map/ppermute | solution.py:28
  27.4 13.2 %collective-permute-start.6 = (bf16[290,128]{1,0:T(8,128)(2,1)S(1)}, bf16[290,128]{1,0:T(8,128)(2,1)S(1)}, u32[]{:S(2)}, u32[]{:S(2)}) collective-permute-start(bf16[290,128]{1,0:T(8,128)(2,1)S(1)} %collective-permute-done.4), channel_id=1, source_target_pairs={{0,1},{1,2},{2,3},{3,0},{4,5},{5,6},{6,7},{7,4},{8,9},{9,10},{10,1... | collective-permute-start | bytes 222728 | tf_op jit(solution)/shard_map/ppermute | solution.py:34
  40.6 15.4 %collective-permute-start.10 = (bf16[15,48,384]{2,1,0:T(8,128)(2,1)S(1)}, bf16[15,48,384]{2,1,0:T(8,128)(2,1)S(1)}, u32[]{:S(2)}, u32[]{:S(2)}) collective-permute-start(bf16[15,48,384]{2,1,0:T(8,128)(2,1)S(1)} %collective-permute-done.5.refs_11_), channel_id=1, source_target_pairs={{0,1},{1,2},{2,3},{3,0},{4,5},{5,6},{6,7},{7,4},{8,9},{9,10},{10,1... | collective-permute-start | bytes 1658888 | tf_op jit(solution)/shard_map/ppermute | solution.py:34
  40.8 19.0 %collective-permute-start.13 = (bf16[23,48,384]{2,1,0:T(8,128)(2,1)S(1)}, bf16[23,48,384]{2,1,0:T(8,128)(2,1)}, u32[]{:S(2)}, u32[]{:S(2)}) collective-permute-start(bf16[23,48,384]{2,1,0:T(8,128)(2,1)S(1)} %pad_maximum_fusion), channel_id=1, source_target_pairs={{0,16},{1,17},{2,18},{3,19},{4,20},{5,21},{6,22},{7,23},{8,24},{9,... | collective-permute-start | bytes 2543624 | tf_op jit(solution)/shard_map/ppermute | solution.py:28
  42.5 17.2 %collective-permute-start.12 = (bf16[22,48,384]{2,1,0:T(8,128)(2,1)S(1)}, bf16[22,48,384]{2,1,0:T(8,128)(2,1)S(1)}, u32[]{:S(2)}, u32[]{:S(2)}) collective-permute-start(bf16[22,48,384]{2,1,0:T(8,128)(2,1)S(1)} %pad_maximum_fusion.1), channel_id=1, source_target_pairs={{0,8},{1,9},{2,10},{3,11},{4,12},{5,13},{6,14},{7,15},{8,0},{9,1},... | collective-permute-start | bytes 2433032 | tf_op jit(solution)/shard_map/ppermute | solution.py:28
  44.1 11.9 %collective-permute-start.11 = (bf16[290,128]{1,0:T(8,128)(2,1)S(1)}, bf16[290,128]{1,0:T(8,128)(2,1)S(1)}, u32[]{:S(2)}, u32[]{:S(2)}) collective-permute-start(bf16[290,128]{1,0:T(8,128)(2,1)S(1)} %collective-permute-done.6), channel_id=1, source_target_pairs={{0,1},{1,2},{2,3},{3,0},{4,5},{5,6},{6,7},{7,4},{8,9},{9,10},{10,1... | collective-permute-start | bytes 222728 | tf_op jit(solution)/shard_map/ppermute | solution.py:34
  44.1 12.4 %collective-permute-start.14 = (bf16[15,48,384]{2,1,0:T(8,128)(2,1)S(1)}, bf16[15,48,384]{2,1,0:T(8,128)(2,1)S(1)}, u32[]{:S(2)}, u32[]{:S(2)}) collective-permute-start(bf16[15,48,384]{2,1,0:T(8,128)(2,1)S(1)} %collective-permute-done.7.refs_7_), channel_id=1, source_target_pairs={{0,4},{1,5},{2,6},{3,7},{4,0},{5,1},{6,2},{7,3},{8,12},{9,13},{10,... | collective-permute-start | bytes 1658888 | tf_op jit(solution)/shard_map/ppermute | solution.py:28
  56.0 2.7 %collective-permute-start.16 = (bf16[15,48,384]{2,1,0:T(8,128)(2,1)S(1)}, bf16[15,48,384]{2,1,0:T(8,128)(2,1)S(1)}, u32[]{:S(2)}, u32[]{:S(2)}) collective-permute-start(bf16[15,48,384]{2,1,0:T(8,128)(2,1)S(1)} %collective-permute-done.5.refs_11_), channel_id=1, source_target_pairs={{0,4},{1,5},{2,6},{3,7},{4,0},{5,1},{6,2},{7,3},{8,12},{9,13},{10,... | collective-permute-start | bytes 1658888 | tf_op jit(solution)/shard_map/ppermute | solution.py:28
  63.0 3.9 %collective-permute-start.22 = (bf16[23,48,384]{2,1,0:T(8,128)(2,1)}, bf16[23,48,384]{2,1,0:T(8,128)(2,1)}, u32[]{:S(2)}, u32[]{:S(2)}) collective-permute-start(bf16[23,48,384]{2,1,0:T(8,128)(2,1)} %collective-permute-done.13.refs_15_), channel_id=1, source_target_pairs={{0,4},{1,5},{2,6},{3,7},{4,0},{5,1},{6,2},{7,3},{8,12},{9,13},{10,... | collective-permute-start | bytes 2543624 | tf_op jit(solution)/shard_map/ppermute | solution.py:28
  64.2 19.3 %collective-permute-start.18 = (bf16[15,48,384]{2,1,0:T(8,128)(2,1)S(1)}, bf16[15,48,384]{2,1,0:T(8,128)(2,1)}, u32[]{:S(2)}, u32[]{:S(2)}) collective-permute-start(bf16[15,48,384]{2,1,0:T(8,128)(2,1)S(1)} %collective-permute-done.10.refs_17_), channel_id=1, source_target_pairs={{0,8},{1,9},{2,10},{3,11},{4,12},{5,13},{6,14},{7,15},{8,0},{9,1},... | collective-permute-start | bytes 1658888 | tf_op jit(solution)/shard_map/ppermute | solution.py:28
  65.8 18.6 %collective-permute-start.19 = (bf16[15,48,384]{2,1,0:T(8,128)(2,1)S(1)}, bf16[15,48,384]{2,1,0:T(8,128)(2,1)}, u32[]{:S(2)}, u32[]{:S(2)}) collective-permute-start(bf16[15,48,384]{2,1,0:T(8,128)(2,1)S(1)} %collective-permute-done.10.refs_17_), channel_id=1, source_target_pairs={{0,16},{1,17},{2,18},{3,19},{4,20},{5,21},{6,22},{7,23},{8,24},{9,... | collective-permute-start | bytes 1658888 | tf_op jit(solution)/shard_map/ppermute | solution.py:28
  66.8 16.7 %collective-permute-start.17 = (bf16[15,48,384]{2,1,0:T(8,128)(2,1)S(1)}, bf16[15,48,384]{2,1,0:T(8,128)(2,1)}, u32[]{:S(2)}, u32[]{:S(2)}) collective-permute-start(bf16[15,48,384]{2,1,0:T(8,128)(2,1)S(1)} %pad_maximum_fusion.3), channel_id=1, source_target_pairs={{0,1},{1,2},{2,3},{3,0},{4,5},{5,6},{6,7},{7,4},{8,9},{9,10},{10,1... | collective-permute-start | bytes 1658888 | tf_op jit(solution)/shard_map/ppermute | solution.py:34
  66.9 17.5 %collective-permute-start.23 = (bf16[15,48,384]{2,1,0:T(8,128)(2,1)S(1)}, bf16[15,48,384]{2,1,0:T(8,128)(2,1)}, u32[]{:S(2)}, u32[]{:S(2)}) collective-permute-start(bf16[15,48,384]{2,1,0:T(8,128)(2,1)S(1)} %collective-permute-done.10.refs_17_), channel_id=1, source_target_pairs={{0,4},{1,5},{2,6},{3,7},{4,0},{5,1},{6,2},{7,3},{8,12},{9,13},{10,... | collective-permute-start | bytes 1658888 | tf_op jit(solution)/shard_map/ppermute | solution.py:28
  67.3 16.2 %collective-permute-start.20 = (bf16[5,48,384]{2,1,0:T(8,128)(2,1)S(1)}, bf16[5,48,384]{2,1,0:T(8,128)(2,1)S(1)}, u32[]{:S(2)}, u32[]{:S(2)}) collective-permute-start(bf16[5,48,384]{2,1,0:T(8,128)(2,1)S(1)} %slice.75), channel_id=1, source_target_pairs={{0,24},{1,25},{2,26},{3,27},{4,28},{5,29},{6,30},{7,31},{8,16},{9,... | collective-permute-start | bytes 552968 | tf_op jit(solution)/shard_map/ppermute | solution.py:28
  84.4 5.4 %collective-permute-start.24 = (bf16[15,48,384]{2,1,0:T(8,128)(2,1)}, bf16[15,48,384]{2,1,0:T(8,128)(2,1)S(1)}, u32[]{:S(2)}, u32[]{:S(2)}) collective-permute-start(bf16[15,48,384]{2,1,0:T(8,128)(2,1)} %collective-permute-done.18.refs_19_), channel_id=1, source_target_pairs={{0,4},{1,5},{2,6},{3,7},{4,0},{5,1},{6,2},{7,3},{8,12},{9,13},{10,... | collective-permute-start | bytes 1658888 | tf_op jit(solution)/shard_map/ppermute | solution.py:28
  84.4 6.2 %collective-permute-start.25 = (bf16[15,48,384]{2,1,0:T(8,128)(2,1)}, bf16[15,48,384]{2,1,0:T(8,128)(2,1)S(1)}, u32[]{:S(2)}, u32[]{:S(2)}) collective-permute-start(bf16[15,48,384]{2,1,0:T(8,128)(2,1)} %collective-permute-done.19.refs_21_), channel_id=1, source_target_pairs={{0,4},{1,5},{2,6},{3,7},{4,0},{5,1},{6,2},{7,3},{8,12},{9,13},{10,... | collective-permute-start | bytes 1658888 | tf_op jit(solution)/shard_map/ppermute | solution.py:28
  84.9 5.7 %collective-permute-start.26 = (bf16[15,48,384]{2,1,0:T(8,128)(2,1)}, bf16[15,48,384]{2,1,0:T(8,128)(2,1)S(1)}, u32[]{:S(2)}, u32[]{:S(2)}) collective-permute-start(bf16[15,48,384]{2,1,0:T(8,128)(2,1)} %collective-permute-done.17.refs_23_), channel_id=1, source_target_pairs={{0,4},{1,5},{2,6},{3,7},{4,0},{5,1},{6,2},{7,3},{8,12},{9,13},{10,... | collective-permute-start | bytes 1658888 | tf_op jit(solution)/shard_map/ppermute | solution.py:28
  84.9 3.9 %collective-permute-start.27 = (bf16[5,48,384]{2,1,0:T(8,128)(2,1)S(1)}, bf16[5,48,384]{2,1,0:T(8,128)(2,1)S(1)}, u32[]{:S(2)}, u32[]{:S(2)}) collective-permute-start(bf16[5,48,384]{2,1,0:T(8,128)(2,1)S(1)} %collective-permute-done.20.refs_25_), channel_id=1, source_target_pairs={{0,4},{1,5},{2,6},{3,7},{4,0},{5,1},{6,2},{7,3},{8,12},{9,13},{10,... | collective-permute-start | bytes 552968 | tf_op jit(solution)/shard_map/ppermute | solution.py:28
  88.8 15.6 %collective-permute-start.32 = (bf16[4,48,384]{2,1,0:T(8,128)(2,1)S(1)}, bf16[4,48,384]{2,1,0:T(8,128)(2,1)S(1)}, u32[]{:S(2)}, u32[]{:S(2)}) collective-permute-start(bf16[4,48,384]{2,1,0:T(8,128)(2,1)S(1)} %slice.87), channel_id=1, source_target_pairs={{0,1},{1,2},{2,3},{3,0},{4,5},{5,6},{6,7},{7,4},{8,9},{9,10},{10,1... | collective-permute-start | bytes 442376 | tf_op jit(solution)/shard_map/ppermute | solution.py:34
  88.8 15.7 %collective-permute-start.30 = (bf16[3,48,384]{2,1,0:T(8,128)(2,1)S(1)}, bf16[3,48,384]{2,1,0:T(8,128)(2,1)S(1)}, u32[]{:S(2)}, u32[]{:S(2)}) collective-permute-start(bf16[3,48,384]{2,1,0:T(8,128)(2,1)S(1)} %slice.86), channel_id=1, source_target_pairs={{0,16},{1,17},{2,18},{3,19},{4,20},{5,21},{6,22},{7,23},{8,24},{9,... | collective-permute-start | bytes 331784 | tf_op jit(solution)/shard_map/ppermute | solution.py:28
  89.7 15.2 %collective-permute-start.28 = (bf16[3,48,384]{2,1,0:T(8,128)(2,1)S(1)}, bf16[3,48,384]{2,1,0:T(8,128)(2,1)S(1)}, u32[]{:S(2)}, u32[]{:S(2)}) collective-permute-start(bf16[3,48,384]{2,1,0:T(8,128)(2,1)S(1)} %slice.85), channel_id=1, source_target_pairs={{0,8},{1,9},{2,10},{3,11},{4,12},{5,13},{6,14},{7,15},{8,0},{9,1},... | collective-permute-start | bytes 331784 | tf_op jit(solution)/shard_map/ppermute | solution.py:28
  122.6 6.9 %collective-permute-start.34 = (bf16[4,48,128]{2,1,0:T(8,128)(2,1)}, bf16[4,48,128]{2,1,0:T(8,128)(2,1)S(1)}, u32[]{:S(2)}, u32[]{:S(2)}) collective-permute-start(bf16[4,48,128]{2,1,0:T(8,128)(2,1)} %get-tuple-element.56), channel_id=1, source_target_pairs={{0,1},{1,2},{2,3},{3,0},{4,5},{5,6},{6,7},{7,4},{8,9},{9,10},{10,1... | collective-permute-start | bytes 147464 | tf_op jit(solution)/shard_map/ppermute | solution.py:34
  123.8 6.0 %collective-permute-start.35 = (bf16[4,48,128]{2,1,0:T(8,128)(2,1)}, bf16[4,48,128]{2,1,0:T(8,128)(2,1)S(1)}, u32[]{:S(2)}, u32[]{:S(2)}) collective-permute-start(bf16[4,48,128]{2,1,0:T(8,128)(2,1)} %get-tuple-element.57), channel_id=1, source_target_pairs={{0,2},{1,3},{2,0},{3,1},{4,6},{5,7},{6,4},{7,5},{8,10},{9,11},{10,... | collective-permute-start | bytes 147464 | tf_op jit(solution)/shard_map/ppermute | solution.py:34
  126.9 4.7 %collective-permute-start.36 = (bf16[4,48,128]{2,1,0:T(8,128)(2,1)}, bf16[4,48,128]{2,1,0:T(8,128)(2,1)S(1)}, u32[]{:S(2)}, u32[]{:S(2)}) collective-permute-start(bf16[4,48,128]{2,1,0:T(8,128)(2,1)} %get-tuple-element.58), channel_id=1, source_target_pairs={{0,3},{1,0},{2,1},{3,2},{4,7},{5,4},{6,5},{7,6},{8,11},{9,8},{10,9... | collective-permute-start | bytes 147464 | tf_op jit(solution)/shard_map/ppermute | solution.py:34
  (29 other events, 217.2 us)

commit v6 on v5

--- a/solution.py
+++ b/solution.py
@@ -282,7 +282,7 @@
     pieces = refs[5 : 5 + len(metas)]
     n_outs = chans if upsamples else 1
     outs = refs[5 + len(metas) : 5 + len(metas) + n_outs]
-    weights, held, cols_a, cols_b, last, woven, sems = refs[5 + len(metas) + n_outs :]
+    weights, held, cols_a, cols_b, last, woven, shares, sems = refs[5 + len(metas) + n_outs :]
     gain, shift_by, bias = 0.5 * params[0], 0.5 * params[1], params[2]
     tile_cols = LAT_W // chans
     n_res = res_ref.shape[0]
@@ -351,11 +351,9 @@
             turned = jnp.concatenate([woven[tile].T for tile in range(woven.shape[0])], 0)
             for owner in range(chans):
                 part = turned[owner * share : (owner + 1) * share].astype(jnp.bfloat16)
-                for step in range(chans):
-
-                    @pl.when(lax.rem(chan + step, chans) == owner)
-                    def _():
-                        outs[step][2 * row + low] = part
+                shares[owner, 2 * row + low] = part
+    for step in range(chans):
+        outs[step][...] = shares[lax.rem(chan + step, chans)]
 
 
 def body(
@@ -458,6 +456,7 @@
                 pltpu.VMEM((rows * width, 3 * ch), jnp.bfloat16),
                 pltpu.VMEM(((slab_rows + 2) * width, ch), jnp.bfloat16),
                 pltpu.VMEM((-(-outs // 128), 2 * tile_cols, 128), jnp.float32),
+                pltpu.VMEM((chans, 2 * slab_rows, outs // chans, 2 * tile_cols), jnp.bfloat16),
                 pltpu.SemaphoreType.DMA((len(groups), 2 * chans - 1)),
             ],
             compiler_params=pltpu.CompilerParams(vmem_limit_bytes=VMEM_BYTES),

time: 134 us -> 134 us (level)
  no operation moved by 1% of the time
where the time goes in v6:
time: 134 us; the launch traced here: 133 us
  waiting for transfers between devices  52 us (39%)
  starting transfers between devices  30.3 us (23%)
  Pallas kernels  28.5 us (21%)
  local copies, waits for them, and re-layouts  16.8 us (13%)
  other arithmetic  4.8 us (4%)
    ppermute x11, waiting for transfers between devices, shift(): return lax.ppermute(array, ('seq', 'chan'), pairs)  28.9 us
    pallas_call x2, Pallas kernels, run(): pl.pallas_call(functools.partial(tile_kernel, (chans, layers, begin, end,...  26.6 us
    ppermute x26, waiting for transfers between devices, swap(): return lax.ppermute(array, ('seq', 'chan'), pairs)  23.1 us
    ppermute x26, starting transfers between devices, swap(): return lax.ppermute(array, ('seq', 'chan'), pairs)  17.2 us
    ppermute x11, starting transfers between devices, shift(): return lax.ppermute(array, ('seq', 'chan'), pairs)  13.1 us
    unnamed x48, local copies, waits for them, and re-layouts  4.82 us
    dynamic_slice x3, local copies, waits for them, and re-layouts, own_slice(): lax.dynamic_slice(units, (first, core * rows, 0), (count, rows, units.sha...  2.91 us
  transfers between devices with their start and end apart: 37, of which 15 were waited for; matrix products, arithmetic and copies ran while one was open for 8% of the time, Pallas kernels for 11%

profile of v6, /device:TPU:0, one launch (start us, length us, event | category | flops | bytes accessed | tf_op | source)
XLA Modules:
  0.0 132.9 jit_solution(5932896593197880218)
XLA Ops:
  0.0 1.0 constant_dynamic-slice_fusion.8
  3.1 1.2 maximum_select_fusion
  4.3 3.1 %collective-permute-start = (bf16[15,48,384]{2,1,0:T(8,128)(2,1)S(1)}, bf16[15,48,384]{2,1,0:T(8,128)(2,1)S(1)}, u32[]{:S(2)}, u32[]{:S(2)}) collective-permute-start(bf16[15,48,384]{2,1,0:T(8,128)(2,1)S(1)} %pad_maximum_fusion.2), channel_id=1, source_target_pairs={{0,1},{1,2},{2,3},{3,0},{4,5},{5,6},{6,7},{7,4},{8,9},{9,10},{10,1... | collective-permute-start | bytes 1658888 | tf_op jit(solution)/shard_map/ppermute | solution.py:34
  10.5 1.5 %collective-permute-start.2 = (bf16[2,16,128]{2,1,0:T(8,128)(2,1)S(1)}, bf16[2,16,128]{2,1,0:T(8,128)(2,1)S(1)}, u32[]{:S(2)}, u32[]{:S(2)}) collective-permute-start(bf16[2,16,128]{2,1,0:T(8,128)(2,1)S(1)} %pad_maximum_fusion.22), channel_id=1, source_target_pairs={{0,8},{1,9},{2,10},{3,11},{4,12},{5,13},{6,14},{7,15},{8,0},{9,1},... | collective-permute-start | bytes 24584 | tf_op jit(solution)/shard_map/ppermute | solution.py:28
  12.1 2.1 %collective-permute-done.2 = bf16[2,16,128]{2,1,0:T(8,128)(2,1)S(1)} collective-permute-done((bf16[2,16,128]{2,1,0:T(8,128)(2,1)S(1)}, bf16[2,16,128]{2,1,0:T(8,128)(2,1)S(1)}, u32[]{:S(2)}, u32[]{:S(2)}) %collective-permute-start.2) | collective-permute-done | bytes 8224 | tf_op jit(solution)/shard_map/ppermute | solution.py:28
  14.2 1.6 %collective-permute-start.3 = (bf16[4,16,128]{2,1,0:T(8,128)(2,1)S(1)}, bf16[4,16,128]{2,1,0:T(8,128)(2,1)S(1)}, u32[]{:S(2)}, u32[]{:S(2)}) collective-permute-start(bf16[4,16,128]{2,1,0:T(8,128)(2,1)S(1)} %pad_maximum_fusion.21), channel_id=1, source_target_pairs={{0,16},{1,17},{2,18},{3,19},{4,20},{5,21},{6,22},{7,23},{8,24},{9,... | collective-permute-start | bytes 49160 | tf_op jit(solution)/shard_map/ppermute | solution.py:28
  15.8 2.2 %collective-permute-done.3 = bf16[4,16,128]{2,1,0:T(8,128)(2,1)S(1)} collective-permute-done((bf16[4,16,128]{2,1,0:T(8,128)(2,1)S(1)}, bf16[4,16,128]{2,1,0:T(8,128)(2,1)S(1)}, u32[]{:S(2)}, u32[]{:S(2)}) %collective-permute-start.3) | collective-permute-done | bytes 16416 | tf_op jit(solution)/shard_map/ppermute | solution.py:28
  18.0 1.6 %collective-permute-start.4 = (bf16[290,128]{1,0:T(8,128)(2,1)S(1)}, bf16[290,128]{1,0:T(8,128)(2,1)S(1)}, u32[]{:S(2)}, u32[]{:S(2)}) collective-permute-start(bf16[290,128]{1,0:T(8,128)(2,1)S(1)} %get-tuple-element.68), channel_id=1, source_target_pairs={{0,1},{1,2},{2,3},{3,0},{4,5},{5,6},{6,7},{7,4},{8,9},{9,10},{10,1... | collective-permute-start | bytes 222728 | tf_op jit(solution)/shard_map/ppermute | solution.py:34
  19.7 4.6 %collective-permute-done.4 = bf16[290,128]{1,0:T(8,128)(2,1)S(1)} collective-permute-done((bf16[290,128]{1,0:T(8,128)(2,1)S(1)}, bf16[290,128]{1,0:T(8,128)(2,1)S(1)}, u32[]{:S(2)}, u32[]{:S(2)}) %collective-permute-start.4) | collective-permute-done | bytes 74272 | tf_op jit(solution)/shard_map/ppermute | solution.py:34
  24.3 1.6 %collective-permute-start.7 = (bf16[15,48,384]{2,1,0:T(8,128)(2,1)S(1)}, bf16[15,48,384]{2,1,0:T(8,128)(2,1)S(1)}, u32[]{:S(2)}, u32[]{:S(2)}) collective-permute-start(bf16[15,48,384]{2,1,0:T(8,128)(2,1)S(1)} %collective-permute-done.refs_5_), channel_id=1, source_target_pairs={{0,8},{1,9},{2,10},{3,11},{4,12},{5,13},{6,14},{7,15},{8,0},{9,1},... | collective-permute-start | bytes 1658888 | tf_op jit(solution)/shard_map/ppermute | solution.py:28
  25.8 1.5 %collective-permute-start.8 = (bf16[15,48,384]{2,1,0:T(8,128)(2,1)S(1)}, bf16[15,48,384]{2,1,0:T(8,128)(2,1)S(1)}, u32[]{:S(2)}, u32[]{:S(2)}) collective-permute-start(bf16[15,48,384]{2,1,0:T(8,128)(2,1)S(1)} %collective-permute-done.refs_5_), channel_id=1, source_target_pairs={{0,16},{1,17},{2,18},{3,19},{4,20},{5,21},{6,22},{7,23},{8,24},{9,... | collective-permute-start | bytes 1658888 | tf_op jit(solution)/shard_map/ppermute | solution.py:28
  27.4 1.3 collective-permute-start.6
  29.2 1.0 reshape.48.refs_4_
  30.2 10.3 %collective-permute-done.6 = bf16[290,128]{1,0:T(8,128)(2,1)S(1)} collective-permute-done((bf16[290,128]{1,0:T(8,128)(2,1)S(1)}, bf16[290,128]{1,0:T(8,128)(2,1)S(1)}, u32[]{:S(2)}, u32[]{:S(2)}) %collective-permute-start.6) | collective-permute-done | bytes 74272 | tf_op jit(solution)/shard_map/ppermute | solution.py:34
  40.8 1.6 %collective-permute-start.13 = (bf16[23,48,384]{2,1,0:T(8,128)(2,1)S(1)}, bf16[23,48,384]{2,1,0:T(8,128)(2,1)}, u32[]{:S(2)}, u32[]{:S(2)}) collective-permute-start(bf16[23,48,384]{2,1,0:T(8,128)(2,1)S(1)} %pad_maximum_fusion), channel_id=1, source_target_pairs={{0,16},{1,17},{2,18},{3,19},{4,20},{5,21},{6,22},{7,23},{8,24},{9,... | collective-permute-start | bytes 2543624 | tf_op jit(solution)/shard_map/ppermute | solution.py:28
  42.5 1.6 %collective-permute-start.12 = (bf16[22,48,384]{2,1,0:T(8,128)(2,1)S(1)}, bf16[22,48,384]{2,1,0:T(8,128)(2,1)S(1)}, u32[]{:S(2)}, u32[]{:S(2)}) collective-permute-start(bf16[22,48,384]{2,1,0:T(8,128)(2,1)S(1)} %pad_maximum_fusion.1), channel_id=1, source_target_pairs={{0,8},{1,9},{2,10},{3,11},{4,12},{5,13},{6,14},{7,15},{8,0},{9,1},... | collective-permute-start | bytes 2433032 | tf_op jit(solution)/shard_map/ppermute | solution.py:28
  44.1 11.9 %collective-permute-done.11 = bf16[290,128]{1,0:T(8,128)(2,1)S(1)} collective-permute-done((bf16[290,128]{1,0:T(8,128)(2,1)S(1)}, bf16[290,128]{1,0:T(8,128)(2,1)S(1)}, u32[]{:S(2)}, u32[]{:S(2)}) %collective-permute-start.11) | collective-permute-done | bytes 74272 | tf_op jit(solution)/shard_map/ppermute | solution.py:34
  56.5 1.4 %collective-permute-done.15.refs_10_ = bf16[15,48,384]{2,1,0:T(8,128)(2,1)S(1)} collective-permute-done((bf16[15,48,384]{2,1,0:T(8,128)(2,1)S(1)}, bf16[15,48,384]{2,1,0:T(8,128)(2,1)S(1)}, u32[]{:S(2)}, u32[]{:S(2)}) %collective-permute-start.15) | collective-permute-done | bytes 552992 | tf_op jit(solution)/shard_map/ppermute | solution.py:28
  58.7 1.0 collective-permute-done.12.refs_13_
  59.9 2.3 %collective-permute-done.21.refs_14_ = bf16[22,48,384]{2,1,0:T(8,128)(2,1)S(1)} collective-permute-done((bf16[22,48,384]{2,1,0:T(8,128)(2,1)S(1)}, bf16[22,48,384]{2,1,0:T(8,128)(2,1)S(1)}, u32[]{:S(2)}, u32[]{:S(2)}) %collective-permute-start.21) | collective-permute-done | bytes 811040 | tf_op jit(solution)/shard_map/ppermute | solution.py:28
  63.2 1.0 slice.74
  64.2 1.6 %collective-permute-start.18 = (bf16[15,48,384]{2,1,0:T(8,128)(2,1)S(1)}, bf16[15,48,384]{2,1,0:T(8,128)(2,1)}, u32[]{:S(2)}, u32[]{:S(2)}) collective-permute-start(bf16[15,48,384]{2,1,0:T(8,128)(2,1)S(1)} %collective-permute-done.10.refs_17_), channel_id=1, source_target_pairs={{0,8},{1,9},{2,10},{3,11},{4,12},{5,13},{6,14},{7,15},{8,0},{9,1},... | collective-permute-start | bytes 1658888 | tf_op jit(solution)/shard_map/ppermute | solution.py:28
  67.3 1.2 collective-permute-start.20
  69.5 1.9 %shard_map.91.refs_2_ = bf16[1280,384]{1,0:T(8,128)(2,1)S(1)} custom-call(f32[4,6,384]{2,1,0:T(8,128)S(1)} %copy.17.params, bf16[3,48,384]{2,1,0:T(8,128)(2,1)S(1)} %reshape.52.in_weight, bf16[32,16,128]{2,1,0:T(8,128)(2,1)S(1)} %bitcast.33), custom_call_target="tpu_custom_call" | custom-call | tf_op jit(solution)/shard_map/pallas_call | solution.py:393
  71.4 1.0 copy-done
  72.4 11.1 %collective-permute-done.20.refs_25_ = bf16[5,48,384]{2,1,0:T(8,128)(2,1)S(1)} collective-permute-done((bf16[5,48,384]{2,1,0:T(8,128)(2,1)S(1)}, bf16[5,48,384]{2,1,0:T(8,128)(2,1)S(1)}, u32[]{:S(2)}, u32[]{:S(2)}) %collective-permute-start.20) | collective-permute-done | bytes 184352 | tf_op jit(solution)/shard_map/ppermute | solution.py:28
  92.2 12.1 %shard_map.92.refs_2_ = bf16[960,384]{1,0:T(8,128)(2,1)} custom-call(f32[4,6,384]{2,1,0:T(8,128)} %copy.19.refs_0_, f32[1,192]{1,0:T(1,128)} %reshape_squeeze.3.refs_1_, bf16[1280,384]{1,0:T(8,128)(2,1)} %copy-done, bf16[54,96,384]{2,1,0:T(8,128)(2,1)} %bitcast.44, bf16[5,96,384]{2,1,0:T(8,128)(2,1)} %reshape.48.refs_4_, bf16[15,48,384]{2,1,0:T(8,128)(2,1)} %copy-done.9, ...), custom_call_target="tpu_custom_call" | custom-call | flops 11041505280 | bytes 5308416 | tf_op jit(solution)/shard_map/pallas_call | solution.py:445
  107.6 14.4 %shard_map.93 = (bf16[4,48,128]{2,1,0:T(8,128)(2,1)}, bf16[4,48,128]{2,1,0:T(8,128)(2,1)}, bf16[4,48,128]{2,1,0:T(8,128)(2,1)}, bf16[4,48,128]{2,1,0:T(8,128)(2,1)}) custom-call(f32[4,6,384]{2,1,0:T(8,128)} %copy.19.refs_0_, f32[1,192]{1,0:T(1,128)} %reshape_squeeze.3.refs_1_, bf16[960,384]{1,0:T(8,128)(2,1)} %shard_map.92.refs_2_, ...), custom_call_target="tpu_custom_call" | custom-call | flops 11890851840 | bytes 12386304 | tf_op jit(solution)/shard_map/pallas_call | solution.py:445
  122.1 1.2 collective-permute-start.34
  123.3 3.1 %collective-permute-start.35 = (bf16[4,48,128]{2,1,0:T(8,128)(2,1)}, bf16[4,48,128]{2,1,0:T(8,128)(2,1)S(1)}, u32[]{:S(2)}, u32[]{:S(2)}) collective-permute-start(bf16[4,48,128]{2,1,0:T(8,128)(2,1)} %get-tuple-element.57), channel_id=1, source_target_pairs={{0,2},{1,3},{2,0},{3,1},{4,6},{5,7},{6,4},{7,5},{8,10},{9,11},{10,... | collective-permute-start | bytes 147464 | tf_op jit(solution)/shard_map/ppermute | solution.py:34
  126.4 2.6 %collective-permute-start.36 = (bf16[4,48,128]{2,1,0:T(8,128)(2,1)}, bf16[4,48,128]{2,1,0:T(8,128)(2,1)S(1)}, u32[]{:S(2)}, u32[]{:S(2)}) collective-permute-start(bf16[4,48,128]{2,1,0:T(8,128)(2,1)} %get-tuple-element.58), channel_id=1, source_target_pairs={{0,3},{1,0},{2,1},{3,2},{4,7},{5,4},{6,5},{7,6},{8,11},{9,8},{10,9... | collective-permute-start | bytes 147464 | tf_op jit(solution)/shard_map/ppermute | solution.py:34
  129.3 1.8 %collective-permute-done.36 = bf16[4,48,128]{2,1,0:T(8,128)(2,1)S(1)} collective-permute-done((bf16[4,48,128]{2,1,0:T(8,128)(2,1)}, bf16[4,48,128]{2,1,0:T(8,128)(2,1)S(1)}, u32[]{:S(2)}, u32[]{:S(2)}) %collective-permute-start.36) | collective-permute-done | bytes 49184 | tf_op jit(solution)/shard_map/ppermute | solution.py:34
  (150 shorter events, 24.8 us)
Async XLA Ops:
  4.3 20.0 %collective-permute-start = (bf16[15,48,384]{2,1,0:T(8,128)(2,1)S(1)}, bf16[15,48,384]{2,1,0:T(8,128)(2,1)S(1)}, u32[]{:S(2)}, u32[]{:S(2)}) collective-permute-start(bf16[15,48,384]{2,1,0:T(8,128)(2,1)S(1)} %pad_maximum_fusion.2), channel_id=1, source_target_pairs={{0,1},{1,2},{2,3},{3,0},{4,5},{5,6},{6,7},{7,4},{8,9},{9,10},{10,1... | collective-permute-start | bytes 1658888 | tf_op jit(solution)/shard_map/ppermute | solution.py:34
  7.4 2.5 %collective-permute-start.1 = (bf16[1,16,128]{2,1,0:T(8,128)(2,1)}, bf16[1,16,128]{2,1,0:T(8,128)(2,1)S(1)}, u32[]{:S(2)}, u32[]{:S(2)}) collective-permute-start(bf16[1,16,128]{2,1,0:T(8,128)(2,1)} %bitcast.53), channel_id=1, source_target_pairs={{0,4},{1,5},{2,6},{3,7},{4,0},{5,1},{6,2},{7,3},{8,12},{9,13},{10,... | collective-permute-start | bytes 12296 | tf_op jit(solution)/shard_map/ppermute | solution.py:28
  10.5 3.7 %collective-permute-start.2 = (bf16[2,16,128]{2,1,0:T(8,128)(2,1)S(1)}, bf16[2,16,128]{2,1,0:T(8,128)(2,1)S(1)}, u32[]{:S(2)}, u32[]{:S(2)}) collective-permute-start(bf16[2,16,128]{2,1,0:T(8,128)(2,1)S(1)} %pad_maximum_fusion.22), channel_id=1, source_target_pairs={{0,8},{1,9},{2,10},{3,11},{4,12},{5,13},{6,14},{7,15},{8,0},{9,1},... | collective-permute-start | bytes 24584 | tf_op jit(solution)/shard_map/ppermute | solution.py:28
  14.2 3.8 %collective-permute-start.3 = (bf16[4,16,128]{2,1,0:T(8,128)(2,1)S(1)}, bf16[4,16,128]{2,1,0:T(8,128)(2,1)S(1)}, u32[]{:S(2)}, u32[]{:S(2)}) collective-permute-start(bf16[4,16,128]{2,1,0:T(8,128)(2,1)S(1)} %pad_maximum_fusion.21), channel_id=1, source_target_pairs={{0,16},{1,17},{2,18},{3,19},{4,20},{5,21},{6,22},{7,23},{8,24},{9,... | collective-permute-start | bytes 49160 | tf_op jit(solution)/shard_map/ppermute | solution.py:28
  18.0 6.2 %collective-permute-start.4 = (bf16[290,128]{1,0:T(8,128)(2,1)S(1)}, bf16[290,128]{1,0:T(8,128)(2,1)S(1)}, u32[]{:S(2)}, u32[]{:S(2)}) collective-permute-start(bf16[290,128]{1,0:T(8,128)(2,1)S(1)} %get-tuple-element.68), channel_id=1, source_target_pairs={{0,1},{1,2},{2,3},{3,0},{4,5},{5,6},{6,7},{7,4},{8,9},{9,10},{10,1... | collective-permute-start | bytes 222728 | tf_op jit(solution)/shard_map/ppermute | solution.py:34
  24.3 16.3 %collective-permute-start.5 = (bf16[15,48,384]{2,1,0:T(8,128)(2,1)S(1)}, bf16[15,48,384]{2,1,0:T(8,128)(2,1)S(1)}, u32[]{:S(2)}, u32[]{:S(2)}) collective-permute-start(bf16[15,48,384]{2,1,0:T(8,128)(2,1)S(1)} %collective-permute-done.refs_5_), channel_id=1, source_target_pairs={{0,1},{1,2},{2,3},{3,0},{4,5},{5,6},{6,7},{7,4},{8,9},{9,10},{10,1... | collective-permute-start | bytes 1658888 | tf_op jit(solution)/shard_map/ppermute | solution.py:34
  24.3 16.3 %collective-permute-start.7 = (bf16[15,48,384]{2,1,0:T(8,128)(2,1)S(1)}, bf16[15,48,384]{2,1,0:T(8,128)(2,1)S(1)}, u32[]{:S(2)}, u32[]{:S(2)}) collective-permute-start(bf16[15,48,384]{2,1,0:T(8,128)(2,1)S(1)} %collective-permute-done.refs_5_), channel_id=1, source_target_pairs={{0,8},{1,9},{2,10},{3,11},{4,12},{5,13},{6,14},{7,15},{8,0},{9,1},... | collective-permute-start | bytes 1658888 | tf_op jit(solution)/shard_map/ppermute | solution.py:28
  25.8 14.7 %collective-permute-start.8 = (bf16[15,48,384]{2,1,0:T(8,128)(2,1)S(1)}, bf16[15,48,384]{2,1,0:T(8,128)(2,1)S(1)}, u32[]{:S(2)}, u32[]{:S(2)}) collective-permute-start(bf16[15,48,384]{2,1,0:T(8,128)(2,1)S(1)} %collective-permute-done.refs_5_), channel_id=1, source_target_pairs={{0,16},{1,17},{2,18},{3,19},{4,20},{5,21},{6,22},{7,23},{8,24},{9,... | collective-permute-start | bytes 1658888 | tf_op jit(solution)/shard_map/ppermute | solution.py:28
  27.4 13.2 %collective-permute-start.9 = (bf16[15,48,384]{2,1,0:T(8,128)(2,1)S(1)}, bf16[15,48,384]{2,1,0:T(8,128)(2,1)}, u32[]{:S(2)}, u32[]{:S(2)}) collective-permute-start(bf16[15,48,384]{2,1,0:T(8,128)(2,1)S(1)} %collective-permute-done.refs_5_), channel_id=1, source_target_pairs={{0,4},{1,5},{2,6},{3,7},{4,0},{5,1},{6,2},{7,3},{8,12},{9,13},{10,... | collective-permute-start | bytes 1658888 | tf_op jit(solution)/shard_map/ppermute | solution.py:28
  27.4 13.2 %collective-permute-start.6 = (bf16[290,128]{1,0:T(8,128)(2,1)S(1)}, bf16[290,128]{1,0:T(8,128)(2,1)S(1)}, u32[]{:S(2)}, u32[]{:S(2)}) collective-permute-start(bf16[290,128]{1,0:T(8,128)(2,1)S(1)} %collective-permute-done.4), channel_id=1, source_target_pairs={{0,1},{1,2},{2,3},{3,0},{4,5},{5,6},{6,7},{7,4},{8,9},{9,10},{10,1... | collective-permute-start | bytes 222728 | tf_op jit(solution)/shard_map/ppermute | solution.py:34
  40.6 15.4 %collective-permute-start.10 = (bf16[15,48,384]{2,1,0:T(8,128)(2,1)S(1)}, bf16[15,48,384]{2,1,0:T(8,128)(2,1)S(1)}, u32[]{:S(2)}, u32[]{:S(2)}) collective-permute-start(bf16[15,48,384]{2,1,0:T(8,128)(2,1)S(1)} %collective-permute-done.5.refs_11_), channel_id=1, source_target_pairs={{0,1},{1,2},{2,3},{3,0},{4,5},{5,6},{6,7},{7,4},{8,9},{9,10},{10,1... | collective-permute-start | bytes 1658888 | tf_op jit(solution)/shard_map/ppermute | solution.py:34
  40.8 19.0 %collective-permute-start.13 = (bf16[23,48,384]{2,1,0:T(8,128)(2,1)S(1)}, bf16[23,48,384]{2,1,0:T(8,128)(2,1)}, u32[]{:S(2)}, u32[]{:S(2)}) collective-permute-start(bf16[23,48,384]{2,1,0:T(8,128)(2,1)S(1)} %pad_maximum_fusion), channel_id=1, source_target_pairs={{0,16},{1,17},{2,18},{3,19},{4,20},{5,21},{6,22},{7,23},{8,24},{9,... | collective-permute-start | bytes 2543624 | tf_op jit(solution)/shard_map/ppermute | solution.py:28
  42.5 17.2 %collective-permute-start.12 = (bf16[22,48,384]{2,1,0:T(8,128)(2,1)S(1)}, bf16[22,48,384]{2,1,0:T(8,128)(2,1)S(1)}, u32[]{:S(2)}, u32[]{:S(2)}) collective-permute-start(bf16[22,48,384]{2,1,0:T(8,128)(2,1)S(1)} %pad_maximum_fusion.1), channel_id=1, source_target_pairs={{0,8},{1,9},{2,10},{3,11},{4,12},{5,13},{6,14},{7,15},{8,0},{9,1},... | collective-permute-start | bytes 2433032 | tf_op jit(solution)/shard_map/ppermute | solution.py:28
  44.1 11.9 %collective-permute-start.11 = (bf16[290,128]{1,0:T(8,128)(2,1)S(1)}, bf16[290,128]{1,0:T(8,128)(2,1)S(1)}, u32[]{:S(2)}, u32[]{:S(2)}) collective-permute-start(bf16[290,128]{1,0:T(8,128)(2,1)S(1)} %collective-permute-done.6), channel_id=1, source_target_pairs={{0,1},{1,2},{2,3},{3,0},{4,5},{5,6},{6,7},{7,4},{8,9},{9,10},{10,1... | collective-permute-start | bytes 222728 | tf_op jit(solution)/shard_map/ppermute | solution.py:34
  44.1 12.4 %collective-permute-start.14 = (bf16[15,48,384]{2,1,0:T(8,128)(2,1)S(1)}, bf16[15,48,384]{2,1,0:T(8,128)(2,1)S(1)}, u32[]{:S(2)}, u32[]{:S(2)}) collective-permute-start(bf16[15,48,384]{2,1,0:T(8,128)(2,1)S(1)} %collective-permute-done.7.refs_7_), channel_id=1, source_target_pairs={{0,4},{1,5},{2,6},{3,7},{4,0},{5,1},{6,2},{7,3},{8,12},{9,13},{10,... | collective-permute-start | bytes 1658888 | tf_op jit(solution)/shard_map/ppermute | solution.py:28
  56.0 2.7 %collective-permute-start.16 = (bf16[15,48,384]{2,1,0:T(8,128)(2,1)S(1)}, bf16[15,48,384]{2,1,0:T(8,128)(2,1)S(1)}, u32[]{:S(2)}, u32[]{:S(2)}) collective-permute-start(bf16[15,48,384]{2,1,0:T(8,128)(2,1)S(1)} %collective-permute-done.5.refs_11_), channel_id=1, source_target_pairs={{0,4},{1,5},{2,6},{3,7},{4,0},{5,1},{6,2},{7,3},{8,12},{9,13},{10,... | collective-permute-start | bytes 1658888 | tf_op jit(solution)/shard_map/ppermute | solution.py:28
  63.0 3.9 %collective-permute-start.22 = (bf16[23,48,384]{2,1,0:T(8,128)(2,1)}, bf16[23,48,384]{2,1,0:T(8,128)(2,1)}, u32[]{:S(2)}, u32[]{:S(2)}) collective-permute-start(bf16[23,48,384]{2,1,0:T(8,128)(2,1)} %collective-permute-done.13.refs_15_), channel_id=1, source_target_pairs={{0,4},{1,5},{2,6},{3,7},{4,0},{5,1},{6,2},{7,3},{8,12},{9,13},{10,... | collective-permute-start | bytes 2543624 | tf_op jit(solution)/shard_map/ppermute | solution.py:28
  64.2 19.3 %collective-permute-start.18 = (bf16[15,48,384]{2,1,0:T(8,128)(2,1)S(1)}, bf16[15,48,384]{2,1,0:T(8,128)(2,1)}, u32[]{:S(2)}, u32[]{:S(2)}) collective-permute-start(bf16[15,48,384]{2,1,0:T(8,128)(2,1)S(1)} %collective-permute-done.10.refs_17_), channel_id=1, source_target_pairs={{0,8},{1,9},{2,10},{3,11},{4,12},{5,13},{6,14},{7,15},{8,0},{9,1},... | collective-permute-start | bytes 1658888 | tf_op jit(solution)/shard_map/ppermute | solution.py:28
  65.8 18.6 %collective-permute-start.19 = (bf16[15,48,384]{2,1,0:T(8,128)(2,1)S(1)}, bf16[15,48,384]{2,1,0:T(8,128)(2,1)}, u32[]{:S(2)}, u32[]{:S(2)}) collective-permute-start(bf16[15,48,384]{2,1,0:T(8,128)(2,1)S(1)} %collective-permute-done.10.refs_17_), channel_id=1, source_target_pairs={{0,16},{1,17},{2,18},{3,19},{4,20},{5,21},{6,22},{7,23},{8,24},{9,... | collective-permute-start | bytes 1658888 | tf_op jit(solution)/shard_map/ppermute | solution.py:28
  66.8 16.7 %collective-permute-start.17 = (bf16[15,48,384]{2,1,0:T(8,128)(2,1)S(1)}, bf16[15,48,384]{2,1,0:T(8,128)(2,1)}, u32[]{:S(2)}, u32[]{:S(2)}) collective-permute-start(bf16[15,48,384]{2,1,0:T(8,128)(2,1)S(1)} %pad_maximum_fusion.3), channel_id=1, source_target_pairs={{0,1},{1,2},{2,3},{3,0},{4,5},{5,6},{6,7},{7,4},{8,9},{9,10},{10,1... | collective-permute-start | bytes 1658888 | tf_op jit(solution)/shard_map/ppermute | solution.py:34
  66.9 17.5 %collective-permute-start.23 = (bf16[15,48,384]{2,1,0:T(8,128)(2,1)S(1)}, bf16[15,48,384]{2,1,0:T(8,128)(2,1)}, u32[]{:S(2)}, u32[]{:S(2)}) collective-permute-start(bf16[15,48,384]{2,1,0:T(8,128)(2,1)S(1)} %collective-permute-done.10.refs_17_), channel_id=1, source_target_pairs={{0,4},{1,5},{2,6},{3,7},{4,0},{5,1},{6,2},{7,3},{8,12},{9,13},{10,... | collective-permute-start | bytes 1658888 | tf_op jit(solution)/shard_map/ppermute | solution.py:28
  67.3 16.2 %collective-permute-start.20 = (bf16[5,48,384]{2,1,0:T(8,128)(2,1)S(1)}, bf16[5,48,384]{2,1,0:T(8,128)(2,1)S(1)}, u32[]{:S(2)}, u32[]{:S(2)}) collective-permute-start(bf16[5,48,384]{2,1,0:T(8,128)(2,1)S(1)} %slice.75), channel_id=1, source_target_pairs={{0,24},{1,25},{2,26},{3,27},{4,28},{5,29},{6,30},{7,31},{8,16},{9,... | collective-permute-start | bytes 552968 | tf_op jit(solution)/shard_map/ppermute | solution.py:28
  84.4 5.4 %collective-permute-start.24 = (bf16[15,48,384]{2,1,0:T(8,128)(2,1)}, bf16[15,48,384]{2,1,0:T(8,128)(2,1)S(1)}, u32[]{:S(2)}, u32[]{:S(2)}) collective-permute-start(bf16[15,48,384]{2,1,0:T(8,128)(2,1)} %collective-permute-done.18.refs_19_), channel_id=1, source_target_pairs={{0,4},{1,5},{2,6},{3,7},{4,0},{5,1},{6,2},{7,3},{8,12},{9,13},{10,... | collective-permute-start | bytes 1658888 | tf_op jit(solution)/shard_map/ppermute | solution.py:28
  84.4 6.2 %collective-permute-start.25 = (bf16[15,48,384]{2,1,0:T(8,128)(2,1)}, bf16[15,48,384]{2,1,0:T(8,128)(2,1)S(1)}, u32[]{:S(2)}, u32[]{:S(2)}) collective-permute-start(bf16[15,48,384]{2,1,0:T(8,128)(2,1)} %collective-permute-done.19.refs_21_), channel_id=1, source_target_pairs={{0,4},{1,5},{2,6},{3,7},{4,0},{5,1},{6,2},{7,3},{8,12},{9,13},{10,... | collective-permute-start | bytes 1658888 | tf_op jit(solution)/shard_map/ppermute | solution.py:28
  84.9 5.7 %collective-permute-start.26 = (bf16[15,48,384]{2,1,0:T(8,128)(2,1)}, bf16[15,48,384]{2,1,0:T(8,128)(2,1)S(1)}, u32[]{:S(2)}, u32[]{:S(2)}) collective-permute-start(bf16[15,48,384]{2,1,0:T(8,128)(2,1)} %collective-permute-done.17.refs_23_), channel_id=1, source_target_pairs={{0,4},{1,5},{2,6},{3,7},{4,0},{5,1},{6,2},{7,3},{8,12},{9,13},{10,... | collective-permute-start | bytes 1658888 | tf_op jit(solution)/shard_map/ppermute | solution.py:28
  84.9 3.9 %collective-permute-start.27 = (bf16[5,48,384]{2,1,0:T(8,128)(2,1)S(1)}, bf16[5,48,384]{2,1,0:T(8,128)(2,1)S(1)}, u32[]{:S(2)}, u32[]{:S(2)}) collective-permute-start(bf16[5,48,384]{2,1,0:T(8,128)(2,1)S(1)} %collective-permute-done.20.refs_25_), channel_id=1, source_target_pairs={{0,4},{1,5},{2,6},{3,7},{4,0},{5,1},{6,2},{7,3},{8,12},{9,13},{10,... | collective-permute-start | bytes 552968 | tf_op jit(solution)/shard_map/ppermute | solution.py:28
  88.8 15.6 %collective-permute-start.32 = (bf16[4,48,384]{2,1,0:T(8,128)(2,1)S(1)}, bf16[4,48,384]{2,1,0:T(8,128)(2,1)S(1)}, u32[]{:S(2)}, u32[]{:S(2)}) collective-permute-start(bf16[4,48,384]{2,1,0:T(8,128)(2,1)S(1)} %slice.87), channel_id=1, source_target_pairs={{0,1},{1,2},{2,3},{3,0},{4,5},{5,6},{6,7},{7,4},{8,9},{9,10},{10,1... | collective-permute-start | bytes 442376 | tf_op jit(solution)/shard_map/ppermute | solution.py:34
  88.8 15.7 %collective-permute-start.30 = (bf16[3,48,384]{2,1,0:T(8,128)(2,1)S(1)}, bf16[3,48,384]{2,1,0:T(8,128)(2,1)S(1)}, u32[]{:S(2)}, u32[]{:S(2)}) collective-permute-start(bf16[3,48,384]{2,1,0:T(8,128)(2,1)S(1)} %slice.86), channel_id=1, source_target_pairs={{0,16},{1,17},{2,18},{3,19},{4,20},{5,21},{6,22},{7,23},{8,24},{9,... | collective-permute-start | bytes 331784 | tf_op jit(solution)/shard_map/ppermute | solution.py:28
  89.7 15.2 %collective-permute-start.28 = (bf16[3,48,384]{2,1,0:T(8,128)(2,1)S(1)}, bf16[3,48,384]{2,1,0:T(8,128)(2,1)S(1)}, u32[]{:S(2)}, u32[]{:S(2)}) collective-permute-start(bf16[3,48,384]{2,1,0:T(8,128)(2,1)S(1)} %slice.85), channel_id=1, source_target_pairs={{0,8},{1,9},{2,10},{3,11},{4,12},{5,13},{6,14},{7,15},{8,0},{9,1},... | collective-permute-start | bytes 331784 | tf_op jit(solution)/shard_map/ppermute | solution.py:28
  122.1 7.0 %collective-permute-start.34 = (bf16[4,48,128]{2,1,0:T(8,128)(2,1)}, bf16[4,48,128]{2,1,0:T(8,128)(2,1)S(1)}, u32[]{:S(2)}, u32[]{:S(2)}) collective-permute-start(bf16[4,48,128]{2,1,0:T(8,128)(2,1)} %get-tuple-element.56), channel_id=1, source_target_pairs={{0,1},{1,2},{2,3},{3,0},{4,5},{5,6},{6,7},{7,4},{8,9},{9,10},{10,1... | collective-permute-start | bytes 147464 | tf_op jit(solution)/shard_map/ppermute | solution.py:34
  123.3 6.0 %collective-permute-start.35 = (bf16[4,48,128]{2,1,0:T(8,128)(2,1)}, bf16[4,48,128]{2,1,0:T(8,128)(2,1)S(1)}, u32[]{:S(2)}, u32[]{:S(2)}) collective-permute-start(bf16[4,48,128]{2,1,0:T(8,128)(2,1)} %get-tuple-element.57), channel_id=1, source_target_pairs={{0,2},{1,3},{2,0},{3,1},{4,6},{5,7},{6,4},{7,5},{8,10},{9,11},{10,... | collective-permute-start | bytes 147464 | tf_op jit(solution)/shard_map/ppermute | solution.py:34
  126.4 4.7 %collective-permute-start.36 = (bf16[4,48,128]{2,1,0:T(8,128)(2,1)}, bf16[4,48,128]{2,1,0:T(8,128)(2,1)S(1)}, u32[]{:S(2)}, u32[]{:S(2)}) collective-permute-start(bf16[4,48,128]{2,1,0:T(8,128)(2,1)} %get-tuple-element.58), channel_id=1, source_target_pairs={{0,3},{1,0},{2,1},{3,2},{4,7},{5,4},{6,5},{7,6},{8,11},{9,8},{10,9... | collective-permute-start | bytes 147464 | tf_op jit(solution)/shard_map/ppermute | solution.py:34
  (29 other events, 217.2 us)
